TPU v7x, 32 devices: a whole 2x2x4 slice. The times are simulated.
32 devices in a mesh: seq: 4 (over y, x), tensor: 8 (over z, core).
Axes of the slice: x: 2, y: 2, z: 4, core: 2. Of those that a mesh axis runs over, the one named last changes fastest.
Arguments:
- frames: bfloat16 [2048, 8192], P('seq', 'tensor'), may hold values from -6 to 6
- up_factors: bfloat16 [6, 128, 256, 256], P(None, 'tensor'), may hold values from -0.15625 to 0.15625
- down_factors: bfloat16 [6, 128, 256, 256], P(None, 'tensor'), may hold values from -0.078125 to 0.078125
- pattern: int32 [128, 5], P('tensor'), may hold values 0 or 1
- level_bits: int32 [5], replicated, may hold values from 0 to 4, each once
- taps: float32 [3, 8192], P(None, 'tensor'), may hold values from -3 to 3
- cotangent: bfloat16 [2048, 8192], P('seq', 'tensor'), may hold values from -6 to 6
Outputs:
- convolved: bfloat16 [2048, 8192], P('seq', 'tensor')
- grad_frames: bfloat16 [2048, 8192], P('seq', 'tensor')
- grad_up: float32 [6, 128, 256, 256], P(None, 'tensor', 'seq')
- grad_down: float32 [6, 128, 256, 256], P(None, 'tensor', 'seq')
Inputs may be any that keep to these rules, and one draw needn't show every extreme that they name: Level l pairs feature block i with block i xor 2^level_bits[l]; each of 0..4 appears once.
All inputs are finite; a program needn't handle non-finite values. No bound on the sum of `pattern` on one device may be relied on, other than what follows from the above.
Results may differ from a plain program's by a relative error of at most 0.012.
Values may be sent and summed in bfloat16 or wider, within the bound.
No kernel may reach another device: no remote copies, remote signals or barrier semaphores. Data moves between devices by JAX's collectives and lax.ppermute only.
A program may use at most 192 MiB of HBM per device.

v0:
```python
import jax
import jax.numpy as jnp
from jax import lax
from jax.sharding import PartitionSpec as P

coef = 0.7978845608028654


def swapped(array, axis, stride):
    return lax.ppermute(array, axis, [(i, i ^ 1 << stride) for i in range(lax.axis_size(axis))])


def extended(array, sides, width):
    for axis, dim in sides:
        peers, length = (lax.axis_size(axis), array.shape[dim])
        up = [(i, (i + 1) % peers) for i in range(peers - 1)]
        down = [(j, i) for i, j in up]
        last = lax.slice_in_dim(array, length - width, length, axis=dim)
        leading = lax.slice_in_dim(array, 0, width, axis=dim)
        before = lax.ppermute(last, axis, up)
        after = lax.ppermute(leading, axis, down)
        array = jnp.concatenate([before, array, after], axis=dim)
    return array


def gelu_value(values):
    return 0.5 * values * (1.0 + jnp.tanh(coef * (values + 0.044715 * values * values * values)))


def gelu_slope(values):
    inner = jnp.tanh(coef * (values + 0.044715 * values * values * values))
    return 0.5 * (1.0 + inner) + 0.5 * values * (1.0 - inner * inner) * coef * (
        1.0 + 3.0 * 0.044715 * values * values
    )


def flip_blocks(stacked, stride):
    rows_dev, count, width = stacked.shape
    shaped = stacked.reshape(rows_dev, count // (2 * stride), 2, stride, width)
    return shaped[:, :, ::-1].reshape(rows_dev, count, width)


def partner_rows(block_rows, bit, blocks_dev, width_block):
    rows_dev, local_width = block_rows.shape
    stride = 1 << bit
    if stride < blocks_dev:
        return flip_blocks(block_rows.reshape(rows_dev, blocks_dev, width_block), stride)
    device_bit = bit - (blocks_dev.bit_length() - 1)
    fetched = swapped(block_rows, "tensor", device_bit)
    return fetched.reshape(rows_dev, blocks_dev, width_block)


def push_partial(partial_value, bit, blocks_dev):
    stride = 1 << bit
    if stride < blocks_dev:
        return flip_blocks(partial_value, stride)
    device_bit = bit - (blocks_dev.bit_length() - 1)
    return swapped(partial_value.astype(jnp.bfloat16), "tensor", device_bit).astype(
        partial_value.dtype
    )


def local(frames, up_factors, down_factors, pattern, level_bits, taps, cotangent):
    f32 = jnp.float32
    rows_dev, local_width = frames.shape
    factors, hidden_dev, width_block, _ = up_factors.shape
    levels = factors - 1
    blocks_dev = local_width // width_block
    ratio = hidden_dev // blocks_dev
    scale = 1.0 / jnp.sqrt(jnp.asarray(rows_dev * lax.axis_size("seq"), f32))
    up_four = up_factors.reshape(factors, blocks_dev, ratio, width_block, width_block)
    down_four = down_factors.reshape(factors, blocks_dev, ratio, width_block, width_block)
    level_of = [jnp.argmax(level_bits == bit) for bit in range(levels)]
    mask_of = [
        jnp.sum(jnp.where(level_bits[None, :] == bit, pattern, 0), axis=1)
        .astype(f32)
        .reshape(blocks_dev, ratio)
        for bit in range(levels)
    ]
    up_of = [
        lax.dynamic_index_in_dim(up_four, level_of[bit] + 1, 0, keepdims=False)
        for bit in range(levels)
    ]
    down_of = [
        lax.dynamic_index_in_dim(down_four, level_of[bit] + 1, 0, keepdims=False)
        for bit in range(levels)
    ]
    inputs = frames.reshape(rows_dev, blocks_dev, width_block)
    pre = jnp.einsum("rbs,bhsf->rbhf", inputs, up_four[0], preferred_element_type=f32)
    moved_inputs = []
    for bit in range(levels):
        moved = partner_rows(frames, bit, blocks_dev, width_block)
        moved_inputs.append(moved)
        pre = pre + mask_of[bit][None, :, :, None] * jnp.einsum(
            "rbs,bhsf->rbhf", moved, up_of[bit], preferred_element_type=f32
        )
    hidden = gelu_value(pre).astype(jnp.bfloat16)
    mixed = jnp.einsum("rbhf,bhfs->rbs", hidden, down_four[0], preferred_element_type=f32)
    for bit in range(levels):
        masked = hidden * mask_of[bit][None, :, :, None].astype(jnp.bfloat16)
        partial_value = jnp.einsum(
            "rbhf,bhfs->rbs", masked, down_of[bit], preferred_element_type=f32
        )
        mixed = mixed + push_partial(partial_value, bit, blocks_dev)
    mixed = mixed.reshape(rows_dev, local_width).astype(jnp.bfloat16)
    mixed_rim, cot_rim = (extended(mixed, (("seq", 0),), 1), extended(cotangent, (("seq", 0),), 1))
    mixed_f = mixed_rim.astype(f32)
    convolved = (taps[0] * mixed_f[:-2] + taps[1] * mixed_f[1:-1] + taps[2] * mixed_f[2:]).astype(
        jnp.bfloat16
    )
    cot_f = cot_rim.astype(f32)
    grad_mixed = (taps[0] * cot_f[2:] + taps[1] * cot_f[1:-1] + taps[2] * cot_f[:-2]).astype(
        jnp.bfloat16
    )
    grad_blocks = grad_mixed.reshape(rows_dev, blocks_dev, width_block)
    grad_hidden = jnp.einsum(
        "rbs,bhfs->rbhf", grad_blocks, down_four[0], preferred_element_type=f32
    )
    down_terms = [jnp.einsum("rbhf,rbs->bhfs", hidden, grad_blocks, preferred_element_type=f32)]
    for bit in range(levels):
        moved = partner_rows(grad_mixed, bit, blocks_dev, width_block)
        grad_hidden = grad_hidden + mask_of[bit][None, :, :, None] * jnp.einsum(
            "rbs,bhfs->rbhf", moved, down_of[bit], preferred_element_type=f32
        )
        down_terms.append(
            mask_of[bit][:, :, None, None]
            * jnp.einsum("rbhf,rbs->bhfs", hidden, moved, preferred_element_type=f32)
        )
    grad_pre = (grad_hidden * gelu_slope(pre)).astype(jnp.bfloat16)
    grad_in = jnp.einsum("rbhf,bhsf->rbs", grad_pre, up_four[0], preferred_element_type=f32)
    up_terms = [jnp.einsum("rbs,rbhf->bhsf", inputs, grad_pre, preferred_element_type=f32)]
    for bit in range(levels):
        masked = grad_pre * mask_of[bit][None, :, :, None].astype(jnp.bfloat16)
        partial_value = jnp.einsum("rbhf,bhsf->rbs", masked, up_of[bit], preferred_element_type=f32)
        grad_in = grad_in + push_partial(partial_value, bit, blocks_dev)
        up_terms.append(
            mask_of[bit][:, :, None, None]
            * jnp.einsum("rbs,rbhf->bhsf", moved_inputs[bit], grad_pre, preferred_element_type=f32)
        )
    grad_frames = grad_in.reshape(rows_dev, local_width).astype(jnp.bfloat16)
    term_shape = up_terms[0].shape
    shape_five = (factors,) + term_shape
    up_stack = jnp.zeros(shape_five, f32).at[0].set(up_terms[0])
    down_stack = jnp.zeros(shape_five, f32).at[0].set(down_terms[0])
    for bit in range(levels):
        up_stack = lax.dynamic_update_index_in_dim(
            up_stack, up_terms[bit + 1], level_of[bit] + 1, 0
        )
        down_stack = lax.dynamic_update_index_in_dim(
            down_stack, down_terms[bit + 1], level_of[bit] + 1, 0
        )
    up_stack = up_stack.reshape(factors, hidden_dev, term_shape[2], term_shape[3])
    down_stack = down_stack.reshape(factors, hidden_dev, term_shape[2], term_shape[3])
    grad_up, grad_down = (
        lax.psum_scatter(
            (up_stack * scale).astype(jnp.bfloat16), "seq", scatter_dimension=2, tiled=True
        ).astype(jnp.float32),
        lax.psum_scatter(
            (down_stack * scale).astype(jnp.bfloat16), "seq", scatter_dimension=2, tiled=True
        ).astype(jnp.float32),
    )
    return (convolved, grad_frames, grad_up, grad_down)


def solution(mesh):
    in_specs = (
        P("seq", "tensor"),
        P(None, "tensor", None, None),
        P(None, "tensor", None, None),
        P("tensor", None),
        P(),
        P(None, "tensor"),
        P("seq", "tensor"),
    )
    out_specs = (
        P("seq", "tensor"),
        P("seq", "tensor"),
        P(None, "tensor", "seq", None),
        P(None, "tensor", "seq", None),
    )
    return jax.shard_map(local, mesh=mesh, in_specs=in_specs, out_specs=out_specs, check_vma=False)
```

profile of v0, /device:TPU:0, one launch (start us, length us, event | category | flops | bytes accessed | tf_op | source)
XLA Modules:
  0.0 642.1 jit_solution(2336533487540224484)
XLA Ops:
  19.0 5.2 collective-permute-start.8
  36.3 10.3 %rev.24 = bf16[512,2,2,1,256]{4,2,1,0,3:T(2,128)(2,1)} reverse(bf16[512,2,2,1,256]{4,2,1,0,3:T(2,128)(2,1)} %reshape_reshape.12), dimensions={2} | reverse | bytes 2097152 | tf_op jit(solution)/shard_map/rev | solution.py:40
  48.9 6.0 fusion.156
  54.9 6.5 %fusion.56 = f32[4,4,256,512]{3,2,1,0:T(8,128)} fusion(bf16[512,4,256,1]{2,0,3,1:T(8,128)(2,1)S(1)} %bitcast.402, bf16[6,4,4,256,256]{4,3,2,1,0:T(8,128)(2,1)} %bitcast.410, s32[]{:T(128)S(6)} %select_n.63), kind=kOutput, calls=%fused_computation.86 | convolution fusion | flops 1073741824 | bytes 11534340 | tf_op jit(solution)/shard_map/rbs,bhsf->rbhf/dot_general | solution.py:94
  61.5 6.5 %fusion.59 = f32[4,4,256,512]{3,2,1,0:T(8,128)} fusion(bf16[512,4,256,1]{2,0,3,1:T(8,128)(2,1)S(1)} %bitcast.404, bf16[6,4,4,256,256]{4,3,2,1,0:T(8,128)(2,1)} %bitcast.411, s32[]{:T(128)S(6)} %select_n.61), kind=kOutput, calls=%fused_computation.89 | convolution fusion | flops 1073741824 | bytes 11534340 | tf_op jit(solution)/shard_map/rbs,bhsf->rbhf/dot_general | solution.py:94
  77.5 6.4 %fusion.50 = f32[4,4,256,512]{3,2,1,0:T(8,128)} fusion(bf16[512,4,256,1]{0,2,3,1:T(8,128)(2,1)} %bitcast.138, bf16[6,4,4,256,256]{4,3,2,1,0:T(8,128)(2,1)} %bitcast.412, s32[]{:T(128)S(6)} %select_n.67), kind=kOutput, calls=%fused_computation.80 | convolution fusion | flops 1073741824 | bytes 11534340 | tf_op jit(solution)/shard_map/rbs,bhsf->rbhf/dot_general | solution.py:94
  83.9 6.4 %fusion.53 = f32[4,4,256,512]{3,2,1,0:T(8,128)} fusion(bf16[512,4,256,1]{0,2,3,1:T(8,128)(2,1)} %bitcast.136, bf16[6,4,4,256,256]{4,3,2,1,0:T(8,128)(2,1)} %bitcast.413, s32[]{:T(128)S(6)} %select_n.65), kind=kOutput, calls=%fused_computation.83 | convolution fusion | flops 1073741824 | bytes 11534340 | tf_op jit(solution)/shard_map/rbs,bhsf->rbhf/dot_general | solution.py:94
  90.3 22.6 %multiply_convert_fusion.2 = (bf16[512,4,4,256]{0,3,2,1:T(8,128)(2,1)}, f32[4,4,256,512]{3,2,1,0:T(8,128)}) fusion(bf16[512,4,256,1]{0,2,3,1:T(8,128)(2,1)} %bitcast.140, bf16[6,4,4,256,256]{4,3,2,1,0:T(8,128)(2,1)} %bitcast.414, s32[]{:T(128)S(6)} %select_n.69, f32[4,4]{1,0:T(4,128)S(1)} %convert_element_type.246, f32[4,4,256,512]{3,2,1,0:T(8,128)} %fusion.50, ...), kind=kOutput, calls=%fused_computation.18 | convolution fusion | flops 1113587712 | bytes 57672004 | tf_op jit(solution)/shard_map/rbs,bhsf->rbhf/dot_general | solution.py:94
  112.9 5.6 fusion.135
  138.1 5.5 fusion.25
  149.8 17.2 %collective-permute-done.5 = bf16[512,4,256]{2,0,1:T(8,128)(2,1)S(1)} collective-permute-done((bf16[512,4,256]{2,0,1:T(8,128)(2,1)}, bf16[512,4,256]{2,0,1:T(8,128)(2,1)S(1)}, u32[]{:S(2)}, u32[]{:S(2)}) %collective-permute-start.5) | collective-permute-done | bytes 1048608 | tf_op jit(solution)/shard_map/ppermute | solution.py:10
  170.7 6.2 fusion.70
  179.9 5.2 collective-permute-start.6
  197.7 4.6 fusion.181
  202.4 6.1 fusion.41
  208.6 6.1 fusion.44
  214.7 23.4 %collective-permute-done.11 = bf16[512,1024]{0,1:T(8,128)(2,1)} collective-permute-done((bf16[512,1024]{0,1:T(8,128)(2,1)S(1)}, bf16[512,1024]{0,1:T(8,128)(2,1)}, u32[]{:S(2)}, u32[]{:S(2)}) %collective-permute-start.11) | collective-permute-done | bytes 1048608 | tf_op jit(solution)/shard_map/ppermute | solution.py:10
  238.2 6.4 fusion.35
  244.6 6.4 fusion.38
  251.0 19.8 %fusion.6 = bf16[512,4,4,256]{0,3,2,1:T(8,128)(2,1)S(1)} fusion(f32[4,512,4,256]{1,3,2,0:T(8,128)} %fusion.181, f32[4,4,256,512]{3,2,1,0:T(8,128)} %get-tuple-element.66, f32[4,4,256,512]{3,2,1,0:T(8,128)} %fusion.35, f32[4,4,256,512]{3,2,1,0:T(8,128)} %fusion.38, f32[4,4,256,512]{3,2,1,0:T(8,128)} %fusion.41, f32[4,4,256,512]{3,2,1,0:T(8,128)} %fusion.44, ...), kind=kOutput, calls=%fused_computation.10 | convolution fusion | flops 1134559232 | bytes 57672004 | tf_op jit(solution)/shard_map/rbs,bhfs->rbhf/dot_general | solution.py:122
  280.9 4.5 multiply_bitcast_fusion.2
  285.3 4.5 multiply_bitcast_fusion.1
  289.8 4.6 multiply_bitcast_fusion
  294.4 5.3 copy.141
  299.7 5.2 copy.143
  304.9 5.2 copy.146
  310.2 5.3 copy.149
  315.4 5.2 copy.152
  320.7 13.7 %scatter.6 = f32[6,4,4,256,256]{3,4,2,1,0:T(8,128)} pad(f32[1,4,4,256,256]{3,4,2,1,0:T(8,128)} %convolution_bitcast_fusion.1, f32[]{:T(128)} %constant.136.clone.1), padding=0_5x0_0x0_0x0_0x0_0 | pad | bytes 29360132 | tf_op jit(solution)/shard_map/scatter | solution.py:143
  334.4 4.8 constant_dynamic-update-slice_fusion.4
  352.7 13.8 %multiply_convert_fusion.1 = bf16[6,4,4,256,256]{3,4,2,1,0:T(8,128)(2,1)} fusion(f32[6,4,4,256,256]{3,4,2,1,0:T(8,128)} %constant_dynamic-update-slice_fusion), kind=kLoop, calls=%fused_computation.1 | loop fusion | flops 12582912 | bytes 37748736 | tf_op jit(solution)/shard_map/convert_element_type | solution.py:156
  366.5 16.7 %copy.153 = bf16[6,16,256,256]{3,2,1,0:T(8,128)(2,1)} copy(bf16[6,16,256,256]{2,3,1,0:T(8,128)(2,1)} %bitcast.392) | data formatting | bytes 25165824 | tf_op jit(solution)/shard_map/convert_element_type | solution.py:156
  383.7 5.4 convolution_bitcast_fusion
  389.1 14.1 %scatter.9 = f32[6,4,4,256,256]{3,4,2,1,0:T(8,128)} pad(f32[1,4,4,256,256]{3,4,2,1,0:T(8,128)} %convolution_bitcast_fusion, f32[]{:T(128)} %constant.136.clone.1), padding=0_5x0_0x0_0x0_0x0_0 | pad | bytes 29360132 | tf_op jit(solution)/shard_map/scatter | solution.py:144
  403.2 5.8 bitcast_dynamic-update-slice_fusion.4
  412.4 4.5 bitcast_dynamic-update-slice_fusion.2
  416.9 4.5 bitcast_dynamic-update-slice_fusion.1
  421.4 4.4 bitcast_dynamic-update-slice_fusion
  425.8 14.3 %multiply_convert_fusion = bf16[6,4,4,256,256]{3,4,2,1,0:T(8,128)(2,1)} fusion(f32[6,4,4,256,256]{3,4,2,1,0:T(8,128)} %bitcast_dynamic-update-slice_fusion), kind=kLoop, calls=%fused_computation | loop fusion | flops 12582912 | bytes 37748736 | tf_op jit(solution)/shard_map/convert_element_type | solution.py:159
  440.2 16.7 %copy.164 = bf16[6,16,256,256]{3,2,1,0:T(8,128)(2,1)} copy(bf16[6,16,256,256]{2,3,1,0:T(8,128)(2,1)} %bitcast.393) | data formatting | bytes 25165824 | tf_op jit(solution)/shard_map/convert_element_type | solution.py:159
  457.6 5.4 fusion.150
  467.0 4.5 fusion.140
  479.6 5.9 fusion.15
  488.7 28.5 %collective-permute-done.15 = bf16[512,4,256]{0,2,1:T(8,128)(2,1)S(1)} collective-permute-done((bf16[512,4,256]{0,2,1:T(8,128)(2,1)}, bf16[512,4,256]{0,2,1:T(8,128)(2,1)S(1)}, u32[]{:S(2)}, u32[]{:S(2)}) %collective-permute-start.15) | collective-permute-done | bytes 1048608 | tf_op jit(solution)/shard_map/ppermute | solution.py:10
  518.2 5.7 fusion.65
  525.2 5.5 convert_element_type.282
  530.7 98.9 %reduce-scatter.5.cloned.1.call-done = bf16[6,16,64,256]{3,2,1,0:T(8,128)(2,1)} async-done(((bf16[6,16,256,256]{3,2,1,0:T(8,128)(2,1)}), bf16[6,16,64,256]{3,2,1,0:T(8,128)(2,1)}) %reduce-scatter.5.cloned.1.call-update) | async-done | bytes 3145744 | tf_op jit(solution)/shard_map/reduce_scatter | solution.py:158
  629.6 5.5 convert_element_type.285
  (166 shorter events, 119.6 us)
Async XLA Ops:
  7.2 18.9 %copy-start.11 = (bf16[512,1024]{1,0:T(8,128)(2,1)S(1)}, bf16[512,1024]{1,0:T(8,128)(2,1)}, u32[]{:S(2)}) copy-start(bf16[512,1024]{1,0:T(8,128)(2,1)} %param.11) | copy-start | bytes 3145732
  7.2 22.0 %copy-start.33 = (s32[5]{0:T(128)S(1)}, s32[5]{0:T(128)}, u32[]{:S(2)}) copy-start(s32[5]{0:T(128)} %param.15) | copy-start | bytes 64
  7.2 518.0 %reduce-scatter.3.cloned.1.call-start = ((), (), s32[]{:S(2)}) async-start(), calls=%async_computation.2 | async-start | bytes 15728640 | tf_op jit(solution)/shard_map/reduce_scatter | solution.py:155
  9.6 80.7 %collective-permute-start.2 = (bf16[512,1024]{0,1:T(8,128)(2,1)}, bf16[512,1024]{0,1:T(8,128)(2,1)}, u32[]{:S(2)}, u32[]{:S(2)}) collective-permute-start(bf16[512,1024]{0,1:T(8,128)(2,1)} %copy.85), channel_id=1, source_target_pairs={{0,4},{1,5},{2,6},{3,7},{4,0},{5,1},{6,2},{7,3},{8,12},{9,13},{10,... | collective-permute-start | bytes 3145736 | tf_op jit(solution)/shard_map/ppermute | solution.py:10
  13.6 63.8 %collective-permute-start.1 = (bf16[512,1024]{0,1:T(8,128)(2,1)}, bf16[512,1024]{0,1:T(8,128)(2,1)}, u32[]{:S(2)}, u32[]{:S(2)}) collective-permute-start(bf16[512,1024]{0,1:T(8,128)(2,1)} %copy.85), channel_id=1, source_target_pairs={{0,2},{1,3},{2,0},{3,1},{4,6},{5,7},{6,4},{7,5},{8,10},{9,11},{10,... | collective-permute-start | bytes 3145736 | tf_op jit(solution)/shard_map/ppermute | solution.py:10
  15.2 68.7 %collective-permute-start = (bf16[512,1024]{0,1:T(8,128)(2,1)}, bf16[512,1024]{0,1:T(8,128)(2,1)}, u32[]{:S(2)}, u32[]{:S(2)}) collective-permute-start(bf16[512,1024]{0,1:T(8,128)(2,1)} %copy.85), channel_id=1, source_target_pairs={{0,1},{1,0},{2,3},{3,2},{4,5},{5,4},{6,7},{7,6},{8,9},{9,8},{10,11... | collective-permute-start | bytes 3145736 | tf_op jit(solution)/shard_map/ppermute | solution.py:10
  16.8 168.4 %collective-permute-start.9 = (bf16[1,1024]{0,1:T(8,128)(2,1)}, bf16[1,1024]{0,1:T(8,128)(2,1)S(1)}, u32[]{:S(2)}, u32[]{:S(2)}) collective-permute-start(bf16[1,1024]{0,1:T(8,128)(2,1)} %copy.113), channel_id=1, source_target_pairs={{8,0},{16,8},{24,16},{9,1},{17,9},{25,17},{10,2},{18,10},{26,18},{... | collective-permute-start | bytes 6152 | tf_op jit(solution)/shard_map/ppermute | solution.py:21
  19.0 166.2 %collective-permute-start.8 = (bf16[1,1024]{0,1:T(8,128)(2,1)}, bf16[1,1024]{0,1:T(8,128)(2,1)}, u32[]{:S(2)}, u32[]{:S(2)}) collective-permute-start(bf16[1,1024]{0,1:T(8,128)(2,1)} %copy.112), channel_id=1, source_target_pairs={{0,8},{8,16},{16,24},{1,9},{9,17},{17,25},{2,10},{10,18},{18,26},{... | collective-permute-start | bytes 6152 | tf_op jit(solution)/shard_map/ppermute | solution.py:20
  34.2 20.8 %copy-start.12 = (bf16[512,1,2,2,256]{4,0,3,2,1:T(8,128)(2,1)}, bf16[512,1,2,2,256]{4,0,3,2,1:T(8,128)(2,1)S(1)}, u32[]{:S(2)}) copy-start(bf16[512,1,2,2,256]{4,0,3,2,1:T(8,128)(2,1)S(1)} %copy.83) | copy-start | bytes 3145732
  36.3 18.7 %copy-start.5 = (bf16[1,16,256,256]{3,2,1,0:T(8,128)(2,1)}, bf16[1,16,256,256]{3,2,1,0:T(8,128)(2,1)S(1)}, u32[]{:S(2)}) copy-start(bf16[1,16,256,256]{3,2,1,0:T(8,128)(2,1)S(1)} %slice.117) | copy-start | bytes 6291460
  54.9 6.5 %copy-start.14 = (bf16[512,2,2,1,256]{4,0,2,1,3:T(8,128)(2,1)S(1)}, bf16[512,2,2,1,256]{4,0,2,1,3:T(8,128)(2,1)}, u32[]{:S(2)}) copy-start(bf16[512,2,2,1,256]{4,0,2,1,3:T(8,128)(2,1)} %copy.81) | copy-start | bytes 3145732
  61.5 8.4 %copy-start.18 = (bf16[512,1024]{1,0:T(8,128)(2,1)S(1)}, bf16[512,1024]{1,0:T(8,128)(2,1)}, u32[]{:S(2)}) copy-start(bf16[512,1024]{1,0:T(8,128)(2,1)} %param.17) | copy-start | bytes 3145732
  61.5 13.6 %copy-start.22 = (s32[16,5]{0,1:T(8,128)S(1)}, s32[16,5]{0,1:T(8,128)}, u32[]{:S(2)}) copy-start(s32[16,5]{0,1:T(8,128)} %param.14) | copy-start | bytes 964
  75.6 52.2 %copy-start.25 = (bf16[4,4]{1,0:T(4,128)(2,1)}, bf16[4,4]{1,0:T(4,128)(2,1)S(1)}, u32[]{:S(2)}) copy-start(bf16[4,4]{1,0:T(4,128)(2,1)S(1)} %convert_element_type.249) | copy-start | bytes 100
  75.6 62.5 %copy-start.23 = (bf16[4,4]{1,0:T(4,128)(2,1)}, bf16[4,4]{1,0:T(4,128)(2,1)S(1)}, u32[]{:S(2)}) copy-start(bf16[4,4]{1,0:T(4,128)(2,1)S(1)} %convert_element_type.248) | copy-start | bytes 100
  75.6 37.3 %copy-start.31 = (bf16[4,4]{1,0:T(4,128)(2,1)}, bf16[4,4]{1,0:T(4,128)(2,1)S(1)}, u32[]{:S(2)}) copy-start(bf16[4,4]{1,0:T(4,128)(2,1)S(1)} %convert_element_type.258) | copy-start | bytes 100
  75.7 43.2 %copy-start.29 = (bf16[4,4]{1,0:T(4,128)(2,1)}, bf16[4,4]{1,0:T(4,128)(2,1)S(1)}, u32[]{:S(2)}) copy-start(bf16[4,4]{1,0:T(4,128)(2,1)S(1)} %convert_element_type.254) | copy-start | bytes 100
  75.7 47.7 %copy-start.27 = (bf16[4,4]{1,0:T(4,128)(2,1)}, bf16[4,4]{1,0:T(4,128)(2,1)S(1)}, u32[]{:S(2)}) copy-start(bf16[4,4]{1,0:T(4,128)(2,1)S(1)} %convert_element_type.250) | copy-start | bytes 100
  112.9 5.9 copy-start
  118.5 48.6 %collective-permute-start.5 = (bf16[512,4,256]{2,0,1:T(8,128)(2,1)}, bf16[512,4,256]{2,0,1:T(8,128)(2,1)S(1)}, u32[]{:S(2)}, u32[]{:S(2)}) collective-permute-start(bf16[512,4,256]{2,0,1:T(8,128)(2,1)} %fusion.135), channel_id=1, source_target_pairs={{0,4},{1,5},{2,6},{3,7},{4,0},{5,1},{6,2},{7,3},{8,12},{9,13},{10,... | collective-permute-start | bytes 3145736 | tf_op jit(solution)/shard_map/ppermute | solution.py:10
  123.2 4.6 copy-start.21
  123.2 47.4 %collective-permute-start.4 = (bf16[512,4,256]{2,0,1:T(8,128)(2,1)}, bf16[512,4,256]{2,0,1:T(8,128)(2,1)}, u32[]{:S(2)}, u32[]{:S(2)}) collective-permute-start(bf16[512,4,256]{2,0,1:T(8,128)(2,1)} %fusion.130), channel_id=1, source_target_pairs={{0,2},{1,3},{2,0},{3,1},{4,6},{5,7},{6,4},{7,5},{8,10},{9,11},{10,... | collective-permute-start | bytes 3145736 | tf_op jit(solution)/shard_map/ppermute | solution.py:10
  127.8 42.9 %collective-permute-start.3 = (bf16[512,4,256]{2,0,1:T(8,128)(2,1)}, bf16[512,4,256]{2,0,1:T(8,128)(2,1)}, u32[]{:S(2)}, u32[]{:S(2)}) collective-permute-start(bf16[512,4,256]{2,0,1:T(8,128)(2,1)} %fusion.125), channel_id=1, source_target_pairs={{0,1},{1,0},{2,3},{3,2},{4,5},{5,4},{6,7},{7,6},{8,9},{9,8},{10,11... | collective-permute-start | bytes 3145736 | tf_op jit(solution)/shard_map/ppermute | solution.py:10
  167.1 3.6 copy-start.19
  177.7 12.1 %collective-permute-start.7 = (bf16[1,1024]{0,1:T(8,128)(2,1)}, bf16[1,1024]{0,1:T(8,128)(2,1)}, u32[]{:S(2)}, u32[]{:S(2)}) collective-permute-start(bf16[1,1024]{0,1:T(8,128)(2,1)} %copy.111), channel_id=1, source_target_pairs={{8,0},{16,8},{24,16},{9,1},{17,9},{25,17},{10,2},{18,10},{26,18},{... | collective-permute-start | bytes 6152 | tf_op jit(solution)/shard_map/ppermute | solution.py:21
  179.9 9.9 %collective-permute-start.6 = (bf16[1,1024]{0,1:T(8,128)(2,1)}, bf16[1,1024]{0,1:T(8,128)(2,1)}, u32[]{:S(2)}, u32[]{:S(2)}) collective-permute-start(bf16[1,1024]{0,1:T(8,128)(2,1)} %copy.109), channel_id=1, source_target_pairs={{0,8},{8,16},{16,24},{1,9},{9,17},{17,25},{2,10},{10,18},{18,26},{... | collective-permute-start | bytes 6152 | tf_op jit(solution)/shard_map/ppermute | solution.py:20
  195.8 42.4 %collective-permute-start.11 = (bf16[512,1024]{0,1:T(8,128)(2,1)S(1)}, bf16[512,1024]{0,1:T(8,128)(2,1)}, u32[]{:S(2)}, u32[]{:S(2)}) collective-permute-start(bf16[512,1024]{0,1:T(8,128)(2,1)S(1)} %get-tuple-element.58), channel_id=1, source_target_pairs={{0,2},{1,3},{2,0},{3,1},{4,6},{5,7},{6,4},{7,5},{8,10},{9,11},{10,... | collective-permute-start | bytes 3145736 | tf_op jit(solution)/shard_map/ppermute | solution.py:10
  195.8 48.8 %collective-permute-start.10 = (bf16[512,1024]{0,1:T(8,128)(2,1)S(1)}, bf16[512,1024]{0,1:T(8,128)(2,1)}, u32[]{:S(2)}, u32[]{:S(2)}) collective-permute-start(bf16[512,1024]{0,1:T(8,128)(2,1)S(1)} %get-tuple-element.58), channel_id=1, source_target_pairs={{0,1},{1,0},{2,3},{3,2},{4,5},{5,4},{6,7},{7,6},{8,9},{9,8},{10,11... | collective-permute-start | bytes 3145736 | tf_op jit(solution)/shard_map/ppermute | solution.py:10
  195.8 55.2 %collective-permute-start.12 = (bf16[512,1024]{0,1:T(8,128)(2,1)S(1)}, bf16[512,1024]{0,1:T(8,128)(2,1)}, u32[]{:S(2)}, u32[]{:S(2)}) collective-permute-start(bf16[512,1024]{0,1:T(8,128)(2,1)S(1)} %get-tuple-element.58), channel_id=1, source_target_pairs={{0,4},{1,5},{2,6},{3,7},{4,0},{5,1},{6,2},{7,3},{8,12},{9,13},{10,... | collective-permute-start | bytes 3145736 | tf_op jit(solution)/shard_map/ppermute | solution.py:10
  251.0 19.9 %copy-start.16 = (bf16[512,4,256]{2,1,0:T(4,128)(2,1)S(1)}, bf16[512,4,256]{2,1,0:T(4,128)(2,1)}, u32[]{:S(2)}) copy-start(bf16[512,4,256]{2,1,0:T(4,128)(2,1)} %reshape.276) | copy-start | bytes 3145732
  270.8 19.0 %copy-start.2 = (bf16[512,4,4,256]{0,3,2,1:T(8,128)(2,1)}, bf16[512,4,4,256]{0,3,2,1:T(8,128)(2,1)S(1)}, u32[]{:S(2)}) copy-start(bf16[512,4,4,256]{0,3,2,1:T(8,128)(2,1)S(1)} %fusion.6) | copy-start | bytes 12582916
  270.8 3.4 copy-start.15
  274.2 3.3 copy-start.13
  334.4 4.8 copy-start.10
  339.2 3.7 copy-start.9
  342.9 3.7 copy-start.8
  346.6 3.7 copy-start.7
  383.2 246.4 %reduce-scatter.5.cloned.1.call-start = ((), (), s32[]{:S(2)}) async-start(), calls=%async_computation.3 | async-start | bytes 15728640 | tf_op jit(solution)/shard_map/reduce_scatter | solution.py:158
  403.2 5.8 copy-start.1
  457.6 5.4 copy-start.3
  457.6 5.4 copy-start.30
  463.0 4.0 copy-start.28
  467.0 5.5 copy-start.17
  467.0 6.8 %copy-start.26 = (bf16[4,4]{1,0:T(4,128)(2,1)S(1)}, bf16[4,4]{1,0:T(4,128)(2,1)}, u32[]{:S(2)}) copy-start(bf16[4,4]{1,0:T(4,128)(2,1)} %copy-done.25) | copy-start | bytes 100
  471.5 45.7 %collective-permute-start.15 = (bf16[512,4,256]{0,2,1:T(8,128)(2,1)}, bf16[512,4,256]{0,2,1:T(8,128)(2,1)S(1)}, u32[]{:S(2)}, u32[]{:S(2)}) collective-permute-start(bf16[512,4,256]{0,2,1:T(8,128)(2,1)} %fusion.150), channel_id=1, source_target_pairs={{0,4},{1,5},{2,6},{3,7},{4,0},{5,1},{6,2},{7,3},{8,12},{9,13},{10,... | collective-permute-start | bytes 3145736 | tf_op jit(solution)/shard_map/ppermute | solution.py:10
  471.5 45.9 %collective-permute-start.14 = (bf16[512,4,256]{0,2,1:T(8,128)(2,1)}, bf16[512,4,256]{0,2,1:T(8,128)(2,1)}, u32[]{:S(2)}, u32[]{:S(2)}) collective-permute-start(bf16[512,4,256]{0,2,1:T(8,128)(2,1)} %fusion.145), channel_id=1, source_target_pairs={{0,2},{1,3},{2,0},{3,1},{4,6},{5,7},{6,4},{7,5},{8,10},{9,11},{10,... | collective-permute-start | bytes 3145736 | tf_op jit(solution)/shard_map/ppermute | solution.py:10
  472.5 45.7 %collective-permute-start.13 = (bf16[512,4,256]{0,2,1:T(8,128)(2,1)}, bf16[512,4,256]{0,2,1:T(8,128)(2,1)}, u32[]{:S(2)}, u32[]{:S(2)}) collective-permute-start(bf16[512,4,256]{0,2,1:T(8,128)(2,1)} %fusion.140), channel_id=1, source_target_pairs={{0,1},{1,0},{2,3},{3,2},{4,5},{5,4},{6,7},{7,6},{8,9},{9,8},{10,11... | collective-permute-start | bytes 3145736 | tf_op jit(solution)/shard_map/ppermute | solution.py:10
  485.5 32.7 %copy-start.6 = (bf16[1,16,256,256]{3,2,1,0:T(8,128)(2,1)S(1)}, bf16[1,16,256,256]{3,2,1,0:T(8,128)(2,1)}, u32[]{:S(2)}) copy-start(bf16[1,16,256,256]{3,2,1,0:T(8,128)(2,1)} %copy-done.5) | copy-start | bytes 6291460
  (4 other events, 5.3 us)
Sparse Core Ops, SparseCore 0:
  383.3 122.3 reduce-scatter.2
  508.8 120.7 reduce-scatter.4
where the time goes:
time: 654 us; the launch traced here: 642 us
  matrix products  216 us (33%)
  waiting for transfers between devices  172 us (26%)
  local copies, waits for them, and re-layouts  159 us (24%)
  other arithmetic  51.8 us (8%)
  starting transfers between devices  22.6 us (3%)
  between operations  21.1 us (3%)
    reduce_scatter x1, waiting for transfers between devices, local(): lax.psum_scatter((down_stack * scale).astype(jnp.bfloat16), 'seq', scatte...  98.9 us
    ppermute x12, waiting for transfers between devices, swapped(): lax.ppermute(array, axis, [(i, i ^ 1 << stride) for i in range(lax.axis_s...  73 us
    dot_general x5, matrix products, local(): jnp.einsum('rbs,bhsf->rbhf', moved, up_of[bit], preferred_element_type=f32)  48.4 us
    dot_general x5, matrix products, local(): jnp.einsum('rbs,bhfs->rbhf', moved, down_of[bit], preferred_element_type=...  44.9 us
    broadcast_in_dim x5, local copies, waits for them, and re-layouts, local(): lax.dynamic_update_index_in_dim(up_stack, up_terms[bit + 1], level_of[bit...  26.2 us
    rev x10, local copies, waits for them, and re-layouts, flip_blocks(): return shaped[:, :, ::-1].reshape(rows_dev, count, width)  24.5 us
    dot_general x5, matrix products, local(): jnp.einsum('rbhf,bhfs->rbs', masked, down_of[bit], preferred_element_type...  24.2 us
    dot_general x5, matrix products, local(): jnp.einsum('rbhf,bhsf->rbs', masked, up_of[bit], preferred_element_type=f32)  24 us
  transfers between devices with their start and end apart: 18, of which 6 were waited for; matrix products, arithmetic and copies ran while one was open for 43% of the time, Pallas kernels for 0%

commit v1 on v0

v1 whole, which is shorter than its diff:
```python
import functools
import math

import jax
import jax.numpy as jnp
from jax import lax
from jax.experimental import pallas as pl
from jax.experimental.pallas import tpu as pltpu
from jax.sharding import PartitionSpec as P

coef = 0.7978845608028654
cubic = 0.044715
f32 = jnp.float32
bf16 = jnp.bfloat16
VMEM_LIMIT = 56 * 1024 * 1024
ANY = pl.BlockSpec(memory_space=pl.ANY)


def swapped(array, axis, bit):
    return lax.ppermute(array, axis, [(i, i ^ 1 << bit) for i in range(lax.axis_size(axis))])


def after(value, *others):
    return lax.optimization_barrier((value,) + others)[0]


def cost(flops, moved, transcendentals=0):
    return pl.CostEstimate(flops=flops, bytes_accessed=moved, transcendentals=transcendentals)


def halo(array):
    peers = lax.axis_size("seq")
    up = [(i, i + 1) for i in range(peers - 1)]
    down = [(i + 1, i) for i in range(peers - 1)]
    rows = array.shape[0]
    before = lax.ppermute(lax.slice_in_dim(array, rows - 1, rows), "seq", up)
    behind = lax.ppermute(lax.slice_in_dim(array, 0, 1), "seq", down)
    return before, behind


def convolution_kernel(x_ref, before_ref, behind_ref, taps_ref, out_ref, *, order, blocked):
    x = x_ref[...].astype(f32)
    rows = x.shape[0]
    at = lax.broadcasted_iota(jnp.int32, x.shape, 0)
    earlier = jnp.where(at == 0, before_ref[...].astype(f32), pltpu.roll(x, 1, 0))
    later = jnp.where(at == rows - 1, behind_ref[...].astype(f32), pltpu.roll(x, rows - 1, 0))
    first, middle, last = order
    out = (
        taps_ref[first : first + 1, :] * earlier
        + taps_ref[middle : middle + 1, :] * x
        + taps_ref[last : last + 1, :] * later
    ).astype(bf16)
    if blocked:
        out_ref[0] = out
    else:
        out_ref[...] = out


def convolution(x, before, behind, taps, order, width, blocked):
    rows, local = x.shape
    column = lambda r: pl.BlockSpec((r, width), lambda i: (0, i))
    if blocked:
        shape = jax.ShapeDtypeStruct((local // width, rows, width), bf16)
        out_spec = pl.BlockSpec((1, rows, width), lambda i: (i, 0, 0))
    else:
        shape = jax.ShapeDtypeStruct((rows, local), bf16)
        out_spec = column(rows)
    return pl.pallas_call(
        functools.partial(convolution_kernel, order=order, blocked=blocked),
        out_shape=shape,
        grid=(local // width,),
        in_specs=[column(rows), column(1), column(1), column(3)],
        out_specs=out_spec,
        compiler_params=pltpu.CompilerParams(vmem_limit_bytes=VMEM_LIMIT),
        cost_estimate=cost(10 * rows * local, 4 * rows * local),
        name="convolution",
    )(x, before, behind, taps)


def layer_kernel(
    level_bits, pattern, place, *refs, first, ratio, levels, local_bits, remote_bits, peers, scale
):
    terms = 1 + levels
    x_refs, refs = refs[:terms], refs[terms:]
    g_refs, refs = refs[:terms], refs[terms:]
    u_ref, d_ref = refs[:2]
    sends = refs[2:6]
    home_ref = refs[6]
    away_refs = refs[7 : 7 + remote_bits]
    x_all, x_turned, g_all, u_all, d_all, h_all, p_all, turned = refs[7 + remote_bits :]
    jj, h = pl.program_id(0), pl.program_id(1)
    rows, width = x_refs[0].shape[1:]
    slab = width // peers
    k = (first + jj) * ratio + h
    me = place[0]
    stages = peers.bit_length() - 1

    level_at, present = [], []
    for bit in range(levels):
        at = jnp.int32(0)
        for level in range(levels):
            at = at + jnp.where(level_bits[level] == bit, level, 0)
        level_at.append(at + 1)
        present.append(pattern[k, at])

    def rearranged(target, base):
        for r in range(peers):
            start = pl.multiple_of((me ^ r) * slab, slab)
            target[base + r * slab : base + (r + 1) * slab, :] = turned[pl.ds(start, slab), :]

    @pl.when(h == 0)
    def _():
        for b in range(terms):
            block = x_refs[b][0]
            x_all[:, b * width : (b + 1) * width] = block
            g_all[:, b * width : (b + 1) * width] = g_refs[b][0]
            turned[...] = block.T
            rearranged(x_turned, b * width)

    wide = pl.ds(pl.multiple_of(h * width, width), width)
    for b in range(terms):
        if b == 0:
            u, d = u_ref[0, 0], d_ref[0, 0]
        else:
            mask = present[b - 1].astype(f32).astype(bf16)
            u, d = u_ref[level_at[b - 1], 0] * mask, d_ref[level_at[b - 1], 0] * mask
        u_all[h, b * width : (b + 1) * width, :] = u
        d_all[wide, b * width : (b + 1) * width] = d

    pre = jnp.dot(x_all[...], u_all[h], preferred_element_type=f32)
    square = pre * pre
    inner = jnp.tanh(coef * (pre + cubic * (square * pre)))
    half = 0.5 * (1.0 + inner)
    slope = half + (0.5 * coef) * pre * (1.0 - inner * inner) * (1.0 + (3.0 * cubic) * square)
    hidden = (pre * half).astype(bf16)
    h_all[h] = hidden
    turned[...] = hidden.T
    hidden_turned = jnp.concatenate(
        [
            turned[pl.ds(pl.multiple_of((me ^ r) * slab, slab), slab), :]
            for r in range(peers)
        ],
        axis=0,
    )
    grad_hidden = lax.dot_general(
        g_all[...], d_all[wide, :], (((1,), (1,)), ((), ())), preferred_element_type=f32
    )
    grad_pre = (grad_hidden * slope).astype(bf16)
    p_all[h] = grad_pre

    for b in range(terms):
        span = slice(b * width, (b + 1) * width)
        up = jnp.dot(x_turned[span, :], grad_pre, preferred_element_type=f32)
        down = jnp.dot(hidden_turned, g_all[:, span], preferred_element_type=f32)
        if b == 0:
            factor, slot = scale, 0
        else:
            factor, slot = present[b - 1].astype(f32) * scale, level_at[b - 1]
        up, down = (up * factor).astype(bf16), (down * factor).astype(bf16)
        for value, sent, kept, bit in ((up, sends[0], sends[1], 0), (down, sends[2], sends[3], stages - 1)):
            counts = [0, 0]
            for r in range(peers):
                which = r >> bit & 1
                target = sent if which else kept
                target[counts[which], slot, 0] = value[r * slab : (r + 1) * slab, :]
                counts[which] += 1

    @pl.when(h == ratio - 1)
    def _():
        for b in range(terms):
            span = slice(b * width, (b + 1) * width)
            for side in range(2):
                total = None
                for other in range(ratio):
                    if side == 0:
                        part = jnp.dot(
                            h_all[other],
                            d_all[other * width : (other + 1) * width, span],
                            preferred_element_type=f32,
                        )
                    else:
                        part = lax.dot_general(
                            p_all[other],
                            u_all[other, span, :],
                            (((1,), (1,)), ((), ())),
                            preferred_element_type=f32,
                        )
                    total = part if total is None else total + part
                total = total.astype(bf16)
                if b <= local_bits:
                    home_ref[side, b, 0] = total
                else:
                    away_refs[b - 1 - local_bits][side, 0] = total


def layer(level_bits, pattern, place, x_home, g_home, x_away, g_away, up_factors, down_factors, first, count, peers, scale):
    terms, hidden_dev, width, _ = up_factors.shape
    levels = terms - 1
    blocks_dev, rows, _ = x_home.shape
    ratio = hidden_dev // blocks_dev
    local_bits = blocks_dev.bit_length() - 1
    remote_bits = levels - local_bits
    slab = width // peers
    home = [
        pl.BlockSpec((1, rows, width), lambda j, h, *s, flip=flip: ((first + j) ^ flip, 0, 0))
        for flip in [0] + [1 << bit for bit in range(local_bits)]
    ]
    away = [pl.BlockSpec((1, rows, width), lambda j, h, *s: (j, 0, 0))] * remote_bits
    weight = pl.BlockSpec((terms, 1, width, width), lambda j, h, *s: (0, (first + j) * ratio + h, 0, 0))
    piece = pl.BlockSpec((peers // 2, terms, 1, slab, width), lambda j, h, *s: (0, 0, j * ratio + h, 0, 0))
    piece_shape = jax.ShapeDtypeStruct((peers // 2, terms, count * ratio, slab, width), bf16)
    home_out = pl.BlockSpec((2, 1 + local_bits, 1, rows, width), lambda j, h, *s: (0, 0, j, 0, 0))
    away_out = pl.BlockSpec((2, 1, rows, width), lambda j, h, *s: (0, j, 0, 0))
    steps = count * ratio
    outs = pl.pallas_call(
        functools.partial(
            layer_kernel,
            first=first,
            ratio=ratio,
            levels=levels,
            local_bits=local_bits,
            remote_bits=remote_bits,
            peers=peers,
            scale=scale,
        ),
        out_shape=[piece_shape] * 4
        + [jax.ShapeDtypeStruct((2, 1 + local_bits, count, rows, width), bf16)]
        + [jax.ShapeDtypeStruct((2, count, rows, width), bf16)] * remote_bits,
        grid_spec=pltpu.PrefetchScalarGridSpec(
            num_scalar_prefetch=3,
            grid=(count, ratio),
            in_specs=home + away + home + away + [weight] * 2,
            out_specs=[piece] * 4 + [home_out] + [away_out] * remote_bits,
            scratch_shapes=[
                pltpu.VMEM((rows, terms * width), bf16),
                pltpu.VMEM((terms * width, rows), bf16),
                pltpu.VMEM((rows, terms * width), bf16),
                pltpu.VMEM((ratio, terms * width, width), bf16),
                pltpu.VMEM((ratio * width, terms * width), bf16),
                pltpu.VMEM((ratio, rows, width), bf16),
                pltpu.VMEM((ratio, rows, width), bf16),
                pltpu.VMEM((width, rows), bf16),
            ],
        ),
        compiler_params=pltpu.CompilerParams(vmem_limit_bytes=VMEM_LIMIT),
        cost_estimate=cost(
            12 * steps * terms * rows * width * width,
            2 * steps * terms * width * width * 4 + 8 * count * terms * rows * width,
            steps * rows * width,
        ),
        name="layer",
    )(
        level_bits, pattern, place,
        *[x_home] * len(home), *x_away, *[g_home] * len(home), *g_away, up_factors, down_factors,
    )
    return outs[:4], outs[4], outs[5:]


def pair_kernel(kept_ref, got_ref, next_sent_ref, next_kept_ref, *, bit):
    counts = [0, 0]
    for r in range(kept_ref.shape[0]):
        which = r >> bit & 1
        total = (kept_ref[r].astype(f32) + got_ref[r].astype(f32)).astype(bf16)
        target = next_sent_ref if which else next_kept_ref
        target[counts[which]] = total
        counts[which] += 1


def pair_sum(kept, got, bit):
    parts, terms, blocks, slab, width = kept.shape
    spec = lambda n: pl.BlockSpec((n, 1, blocks, slab, width), lambda i: (0, i, 0, 0, 0))
    half = jax.ShapeDtypeStruct((parts // 2, terms, blocks, slab, width), bf16)
    return pl.pallas_call(
        functools.partial(pair_kernel, bit=bit),
        out_shape=[half, half],
        grid=(terms,),
        in_specs=[spec(parts)] * 2,
        out_specs=[spec(parts // 2)] * 2,
        compiler_params=pltpu.CompilerParams(vmem_limit_bytes=VMEM_LIMIT),
        cost_estimate=cost(kept.size, 6 * kept.size),
        name="pair_sum",
    )(kept, got)


def finish_kernel(a_kept, a_got, b_kept, b_got, *refs):
    a_out, b_out = refs[-2:]
    a_out[...] = a_kept[0].astype(f32) + a_got[0].astype(f32)
    b_out[...] = b_kept[0].astype(f32) + b_got[0].astype(f32)


def finish(a_kept, a_got, b_kept, b_got, outs, first, hidden_dev):
    _, terms, blocks, slab, width = a_kept.shape
    spec = pl.BlockSpec((1, terms, 1, slab, width), lambda i: (0, 0, i, 0, 0))
    out_spec = pl.BlockSpec((terms, 1, slab, width), lambda i: (0, first + i, 0, 0))
    shape = jax.ShapeDtypeStruct((terms, hidden_dev, slab, width), f32)
    extra = [] if outs is None else list(outs)
    return pl.pallas_call(
        finish_kernel,
        out_shape=[shape, shape],
        grid=(blocks,),
        in_specs=[spec] * 4 + [ANY] * len(extra),
        out_specs=[out_spec] * 2,
        input_output_aliases={4 + i: i for i in range(len(extra))},
        compiler_params=pltpu.CompilerParams(vmem_limit_bytes=VMEM_LIMIT),
        cost_estimate=cost(2 * a_kept.size, 16 * a_kept.size),
        name="finish",
    )(a_kept, a_got, b_kept, b_got, *extra)


def combine_kernel(*refs, sizes, remote_bits, local_bits, blocks_dev):
    homes, refs = refs[: len(sizes)], refs[len(sizes) :]
    aways, (mixed_ref, grad_ref) = refs[:-2], refs[-2:]
    where = [(g, i) for g, size in enumerate(sizes) for i in range(size)]
    width = homes[0].shape[-1]
    for j in range(blocks_dev):
        for side, target in ((0, mixed_ref), (1, grad_ref)):
            g, i = where[j]
            total = homes[g][side, 0, i].astype(f32)
            for bit in range(local_bits):
                g, i = where[j ^ 1 << bit]
                total = total + homes[g][side, 1 + bit, i].astype(f32)
            g, i = where[j]
            for bit in range(remote_bits):
                total = total + aways[g * remote_bits + bit][side, i].astype(f32)
            target[:, j * width : (j + 1) * width] = total.astype(bf16)


def combine(homes, aways, sizes, blocks_dev):
    rows, width = homes[0].shape[-2:]
    local_bits, remote_bits = homes[0].shape[1] - 1, len(aways[0])
    chunk = min(rows, 128)
    home = [pl.BlockSpec((2, 1 + local_bits, n, chunk, width), lambda i: (0, 0, 0, i, 0)) for n in sizes]
    away = [pl.BlockSpec((2, n, chunk, width), lambda i: (0, 0, i, 0)) for n in sizes for _ in range(remote_bits)]
    out = pl.BlockSpec((chunk, blocks_dev * width), lambda i: (i, 0))
    shape = jax.ShapeDtypeStruct((rows, blocks_dev * width), bf16)
    return pl.pallas_call(
        functools.partial(
            combine_kernel, sizes=sizes, remote_bits=remote_bits, local_bits=local_bits, blocks_dev=blocks_dev
        ),
        out_shape=[shape, shape],
        grid=(rows // chunk,),
        in_specs=home + away,
        out_specs=[out, out],
        compiler_params=pltpu.CompilerParams(vmem_limit_bytes=VMEM_LIMIT),
        cost_estimate=cost(12 * shape.size, 28 * shape.size),
        name="combine",
    )(*homes, *[part for group in aways for part in group])


def local(frames, up_factors, down_factors, pattern, level_bits, taps, cotangent):
    rows, local_width = frames.shape
    terms, hidden_dev, width, _ = up_factors.shape
    blocks_dev = local_width // width
    ratio = hidden_dev // blocks_dev
    levels = terms - 1
    local_bits = blocks_dev.bit_length() - 1
    remote_bits = levels - local_bits
    peers = lax.axis_size("seq")
    stages = peers.bit_length() - 1
    scale = 1.0 / math.sqrt(rows * peers)
    place = lax.axis_index("seq").astype(jnp.int32).reshape(1)
    sizes = [1] * blocks_dev
    starts = [sum(sizes[:g]) for g in range(len(sizes))]
    bits = range(remote_bits)

    before, behind = halo(cotangent)
    x_home = frames.reshape(rows, blocks_dev, width).transpose(1, 0, 2)

    def fetch(pieces):
        return [swapped(piece, "tensor", bit) for bit, piece in zip(bits, pieces)]

    x_first = x_home[: sizes[0]]
    x_away = [fetch([x_first] * remote_bits)]
    g_home = convolution(cotangent, before, behind, taps, (2, 1, 0), width, True)
    g_away = [fetch([g_home[: sizes[0]]] * remote_bits)]

    grads, homes, aways = [], [], []
    outs = None
    pending = []

    def start_sums(pieces):
        up_sent, up_kept, down_sent, down_kept = pieces
        return {
            "up": (up_kept, swapped(up_sent, "seq", 0)),
            "down": (down_kept, swapped(down_sent, "seq", stages - 1)),
            "done": 1,
        }

    def next_sums(state, behind_value):
        stage = state["done"]
        order_up = list(range(stages))
        order_down = order_up[::-1]
        result = {"done": stage + 1}
        for name, order in (("up", order_up), ("down", order_down)):
            kept, got = state[name]
            if behind_value is not None:
                got = after(got, behind_value)
            remaining = [bit for bit in range(stages) if bit not in order[:stage]]
            sent, kept = pair_sum(kept, got, remaining.index(order[stage]))
            result[name] = (kept, swapped(sent, "seq", order[stage]))
        return result

    for g, (first, size) in enumerate(zip(starts, sizes)):
        if g + 1 < len(sizes):
            nxt = slice(starts[g + 1], starts[g + 1] + sizes[g + 1])
            both = jnp.stack([x_home[nxt], g_home[nxt]])
            tied = [after(both, x_away[g][bit], g_away[g][bit]) for bit in bits]
            arrived = fetch(tied)
            x_away.append([value[0] for value in arrived])
            g_away.append([value[1] for value in arrived])
        pieces, home, away = layer(
            level_bits, pattern, place, x_home, g_home, x_away[g], g_away[g],
            up_factors, down_factors, first, size, peers, scale,
        )
        homes.append(home)
        state = start_sums(pieces)
        aways.append(fetch(away))
        for index, older in enumerate(pending):
            if older["done"] < stages:
                pending[index] = next_sums(older, home)
        pending.append(state)

    while any(state["done"] < stages for state in pending):
        for index, older in enumerate(pending):
            if older["done"] < stages:
                pending[index] = next_sums(older, None)
    mixed, grad_frames = combine(homes, aways, sizes, blocks_dev)
    before, behind = halo(mixed)
    convolved = convolution(mixed, before, behind, taps, (0, 1, 2), width, False)
    for state, first in zip(pending, starts):
        outs = finish(*state["up"], *state["down"], outs, first * ratio, hidden_dev)
    return convolved, grad_frames, outs[0], outs[1]


def solution(mesh):
    in_specs = (
        P("seq", "tensor"),
        P(None, "tensor", None, None),
        P(None, "tensor", None, None),
        P("tensor", None),
        P(),
        P(None, "tensor"),
        P("seq", "tensor"),
    )
    out_specs = (
        P("seq", "tensor"),
        P("seq", "tensor"),
        P(None, "tensor", "seq", None),
        P(None, "tensor", "seq", None),
    )
    return jax.shard_map(local, mesh=mesh, in_specs=in_specs, out_specs=out_specs, check_vma=False)
```

time: 654 us -> 369 us (0.56); the launches traced: 642 us -> 367 us
  matrix products: 216 us -> 0 us
  Pallas kernels: 0 us -> 145 us
  local copies, waits for them, and re-layouts: 159 us -> 19.6 us
  other arithmetic: 51.8 us -> 0.15 us
  starting transfers between devices: 22.6 us -> 55.7 us
  waiting for transfers between devices: 172 us -> 145 us
  between operations: 21.1 us -> 1.15 us
    dot_general x36 -> x0, matrix products: 216 us -> none  [the longest x5 48.4 us: local(): jnp.einsum('rbs,bhsf->rbhf', moved, up_of[bit], preferred_element_type=f32)]
    pallas_call x0 -> x19, Pallas kernels: none -> 145 us  [the longest x4 73.8 us: layer(): pl.pallas_call(functools.partial(layer_kernel, first=first, ratio=ratio,...]
    reduce_scatter x2 -> x0, waiting for transfers between devices: 98.9 us -> none  [the longest x1 98.9 us: local(): lax.psum_scatter((down_stack * scale).astype(jnp.bfloat16), 'seq', scatte...]
    ppermute x16 -> x47, waiting for transfers between devices: 73 us -> 145 us  [the longest x43 119 us: swapped(): lax.ppermute(array, axis, [(i, i ^ 1 << bit) for i in range(lax.axis_size...]
    convert_element_type x17 -> x0, other arithmetic: 48.3 us -> none  [the longest x1 14.3 us: local(): (down_stack * scale).astype(jnp.bfloat16)]
    convert_element_type x8 -> x0, local copies, waits for them, and re-layouts: 35.2 us -> none  [the longest x1 16.7 us: local(): (down_stack * scale).astype(jnp.bfloat16)]
    ppermute x16 -> x47, starting transfers between devices: 22.1 us -> 55.7 us  [the longest x43 46.1 us: swapped(): lax.ppermute(array, axis, [(i, i ^ 1 << bit) for i in range(lax.axis_size...]
    scatter x2 -> x0, local copies, waits for them, and re-layouts: 27.8 us -> none  [the longest x1 14.1 us: local(): down_stack = jnp.zeros(shape_five, f32).at[0].set(down_terms[0])]
  transfers between devices with their start and end apart: 18 -> 47, of which waited for: 6 -> 17; matrix products, arithmetic and copies ran while one was open for 43% -> 3% of each run, Pallas kernels for 0% -> 38%
where the time goes in v1:
time: 369 us; the launch traced here: 367 us
  waiting for transfers between devices  145 us (39%)
  Pallas kernels  145 us (39%)
  starting transfers between devices  55.7 us (15%)
  local copies, waits for them, and re-layouts  19.6 us (5%)
    ppermute x43, waiting for transfers between devices, swapped(): lax.ppermute(array, axis, [(i, i ^ 1 << bit) for i in range(lax.axis_size...  119 us
    pallas_call x4, Pallas kernels, layer(): pl.pallas_call(functools.partial(layer_kernel, first=first, ratio=ratio,...  73.8 us
    ppermute x43, starting transfers between devices, swapped(): lax.ppermute(array, axis, [(i, i ^ 1 << bit) for i in range(lax.axis_size...  46.1 us
    pallas_call x8, Pallas kernels, pair_sum(): pl.pallas_call(functools.partial(pair_kernel, bit=bit), out_shape=[half,...  39.1 us
    ppermute x2, waiting for transfers between devices, halo(): behind = lax.ppermute(lax.slice_in_dim(array, 0, 1), 'seq', down)  26.6 us
    pallas_call x4, Pallas kernels, finish(): pl.pallas_call(finish_kernel, out_shape=[shape, shape], grid=(blocks,), i...  17.2 us
    unnamed x92, local copies, waits for them, and re-layouts  8.76 us
    squeeze x9, local copies, waits for them, and re-layouts, local(): g_away.append([value[1] for value in arrived])  7.54 us
  transfers between devices with their start and end apart: 47, of which 17 were waited for; matrix products, arithmetic and copies ran while one was open for 3% of the time, Pallas kernels for 38%

profile of v1, /device:TPU:0, one launch (start us, length us, event | category | flops | bytes accessed | tf_op | source)
XLA Modules:
  0.0 366.7 jit_solution(16216139517949051389)
XLA Ops:
  2.8 4.1 %collective-permute-start.2 = (bf16[1,512,256]{2,1,0:T(8,128)(2,1)S(1)}, bf16[1,512,256]{2,1,0:T(8,128)(2,1)S(1)}, u32[]{:S(2)}, u32[]{:S(2)}) collective-permute-start(bf16[1,512,256]{2,1,0:T(8,128)(2,1)S(1)} %get-tuple-element.155), channel_id=1, source_target_pairs={{0,4},{1,5},{2,6},{3,7},{4,0},{5,1},{6,2},{7,3},{8,12},{9,13},{10,... | collective-permute-start | bytes 786440 | tf_op jit(solution)/shard_map/ppermute | solution.py:20
  8.9 4.5 %collective-permute-start.3 = (bf16[1,1024]{1,0:T(2,128)(2,1)S(1)}, bf16[1,1024]{1,0:T(2,128)(2,1)S(1)}, u32[]{:S(2)}, u32[]{:S(2)}) collective-permute-start(bf16[1,1024]{1,0:T(2,128)(2,1)S(1)} %get-tuple-element.161), channel_id=1, source_target_pairs={{0,8},{8,16},{16,24},{1,9},{9,17},{17,25},{2,10},{10,18},{18,26},{... | collective-permute-start | bytes 6152 | tf_op jit(solution)/shard_map/ppermute | solution.py:36
  17.0 3.7 %convolution.2.refs_6_.refs_7_.refs_8_ = bf16[4,512,256]{2,1,0:T(8,128)(2,1)} custom-call(bf16[512,1024]{1,0:T(8,128)(2,1)} %x_ref.1, bf16[1,1024]{1,0:T(2,128)(2,1)} %copy-done.29, bf16[1,1024]{1,0:T(2,128)(2,1)} %copy-done.28, f32[3,1024]{1,0:T(4,128)} %taps_ref.3), custom_call_target="tpu_custom_call" | custom-call | flops 5242880 | bytes 2097152 | tf_op jit(solution)/shard_map/convolution/pallas_call | solution.py:68
  23.3 13.8 %collective-permute-done.7.refs_11_ = bf16[1,512,256]{2,1,0:T(8,128)(2,1)S(1)} collective-permute-done((bf16[1,512,256]{2,1,0:T(8,128)(2,1)S(1)}, bf16[1,512,256]{2,1,0:T(8,128)(2,1)S(1)}, u32[]{:S(2)}, u32[]{:S(2)}) %collective-permute-start.7) | collective-permute-done | bytes 262176 | tf_op jit(solution)/shard_map/ppermute | solution.py:20
  37.4 2.3 collective-permute-start.10
  39.7 18.4 %layer.4 = (bf16[2,6,4,64,256]{4,3,2,1,0:T(8,128)(2,1)}, bf16[2,6,4,64,256]{4,3,2,1,0:T(8,128)(2,1)}, bf16[2,6,4,64,256]{4,3,2,1,0:T(8,128)(2,1)}, bf16[2,6,4,64...) custom-call(s32[5]{0:T(128)} %level_bits.7, ...), custom_call_target="tpu_custom_call" | custom-call | flops 9663676416 | bytes 18874368 | tf_op jit(solution)/shard_map/layer/pallas_call | solution.py:215
  59.5 3.0 collective-permute-done.9
  64.8 2.0 collective-permute-start.13
  66.8 18.5 %layer.5 = (bf16[2,6,4,64,256]{4,3,2,1,0:T(8,128)(2,1)}, bf16[2,6,4,64,256]{4,3,2,1,0:T(8,128)(2,1)}, bf16[2,6,4,64,256]{4,3,2,1,0:T(8,128)(2,1)}, bf16[2,6,4,64...) custom-call(s32[5]{0:T(128)} %level_bits.7, ...), custom_call_target="tpu_custom_call" | custom-call | flops 9663676416 | bytes 18874368 | tf_op jit(solution)/shard_map/layer/pallas_call | solution.py:215
  87.2 9.5 %collective-permute-done.12 = bf16[2,1,512,256]{3,2,1,0:T(8,128)(2,1)S(1)} collective-permute-done((bf16[2,1,512,256]{3,2,1,0:T(8,128)(2,1)S(1)}, bf16[2,1,512,256]{3,2,1,0:T(8,128)(2,1)S(1)}, u32[]{:S(2)}, u32[]{:S(2)}) %collective-permute-start.12) | collective-permute-done | bytes 524320 | tf_op jit(solution)/shard_map/ppermute | solution.py:20
  99.0 2.3 collective-permute-start.16
  101.3 18.4 %layer.6 = (bf16[2,6,4,64,256]{4,3,2,1,0:T(8,128)(2,1)}, bf16[2,6,4,64,256]{4,3,2,1,0:T(8,128)(2,1)}, bf16[2,6,4,64,256]{4,3,2,1,0:T(8,128)(2,1)}, bf16[2,6,4,64...) custom-call(s32[5]{0:T(128)} %level_bits.7, ...), custom_call_target="tpu_custom_call" | custom-call | flops 9663676416 | bytes 18874368 | tf_op jit(solution)/shard_map/layer/pallas_call | solution.py:215
  119.9 2.6 collective-permute-start.22
  122.5 2.6 collective-permute-done.15
  126.7 2.5 collective-permute-start.43
  129.2 13.1 %collective-permute-done.16 = bf16[2,1,512,256]{3,2,1,0:T(8,128)(2,1)S(1)} collective-permute-done((bf16[2,1,512,256]{3,2,1,0:T(8,128)(2,1)S(1)}, bf16[2,1,512,256]{3,2,1,0:T(8,128)(2,1)S(1)}, u32[]{:S(2)}, u32[]{:S(2)}) %collective-permute-start.16) | collective-permute-done | bytes 524320 | tf_op jit(solution)/shard_map/ppermute | solution.py:20
  144.6 1.9 collective-permute-done.21.refs_8_
  147.3 2.4 collective-permute-start.39
  149.7 14.4 %collective-permute-done.22.refs_9_ = bf16[2,1,512,256]{3,2,1,0:T(8,128)(2,1)S(1)} collective-permute-done((bf16[2,1,512,256]{3,2,1,0:T(8,128)(2,1)S(1)}, bf16[2,1,512,256]{3,2,1,0:T(8,128)(2,1)S(1)}, u32[]{:S(2)}, u32[]{:S(2)}) %collective-permute-start.22) | collective-permute-done | bytes 524320 | tf_op jit(solution)/shard_map/ppermute | solution.py:20
  164.2 2.7 collective-permute-start.25
  166.8 18.5 %layer.7 = (bf16[2,6,4,64,256]{4,3,2,1,0:T(8,128)(2,1)}, bf16[2,6,4,64,256]{4,3,2,1,0:T(8,128)(2,1)}, bf16[2,6,4,64,256]{4,3,2,1,0:T(8,128)(2,1)}, bf16[2,6,4,64...) custom-call(s32[5]{0:T(128)} %level_bits.7, ...), custom_call_target="tpu_custom_call" | custom-call | flops 9663676416 | bytes 18874368 | tf_op jit(solution)/shard_map/layer/pallas_call | solution.py:215
  185.3 3.3 collective-permute-done.24.refs_11_
  193.6 1.9 collective-permute-start.37
  195.5 7.6 %collective-permute-done.27.refs_14_ = bf16[2,1,512,256]{3,2,1,0:T(8,128)(2,1)S(1)} collective-permute-done((bf16[2,1,512,256]{3,2,1,0:T(8,128)(2,1)}, bf16[2,1,512,256]{3,2,1,0:T(8,128)(2,1)S(1)}, u32[]{:S(2)}, u32[]{:S(2)}) %collective-permute-start.27) | collective-permute-done | bytes 524320 | tf_op jit(solution)/shard_map/ppermute | solution.py:20
  204.0 23.4 %collective-permute-done.28.refs_15_ = bf16[2,1,512,256]{3,2,1,0:T(8,128)(2,1)S(1)} collective-permute-done((bf16[2,1,512,256]{3,2,1,0:T(8,128)(2,1)}, bf16[2,1,512,256]{3,2,1,0:T(8,128)(2,1)S(1)}, u32[]{:S(2)}, u32[]{:S(2)}) %collective-permute-start.28) | collective-permute-done | bytes 524320 | tf_op jit(solution)/shard_map/ppermute | solution.py:20
  227.4 2.4 collective-permute-start.31
  229.9 7.1 %combine.1 = (bf16[512,1024]{1,0:T(8,128)(2,1)}, bf16[512,1024]{1,0:T(8,128)(2,1)}) custom-call(bf16[2,3,1,512,256]{4,3,2,1,0:T(8,128)(2,1)} %get-tuple-element.77.refs_0_, bf16[2,3,1,512,256]{4,3,2,1,0:T(8,128)(2,1)} %get-tuple-element.81.refs_1_, bf16[2,3,1,512,256]{4,3,2,1,0:T(8,128)(2,1)} %get-tuple-element.85.refs_2_, ...), custom_call_target="tpu_custom_call" | custom-call | flops 6291456 | bytes 14680064 | tf_op jit(solution)/shard_map/combine/pallas_call | solution.py:336
  239.1 26.6 %collective-permute-done.30.behind_ref = bf16[1,1024]{1,0:T(2,128)(2,1)S(1)} collective-permute-done((bf16[1,1024]{1,0:T(2,128)(2,1)S(1)}, bf16[1,1024]{1,0:T(2,128)(2,1)S(1)}, u32[]{:S(2)}, u32[]{:S(2)}) %collective-permute-start.30) | collective-permute-done | bytes 2080 | tf_op jit(solution)/shard_map/ppermute | solution.py:37
  265.7 2.5 collective-permute-start.29
  268.2 4.9 %pair_sum.14 = (bf16[1,6,4,64,256]{4,3,2,1,0:T(8,128)(2,1)}, bf16[1,6,4,64,256]{4,3,2,1,0:T(8,128)(2,1)}) custom-call(bf16[2,6,4,64,256]{4,3,2,1,0:T(8,128)(2,1)} %get-tuple-element.132.kept_ref, bf16[2,6,4,64,256]{4,3,2,1,0:T(8,128)(2,1)} %copy-done.1), custom_call_target="tpu_custom_call" | custom-call | flops 786432 | bytes 4718592 | tf_op jit(solution)/shard_map/pair_sum/pallas_call | solution.py:273
  273.1 4.9 %pair_sum.15 = (bf16[1,6,4,64,256]{4,3,2,1,0:T(8,128)(2,1)}, bf16[1,6,4,64,256]{4,3,2,1,0:T(8,128)(2,1)}) custom-call(bf16[2,6,4,64,256]{4,3,2,1,0:T(8,128)(2,1)} %get-tuple-element.137.kept_ref, bf16[2,6,4,64,256]{4,3,2,1,0:T(8,128)(2,1)} %copy-done.3), custom_call_target="tpu_custom_call" | custom-call | flops 786432 | bytes 4718592 | tf_op jit(solution)/shard_map/pair_sum/pallas_call | solution.py:273
  278.4 4.8 %pair_sum.12 = (bf16[1,6,4,64,256]{4,3,2,1,0:T(8,128)(2,1)}, bf16[1,6,4,64,256]{4,3,2,1,0:T(8,128)(2,1)}) custom-call(bf16[2,6,4,64,256]{4,3,2,1,0:T(8,128)(2,1)} %get-tuple-element.122.kept_ref, bf16[2,6,4,64,256]{4,3,2,1,0:T(8,128)(2,1)} %copy-done.2), custom_call_target="tpu_custom_call" | custom-call | flops 786432 | bytes 4718592 | tf_op jit(solution)/shard_map/pair_sum/pallas_call | solution.py:273
  284.8 2.0 collective-permute-start.40
  286.8 4.9 %pair_sum.13 = (bf16[1,6,4,64,256]{4,3,2,1,0:T(8,128)(2,1)}, bf16[1,6,4,64,256]{4,3,2,1,0:T(8,128)(2,1)}) custom-call(bf16[2,6,4,64,256]{4,3,2,1,0:T(8,128)(2,1)} %get-tuple-element.127.kept_ref, bf16[2,6,4,64,256]{4,3,2,1,0:T(8,128)(2,1)} %copy-done.5), custom_call_target="tpu_custom_call" | custom-call | flops 786432 | bytes 4718592 | tf_op jit(solution)/shard_map/pair_sum/pallas_call | solution.py:273
  291.6 4.9 %pair_sum.10 = (bf16[1,6,4,64,256]{4,3,2,1,0:T(8,128)(2,1)}, bf16[1,6,4,64,256]{4,3,2,1,0:T(8,128)(2,1)}) custom-call(bf16[2,6,4,64,256]{4,3,2,1,0:T(8,128)(2,1)} %get-tuple-element.112.kept_ref, bf16[2,6,4,64,256]{4,3,2,1,0:T(8,128)(2,1)} %collective-permute-done.35.got_ref), custom_call_target="tpu_custom_call" | custom-call | flops 786432 | bytes 4718592 | tf_op jit(solution)/shard_map/pair_sum/pallas_call | solution.py:273
  296.5 4.9 %pair_sum.11 = (bf16[1,6,4,64,256]{4,3,2,1,0:T(8,128)(2,1)}, bf16[1,6,4,64,256]{4,3,2,1,0:T(8,128)(2,1)}) custom-call(bf16[2,6,4,64,256]{4,3,2,1,0:T(8,128)(2,1)} %get-tuple-element.117.kept_ref, bf16[2,6,4,64,256]{4,3,2,1,0:T(8,128)(2,1)} %collective-permute-done.37.got_ref), custom_call_target="tpu_custom_call" | custom-call | flops 786432 | bytes 4718592 | tf_op jit(solution)/shard_map/pair_sum/pallas_call | solution.py:273
  301.7 4.9 %pair_sum.8 = (bf16[1,6,4,64,256]{4,3,2,1,0:T(8,128)(2,1)}, bf16[1,6,4,64,256]{4,3,2,1,0:T(8,128)(2,1)}) custom-call(bf16[2,6,4,64,256]{4,3,2,1,0:T(8,128)(2,1)} %get-tuple-element.104.kept_ref, bf16[2,6,4,64,256]{4,3,2,1,0:T(8,128)(2,1)} %collective-permute-done.31.got_ref), custom_call_target="tpu_custom_call" | custom-call | flops 786432 | bytes 4718592 | tf_op jit(solution)/shard_map/pair_sum/pallas_call | solution.py:273
  306.7 6.2 %collective-permute-done.44.a_got = bf16[1,6,4,64,256]{4,3,2,1,0:T(8,128)(2,1)S(1)} collective-permute-done((bf16[1,6,4,64,256]{4,3,2,1,0:T(8,128)(2,1)S(1)}, bf16[1,6,4,64,256]{4,3,2,1,0:T(8,128)(2,1)S(1)}, u32[]{:S(2)}, u32[]{:S(2)}) %collective-permute-start.44) | collective-permute-done | bytes 786464 | tf_op jit(solution)/shard_map/ppermute | solution.py:20
  315.6 5.0 %pair_sum.9 = (bf16[1,6,4,64,256]{4,3,2,1,0:T(8,128)(2,1)}, bf16[1,6,4,64,256]{4,3,2,1,0:T(8,128)(2,1)}) custom-call(bf16[2,6,4,64,256]{4,3,2,1,0:T(8,128)(2,1)} %get-tuple-element.108.kept_ref, bf16[2,6,4,64,256]{4,3,2,1,0:T(8,128)(2,1)} %copy-done.4), custom_call_target="tpu_custom_call" | custom-call | flops 786432 | bytes 4718592 | tf_op jit(solution)/shard_map/pair_sum/pallas_call | solution.py:273
  320.6 1.8 collective-permute-start.32
  322.5 7.3 %collective-permute-done.40.a_got = bf16[1,6,4,64,256]{4,3,2,1,0:T(8,128)(2,1)S(1)} collective-permute-done((bf16[1,6,4,64,256]{4,3,2,1,0:T(8,128)(2,1)}, bf16[1,6,4,64,256]{4,3,2,1,0:T(8,128)(2,1)S(1)}, u32[]{:S(2)}, u32[]{:S(2)}) %collective-permute-start.40) | collective-permute-done | bytes 786464 | tf_op jit(solution)/shard_map/ppermute | solution.py:20
  329.7 2.5 collective-permute-start.34
  332.2 3.7 %convolution.3 = bf16[512,1024]{1,0:T(8,128)(2,1)} custom-call(bf16[512,1024]{1,0:T(8,128)(2,1)} %get-tuple-element.102.x_ref, bf16[1,1024]{1,0:T(2,128)(2,1)} %copy-done.27, bf16[1,1024]{1,0:T(2,128)(2,1)} %copy-done.26, f32[3,1024]{1,0:T(4,128)} %taps_ref.3), custom_call_target="tpu_custom_call" | custom-call | flops 5242880 | bytes 2097152 | tf_op jit(solution)/shard_map/convolution/pallas_call | solution.py:68
  335.9 4.3 %finish.4 = (f32[6,16,64,256]{3,2,1,0:T(8,128)}, f32[6,16,64,256]{3,2,1,0:T(8,128)}) custom-call(bf16[1,6,4,64,256]{4,3,2,1,0:T(8,128)(2,1)} %get-tuple-element.135.a_kept, bf16[1,6,4,64,256]{4,3,2,1,0:T(8,128)(2,1)} %copy-done.6, bf16[1,6,4,64,256]{4,3,2,1,0:T(8,128)(2,1)} %get-tuple-element.140.b_kept, bf16[1,6,4,64,256]{4,3,2,1,0:T(8,128)(2,1)} %copy-done.7), custom_call_target="tpu_custom_call" | custom-call | flops 786432 | bytes 6291456 | tf_op jit(solution)/shard_map/finish/pallas_call | solution.py:297
  341.1 4.3 %finish.5 = (f32[6,16,64,256]{3,2,1,0:T(8,128)}, f32[6,16,64,256]{3,2,1,0:T(8,128)}) custom-call(bf16[1,6,4,64,256]{4,3,2,1,0:T(8,128)(2,1)} %get-tuple-element.125.a_kept, bf16[1,6,4,64,256]{4,3,2,1,0:T(8,128)(2,1)} %copy-done.8, bf16[1,6,4,64,256]{4,3,2,1,0:T(8,128)(2,1)} %get-tuple-element.130.b_kept, ...), custom_call_target="tpu_custom_call", output_to_operand_aliasing={{0}: (4, {}), {1}: (5, {})} | custom-call | flops 786432 | bytes 6291456 | tf_op jit(solution)/shard_map/finish/pallas_call | solution.py:297
  347.7 4.3 %finish.6 = (f32[6,16,64,256]{3,2,1,0:T(8,128)}, f32[6,16,64,256]{3,2,1,0:T(8,128)}) custom-call(bf16[1,6,4,64,256]{4,3,2,1,0:T(8,128)(2,1)} %get-tuple-element.115.a_kept, bf16[1,6,4,64,256]{4,3,2,1,0:T(8,128)(2,1)} %copy-done.9, bf16[1,6,4,64,256]{4,3,2,1,0:T(8,128)(2,1)} %get-tuple-element.120.b_kept, ...), custom_call_target="tpu_custom_call", output_to_operand_aliasing={{0}: (4, {}), {1}: (5, {})} | custom-call | flops 786432 | bytes 6291456 | tf_op jit(solution)/shard_map/finish/pallas_call | solution.py:297
  352.0 9.2 %collective-permute-done.32.a_got = bf16[1,6,4,64,256]{4,3,2,1,0:T(8,128)(2,1)S(1)} collective-permute-done((bf16[1,6,4,64,256]{4,3,2,1,0:T(8,128)(2,1)S(1)}, bf16[1,6,4,64,256]{4,3,2,1,0:T(8,128)(2,1)S(1)}, u32[]{:S(2)}, u32[]{:S(2)}) %collective-permute-start.32) | collective-permute-done | bytes 786464 | tf_op jit(solution)/shard_map/ppermute | solution.py:20
  362.4 4.3 %finish.7 = (f32[6,16,64,256]{3,2,1,0:T(8,128)}, f32[6,16,64,256]{3,2,1,0:T(8,128)}) custom-call(bf16[1,6,4,64,256]{4,3,2,1,0:T(8,128)(2,1)} %get-tuple-element.106.a_kept, bf16[1,6,4,64,256]{4,3,2,1,0:T(8,128)(2,1)} %copy-done.10, bf16[1,6,4,64,256]{4,3,2,1,0:T(8,128)(2,1)} %get-tuple-element.110.b_kept, ...), custom_call_target="tpu_custom_call", output_to_operand_aliasing={{0}: (4, {}), {1}: (5, {})} | custom-call | flops 786432 | bytes 6291456 | tf_op jit(solution)/shard_map/finish/pallas_call | solution.py:297
  (174 shorter events, 40.6 us)
Async XLA Ops:
  2.8 19.8 %collective-permute-start.2 = (bf16[1,512,256]{2,1,0:T(8,128)(2,1)S(1)}, bf16[1,512,256]{2,1,0:T(8,128)(2,1)S(1)}, u32[]{:S(2)}, u32[]{:S(2)}) collective-permute-start(bf16[1,512,256]{2,1,0:T(8,128)(2,1)S(1)} %get-tuple-element.155), channel_id=1, source_target_pairs={{0,4},{1,5},{2,6},{3,7},{4,0},{5,1},{6,2},{7,3},{8,12},{9,13},{10,... | collective-permute-start | bytes 786440 | tf_op jit(solution)/shard_map/ppermute | solution.py:20
  7.6 8.2 %collective-permute-start.4 = (bf16[1,1024]{1,0:T(2,128)(2,1)S(1)}, bf16[1,1024]{1,0:T(2,128)(2,1)S(1)}, u32[]{:S(2)}, u32[]{:S(2)}) collective-permute-start(bf16[1,1024]{1,0:T(2,128)(2,1)S(1)} %get-tuple-element.160), channel_id=1, source_target_pairs={{8,0},{16,8},{24,16},{9,1},{17,9},{25,17},{10,2},{18,10},{26,18},{... | collective-permute-start | bytes 6152 | tf_op jit(solution)/shard_map/ppermute | solution.py:37
  8.9 6.9 %collective-permute-start.3 = (bf16[1,1024]{1,0:T(2,128)(2,1)S(1)}, bf16[1,1024]{1,0:T(2,128)(2,1)S(1)}, u32[]{:S(2)}, u32[]{:S(2)}) collective-permute-start(bf16[1,1024]{1,0:T(2,128)(2,1)S(1)} %get-tuple-element.161), channel_id=1, source_target_pairs={{0,8},{8,16},{16,24},{1,9},{9,17},{17,25},{2,10},{10,18},{18,26},{... | collective-permute-start | bytes 6152 | tf_op jit(solution)/shard_map/ppermute | solution.py:36
  13.5 23.7 %collective-permute-start.1 = (bf16[1,512,256]{2,1,0:T(8,128)(2,1)S(1)}, bf16[1,512,256]{2,1,0:T(8,128)(2,1)S(1)}, u32[]{:S(2)}, u32[]{:S(2)}) collective-permute-start(bf16[1,512,256]{2,1,0:T(8,128)(2,1)S(1)} %get-tuple-element.155), channel_id=1, source_target_pairs={{0,2},{1,3},{2,0},{3,1},{4,6},{5,7},{6,4},{7,5},{8,10},{9,11},{10,... | collective-permute-start | bytes 786440 | tf_op jit(solution)/shard_map/ppermute | solution.py:20
  15.1 22.1 %collective-permute-start = (bf16[1,512,256]{2,1,0:T(8,128)(2,1)S(1)}, bf16[1,512,256]{2,1,0:T(8,128)(2,1)S(1)}, u32[]{:S(2)}, u32[]{:S(2)}) collective-permute-start(bf16[1,512,256]{2,1,0:T(8,128)(2,1)S(1)} %get-tuple-element.155), channel_id=1, source_target_pairs={{0,1},{1,0},{2,3},{3,2},{4,5},{5,4},{6,7},{7,6},{8,9},{9,8},{10,11... | collective-permute-start | bytes 786440 | tf_op jit(solution)/shard_map/ppermute | solution.py:20
  22.0 15.2 %collective-permute-start.7 = (bf16[1,512,256]{2,1,0:T(8,128)(2,1)S(1)}, bf16[1,512,256]{2,1,0:T(8,128)(2,1)S(1)}, u32[]{:S(2)}, u32[]{:S(2)}) collective-permute-start(bf16[1,512,256]{2,1,0:T(8,128)(2,1)S(1)} %get-tuple-element.159), channel_id=1, source_target_pairs={{0,4},{1,5},{2,6},{3,7},{4,0},{5,1},{6,2},{7,3},{8,12},{9,13},{10,... | collective-permute-start | bytes 786440 | tf_op jit(solution)/shard_map/ppermute | solution.py:20
  22.4 14.8 %collective-permute-start.6 = (bf16[1,512,256]{2,1,0:T(8,128)(2,1)S(1)}, bf16[1,512,256]{2,1,0:T(8,128)(2,1)S(1)}, u32[]{:S(2)}, u32[]{:S(2)}) collective-permute-start(bf16[1,512,256]{2,1,0:T(8,128)(2,1)S(1)} %get-tuple-element.159), channel_id=1, source_target_pairs={{0,2},{1,3},{2,0},{3,1},{4,6},{5,7},{6,4},{7,5},{8,10},{9,11},{10,... | collective-permute-start | bytes 786440 | tf_op jit(solution)/shard_map/ppermute | solution.py:20
  22.6 14.6 %collective-permute-start.5 = (bf16[1,512,256]{2,1,0:T(8,128)(2,1)S(1)}, bf16[1,512,256]{2,1,0:T(8,128)(2,1)S(1)}, u32[]{:S(2)}, u32[]{:S(2)}) collective-permute-start(bf16[1,512,256]{2,1,0:T(8,128)(2,1)S(1)} %get-tuple-element.159), channel_id=1, source_target_pairs={{0,1},{1,0},{2,3},{3,2},{4,5},{5,4},{6,7},{7,6},{8,9},{9,8},{10,11... | collective-permute-start | bytes 786440 | tf_op jit(solution)/shard_map/ppermute | solution.py:20
  37.2 21.3 %collective-permute-start.8 = (bf16[2,1,512,256]{3,2,1,0:T(8,128)(2,1)S(1)}, bf16[2,1,512,256]{3,2,1,0:T(8,128)(2,1)S(1)}, u32[]{:S(2)}, u32[]{:S(2)}) collective-permute-start(bf16[2,1,512,256]{3,2,1,0:T(8,128)(2,1)S(1)} %pad_maximum_fusion), channel_id=1, source_target_pairs={{0,1},{1,0},{2,3},{3,2},{4,5},{5,4},{6,7},{7,6},{8,9},{9,8},{10,11... | collective-permute-start | bytes 1572872 | tf_op jit(solution)/shard_map/ppermute | solution.py:20
  37.4 25.1 %collective-permute-start.9 = (bf16[2,1,512,256]{3,2,1,0:T(8,128)(2,1)S(1)}, bf16[2,1,512,256]{3,2,1,0:T(8,128)(2,1)S(1)}, u32[]{:S(2)}, u32[]{:S(2)}) collective-permute-start(bf16[2,1,512,256]{3,2,1,0:T(8,128)(2,1)S(1)} %pad_maximum_fusion), channel_id=1, source_target_pairs={{0,2},{1,3},{2,0},{3,1},{4,6},{5,7},{6,4},{7,5},{8,10},{9,11},{10,... | collective-permute-start | bytes 1572872 | tf_op jit(solution)/shard_map/ppermute | solution.py:20
  37.4 26.5 %collective-permute-start.10 = (bf16[2,1,512,256]{3,2,1,0:T(8,128)(2,1)S(1)}, bf16[2,1,512,256]{3,2,1,0:T(8,128)(2,1)S(1)}, u32[]{:S(2)}, u32[]{:S(2)}) collective-permute-start(bf16[2,1,512,256]{3,2,1,0:T(8,128)(2,1)S(1)} %pad_maximum_fusion), channel_id=1, source_target_pairs={{0,4},{1,5},{2,6},{3,7},{4,0},{5,1},{6,2},{7,3},{8,12},{9,13},{10,... | collective-permute-start | bytes 1572872 | tf_op jit(solution)/shard_map/ppermute | solution.py:20
  58.1 40.8 %collective-permute-start.17 = (bf16[2,1,512,256]{3,2,1,0:T(8,128)(2,1)}, bf16[2,1,512,256]{3,2,1,0:T(8,128)(2,1)S(1)}, u32[]{:S(2)}, u32[]{:S(2)}) collective-permute-start(bf16[2,1,512,256]{3,2,1,0:T(8,128)(2,1)} %get-tuple-element.90), channel_id=1, source_target_pairs={{0,1},{1,0},{2,3},{3,2},{4,5},{5,4},{6,7},{7,6},{8,9},{9,8},{10,11... | collective-permute-start | bytes 1572872 | tf_op jit(solution)/shard_map/ppermute | solution.py:20
  58.2 40.9 %collective-permute-start.18 = (bf16[2,1,512,256]{3,2,1,0:T(8,128)(2,1)}, bf16[2,1,512,256]{3,2,1,0:T(8,128)(2,1)S(1)}, u32[]{:S(2)}, u32[]{:S(2)}) collective-permute-start(bf16[2,1,512,256]{3,2,1,0:T(8,128)(2,1)} %get-tuple-element.91), channel_id=1, source_target_pairs={{0,2},{1,3},{2,0},{3,1},{4,6},{5,7},{6,4},{7,5},{8,10},{9,11},{10,... | collective-permute-start | bytes 1572872 | tf_op jit(solution)/shard_map/ppermute | solution.py:20
  59.4 25.9 %collective-permute-start.11 = (bf16[2,1,512,256]{3,2,1,0:T(8,128)(2,1)S(1)}, bf16[2,1,512,256]{3,2,1,0:T(8,128)(2,1)S(1)}, u32[]{:S(2)}, u32[]{:S(2)}) collective-permute-start(bf16[2,1,512,256]{3,2,1,0:T(8,128)(2,1)S(1)} %pad_maximum_fusion.1), channel_id=1, source_target_pairs={{0,1},{1,0},{2,3},{3,2},{4,5},{5,4},{6,7},{7,6},{8,9},{9,8},{10,11... | collective-permute-start | bytes 1572872 | tf_op jit(solution)/shard_map/ppermute | solution.py:20
  63.3 33.4 %collective-permute-start.12 = (bf16[2,1,512,256]{3,2,1,0:T(8,128)(2,1)S(1)}, bf16[2,1,512,256]{3,2,1,0:T(8,128)(2,1)S(1)}, u32[]{:S(2)}, u32[]{:S(2)}) collective-permute-start(bf16[2,1,512,256]{3,2,1,0:T(8,128)(2,1)S(1)} %pad_maximum_fusion.1), channel_id=1, source_target_pairs={{0,2},{1,3},{2,0},{3,1},{4,6},{5,7},{6,4},{7,5},{8,10},{9,11},{10,... | collective-permute-start | bytes 1572872 | tf_op jit(solution)/shard_map/ppermute | solution.py:20
  64.8 32.7 %collective-permute-start.13 = (bf16[2,1,512,256]{3,2,1,0:T(8,128)(2,1)S(1)}, bf16[2,1,512,256]{3,2,1,0:T(8,128)(2,1)S(1)}, u32[]{:S(2)}, u32[]{:S(2)}) collective-permute-start(bf16[2,1,512,256]{3,2,1,0:T(8,128)(2,1)S(1)} %pad_maximum_fusion.1), channel_id=1, source_target_pairs={{0,4},{1,5},{2,6},{3,7},{4,0},{5,1},{6,2},{7,3},{8,12},{9,13},{10,... | collective-permute-start | bytes 1572872 | tf_op jit(solution)/shard_map/ppermute | solution.py:20
  85.3 34.4 %collective-permute-start.19 = (bf16[2,1,512,256]{3,2,1,0:T(8,128)(2,1)S(1)}, bf16[2,1,512,256]{3,2,1,0:T(8,128)(2,1)S(1)}, u32[]{:S(2)}, u32[]{:S(2)}) collective-permute-start(bf16[2,1,512,256]{3,2,1,0:T(8,128)(2,1)S(1)} %copy-done.34), channel_id=1, source_target_pairs={{0,4},{1,5},{2,6},{3,7},{4,0},{5,1},{6,2},{7,3},{8,12},{9,13},{10,... | collective-permute-start | bytes 1572872 | tf_op jit(solution)/shard_map/ppermute | solution.py:20
  96.7 30.0 %collective-permute-start.20 = (bf16[2,1,512,256]{3,2,1,0:T(8,128)(2,1)}, bf16[2,1,512,256]{3,2,1,0:T(8,128)(2,1)S(1)}, u32[]{:S(2)}, u32[]{:S(2)}) collective-permute-start(bf16[2,1,512,256]{3,2,1,0:T(8,128)(2,1)} %get-tuple-element.93), channel_id=1, source_target_pairs={{0,1},{1,0},{2,3},{3,2},{4,5},{5,4},{6,7},{7,6},{8,9},{9,8},{10,11... | collective-permute-start | bytes 1572872 | tf_op jit(solution)/shard_map/ppermute | solution.py:20
  97.5 22.4 %collective-permute-start.14 = (bf16[2,1,512,256]{3,2,1,0:T(8,128)(2,1)S(1)}, bf16[2,1,512,256]{3,2,1,0:T(8,128)(2,1)S(1)}, u32[]{:S(2)}, u32[]{:S(2)}) collective-permute-start(bf16[2,1,512,256]{3,2,1,0:T(8,128)(2,1)S(1)} %pad_maximum_fusion.2), channel_id=1, source_target_pairs={{0,1},{1,0},{2,3},{3,2},{4,5},{5,4},{6,7},{7,6},{8,9},{9,8},{10,11... | collective-permute-start | bytes 1572872 | tf_op jit(solution)/shard_map/ppermute | solution.py:20
  98.9 26.1 %collective-permute-start.15 = (bf16[2,1,512,256]{3,2,1,0:T(8,128)(2,1)S(1)}, bf16[2,1,512,256]{3,2,1,0:T(8,128)(2,1)S(1)}, u32[]{:S(2)}, u32[]{:S(2)}) collective-permute-start(bf16[2,1,512,256]{3,2,1,0:T(8,128)(2,1)S(1)} %pad_maximum_fusion.2), channel_id=1, source_target_pairs={{0,2},{1,3},{2,0},{3,1},{4,6},{5,7},{6,4},{7,5},{8,10},{9,11},{10,... | collective-permute-start | bytes 1572872 | tf_op jit(solution)/shard_map/ppermute | solution.py:20
  99.0 43.2 %collective-permute-start.16 = (bf16[2,1,512,256]{3,2,1,0:T(8,128)(2,1)S(1)}, bf16[2,1,512,256]{3,2,1,0:T(8,128)(2,1)S(1)}, u32[]{:S(2)}, u32[]{:S(2)}) collective-permute-start(bf16[2,1,512,256]{3,2,1,0:T(8,128)(2,1)S(1)} %pad_maximum_fusion.2), channel_id=1, source_target_pairs={{0,4},{1,5},{2,6},{3,7},{4,0},{5,1},{6,2},{7,3},{8,12},{9,13},{10,... | collective-permute-start | bytes 1572872 | tf_op jit(solution)/shard_map/ppermute | solution.py:20
  119.7 26.8 %collective-permute-start.21 = (bf16[2,1,512,256]{3,2,1,0:T(8,128)(2,1)S(1)}, bf16[2,1,512,256]{3,2,1,0:T(8,128)(2,1)S(1)}, u32[]{:S(2)}, u32[]{:S(2)}) collective-permute-start(bf16[2,1,512,256]{3,2,1,0:T(8,128)(2,1)S(1)} %copy-done.36), channel_id=1, source_target_pairs={{0,2},{1,3},{2,0},{3,1},{4,6},{5,7},{6,4},{7,5},{8,10},{9,11},{10,... | collective-permute-start | bytes 1572872 | tf_op jit(solution)/shard_map/ppermute | solution.py:20
  119.9 44.3 %collective-permute-start.22 = (bf16[2,1,512,256]{3,2,1,0:T(8,128)(2,1)S(1)}, bf16[2,1,512,256]{3,2,1,0:T(8,128)(2,1)S(1)}, u32[]{:S(2)}, u32[]{:S(2)}) collective-permute-start(bf16[2,1,512,256]{3,2,1,0:T(8,128)(2,1)S(1)} %copy-done.35), channel_id=1, source_target_pairs={{0,4},{1,5},{2,6},{3,7},{4,0},{5,1},{6,2},{7,3},{8,12},{9,13},{10,... | collective-permute-start | bytes 1572872 | tf_op jit(solution)/shard_map/ppermute | solution.py:20
  125.0 39.1 %collective-permute-start.23 = (bf16[2,1,512,256]{3,2,1,0:T(8,128)(2,1)}, bf16[2,1,512,256]{3,2,1,0:T(8,128)(2,1)S(1)}, u32[]{:S(2)}, u32[]{:S(2)}) collective-permute-start(bf16[2,1,512,256]{3,2,1,0:T(8,128)(2,1)} %get-tuple-element.96), channel_id=1, source_target_pairs={{0,1},{1,0},{2,3},{3,2},{4,5},{5,4},{6,7},{7,6},{8,9},{9,8},{10,11... | collective-permute-start | bytes 1572872 | tf_op jit(solution)/shard_map/ppermute | solution.py:20
  126.7 63.6 %collective-permute-start.43 = (bf16[2,6,4,64,256]{4,3,2,1,0:T(8,128)(2,1)}, bf16[2,6,4,64,256]{4,3,2,1,0:T(8,128)(2,1)S(1)}, u32[]{:S(2)}, u32[]{:S(2)}) collective-permute-start(bf16[2,6,4,64,256]{4,3,2,1,0:T(8,128)(2,1)} %get-tuple-element.133), channel_id=1, source_target_pairs={{0,8},{8,0},{16,24},{24,16},{1,9},{9,1},{17,25},{25,17},{2,10},{10... | collective-permute-start | bytes 4718600 | tf_op jit(solution)/shard_map/ppermute | solution.py:20
  142.2 50.4 %collective-permute-start.45 = (bf16[2,6,4,64,256]{4,3,2,1,0:T(8,128)(2,1)}, bf16[2,6,4,64,256]{4,3,2,1,0:T(8,128)(2,1)S(1)}, u32[]{:S(2)}, u32[]{:S(2)}) collective-permute-start(bf16[2,6,4,64,256]{4,3,2,1,0:T(8,128)(2,1)} %get-tuple-element.138), channel_id=1, source_target_pairs={{0,16},{8,24},{16,0},{24,8},{1,17},{9,25},{17,1},{25,9},{2,18},{10... | collective-permute-start | bytes 4718600 | tf_op jit(solution)/shard_map/ppermute | solution.py:20
  147.3 82.4 %collective-permute-start.39 = (bf16[2,6,4,64,256]{4,3,2,1,0:T(8,128)(2,1)}, bf16[2,6,4,64,256]{4,3,2,1,0:T(8,128)(2,1)S(1)}, u32[]{:S(2)}, u32[]{:S(2)}) collective-permute-start(bf16[2,6,4,64,256]{4,3,2,1,0:T(8,128)(2,1)} %get-tuple-element.123), channel_id=1, source_target_pairs={{0,8},{8,0},{16,24},{24,16},{1,9},{9,1},{17,25},{25,17},{2,10},{10... | collective-permute-start | bytes 4718600 | tf_op jit(solution)/shard_map/ppermute | solution.py:20
  164.1 24.5 %collective-permute-start.24 = (bf16[2,1,512,256]{3,2,1,0:T(8,128)(2,1)S(1)}, bf16[2,1,512,256]{3,2,1,0:T(8,128)(2,1)S(1)}, u32[]{:S(2)}, u32[]{:S(2)}) collective-permute-start(bf16[2,1,512,256]{3,2,1,0:T(8,128)(2,1)S(1)} %copy-done.38), channel_id=1, source_target_pairs={{0,2},{1,3},{2,0},{3,1},{4,6},{5,7},{6,4},{7,5},{8,10},{9,11},{10,... | collective-permute-start | bytes 1572872 | tf_op jit(solution)/shard_map/ppermute | solution.py:20
  164.2 26.1 %collective-permute-start.25 = (bf16[2,1,512,256]{3,2,1,0:T(8,128)(2,1)S(1)}, bf16[2,1,512,256]{3,2,1,0:T(8,128)(2,1)S(1)}, u32[]{:S(2)}, u32[]{:S(2)}) collective-permute-start(bf16[2,1,512,256]{3,2,1,0:T(8,128)(2,1)S(1)} %copy-done.37), channel_id=1, source_target_pairs={{0,4},{1,5},{2,6},{3,7},{4,0},{5,1},{6,2},{7,3},{8,12},{9,13},{10,... | collective-permute-start | bytes 1572872 | tf_op jit(solution)/shard_map/ppermute | solution.py:20
  188.6 5.0 %collective-permute-start.26 = (bf16[2,1,512,256]{3,2,1,0:T(8,128)(2,1)}, bf16[2,1,512,256]{3,2,1,0:T(8,128)(2,1)S(1)}, u32[]{:S(2)}, u32[]{:S(2)}) collective-permute-start(bf16[2,1,512,256]{3,2,1,0:T(8,128)(2,1)} %get-tuple-element.99), channel_id=1, source_target_pairs={{0,1},{1,0},{2,3},{3,2},{4,5},{5,4},{6,7},{7,6},{8,9},{9,8},{10,11... | collective-permute-start | bytes 1572872 | tf_op jit(solution)/shard_map/ppermute | solution.py:20
  190.3 12.9 %collective-permute-start.27 = (bf16[2,1,512,256]{3,2,1,0:T(8,128)(2,1)}, bf16[2,1,512,256]{3,2,1,0:T(8,128)(2,1)S(1)}, u32[]{:S(2)}, u32[]{:S(2)}) collective-permute-start(bf16[2,1,512,256]{3,2,1,0:T(8,128)(2,1)} %get-tuple-element.100), channel_id=1, source_target_pairs={{0,2},{1,3},{2,0},{3,1},{4,6},{5,7},{6,4},{7,5},{8,10},{9,11},{10,... | collective-permute-start | bytes 1572872 | tf_op jit(solution)/shard_map/ppermute | solution.py:20
  191.1 45.9 %copy-start.1 = (bf16[2,6,4,64,256]{4,3,2,1,0:T(8,128)(2,1)}, bf16[2,6,4,64,256]{4,3,2,1,0:T(8,128)(2,1)S(1)}, u32[]{:S(2)}) copy-start(bf16[2,6,4,64,256]{4,3,2,1,0:T(8,128)(2,1)S(1)} %collective-permute-done.43.got_ref) | copy-start | bytes 4718596
  191.1 46.7 %collective-permute-start.41 = (bf16[2,6,4,64,256]{4,3,2,1,0:T(8,128)(2,1)}, bf16[2,6,4,64,256]{4,3,2,1,0:T(8,128)(2,1)S(1)}, u32[]{:S(2)}, u32[]{:S(2)}) collective-permute-start(bf16[2,6,4,64,256]{4,3,2,1,0:T(8,128)(2,1)} %get-tuple-element.128), channel_id=1, source_target_pairs={{0,16},{8,24},{16,0},{24,8},{1,17},{9,25},{17,1},{25,9},{2,18},{10... | collective-permute-start | bytes 4718600 | tf_op jit(solution)/shard_map/ppermute | solution.py:20
  192.6 90.6 %collective-permute-start.35 = (bf16[2,6,4,64,256]{4,3,2,1,0:T(8,128)(2,1)}, bf16[2,6,4,64,256]{4,3,2,1,0:T(8,128)(2,1)}, u32[]{:S(2)}, u32[]{:S(2)}) collective-permute-start(bf16[2,6,4,64,256]{4,3,2,1,0:T(8,128)(2,1)} %get-tuple-element.113), channel_id=1, source_target_pairs={{0,8},{8,0},{16,24},{24,16},{1,9},{9,1},{17,25},{25,17},{2,10},{10... | collective-permute-start | bytes 4718600 | tf_op jit(solution)/shard_map/ppermute | solution.py:20
  193.6 91.2 %collective-permute-start.37 = (bf16[2,6,4,64,256]{4,3,2,1,0:T(8,128)(2,1)}, bf16[2,6,4,64,256]{4,3,2,1,0:T(8,128)(2,1)}, u32[]{:S(2)}, u32[]{:S(2)}) collective-permute-start(bf16[2,6,4,64,256]{4,3,2,1,0:T(8,128)(2,1)} %get-tuple-element.118), channel_id=1, source_target_pairs={{0,16},{8,24},{16,0},{24,8},{1,17},{9,25},{17,1},{25,9},{2,18},{10... | collective-permute-start | bytes 4718600 | tf_op jit(solution)/shard_map/ppermute | solution.py:20
  203.2 24.2 %collective-permute-start.28 = (bf16[2,1,512,256]{3,2,1,0:T(8,128)(2,1)}, bf16[2,1,512,256]{3,2,1,0:T(8,128)(2,1)S(1)}, u32[]{:S(2)}, u32[]{:S(2)}) collective-permute-start(bf16[2,1,512,256]{3,2,1,0:T(8,128)(2,1)} %get-tuple-element.101), channel_id=1, source_target_pairs={{0,4},{1,5},{2,6},{3,7},{4,0},{5,1},{6,2},{7,3},{8,12},{9,13},{10,... | collective-permute-start | bytes 1572872 | tf_op jit(solution)/shard_map/ppermute | solution.py:20
  227.4 74.0 %collective-permute-start.31 = (bf16[2,6,4,64,256]{4,3,2,1,0:T(8,128)(2,1)}, bf16[2,6,4,64,256]{4,3,2,1,0:T(8,128)(2,1)}, u32[]{:S(2)}, u32[]{:S(2)}) collective-permute-start(bf16[2,6,4,64,256]{4,3,2,1,0:T(8,128)(2,1)} %get-tuple-element.105), channel_id=1, source_target_pairs={{0,8},{8,0},{16,24},{24,16},{1,9},{9,1},{17,25},{25,17},{2,10},{10... | collective-permute-start | bytes 4718600 | tf_op jit(solution)/shard_map/ppermute | solution.py:20
  229.8 84.7 %collective-permute-start.33 = (bf16[2,6,4,64,256]{4,3,2,1,0:T(8,128)(2,1)}, bf16[2,6,4,64,256]{4,3,2,1,0:T(8,128)(2,1)S(1)}, u32[]{:S(2)}, u32[]{:S(2)}) collective-permute-start(bf16[2,6,4,64,256]{4,3,2,1,0:T(8,128)(2,1)} %get-tuple-element.109), channel_id=1, source_target_pairs={{0,16},{8,24},{16,0},{24,8},{1,17},{9,25},{17,1},{25,9},{2,18},{10... | collective-permute-start | bytes 4718600 | tf_op jit(solution)/shard_map/ppermute | solution.py:20
  237.8 27.9 %collective-permute-start.30 = (bf16[1,1024]{1,0:T(2,128)(2,1)S(1)}, bf16[1,1024]{1,0:T(2,128)(2,1)S(1)}, u32[]{:S(2)}, u32[]{:S(2)}) collective-permute-start(bf16[1,1024]{1,0:T(2,128)(2,1)S(1)} %get-tuple-element.150), channel_id=1, source_target_pairs={{8,0},{16,8},{24,16},{9,1},{17,9},{25,17},{10,2},{18,10},{26,18},{... | collective-permute-start | bytes 6152 | tf_op jit(solution)/shard_map/ppermute | solution.py:37
  265.7 12.3 %collective-permute-start.29 = (bf16[1,1024]{1,0:T(2,128)(2,1)S(1)}, bf16[1,1024]{1,0:T(2,128)(2,1)S(1)}, u32[]{:S(2)}, u32[]{:S(2)}) collective-permute-start(bf16[1,1024]{1,0:T(2,128)(2,1)S(1)} %get-tuple-element.151), channel_id=1, source_target_pairs={{0,8},{8,16},{16,24},{1,9},{9,17},{17,25},{2,10},{10,18},{18,26},{... | collective-permute-start | bytes 6152 | tf_op jit(solution)/shard_map/ppermute | solution.py:36
  278.1 34.8 %collective-permute-start.44 = (bf16[1,6,4,64,256]{4,3,2,1,0:T(8,128)(2,1)S(1)}, bf16[1,6,4,64,256]{4,3,2,1,0:T(8,128)(2,1)S(1)}, u32[]{:S(2)}, u32[]{:S(2)}) collective-permute-start(bf16[1,6,4,64,256]{4,3,2,1,0:T(8,128)(2,1)S(1)} %copy-done.33), channel_id=1, source_target_pairs={{0,16},{8,24},{16,0},{24,8},{1,17},{9,25},{17,1},{25,9},{2,18},{10... | collective-permute-start | bytes 2359304 | tf_op jit(solution)/shard_map/ppermute | solution.py:20
  283.2 37.4 %collective-permute-start.46 = (bf16[1,6,4,64,256]{4,3,2,1,0:T(8,128)(2,1)}, bf16[1,6,4,64,256]{4,3,2,1,0:T(8,128)(2,1)S(1)}, u32[]{:S(2)}, u32[]{:S(2)}) collective-permute-start(bf16[1,6,4,64,256]{4,3,2,1,0:T(8,128)(2,1)} %get-tuple-element.141), channel_id=1, source_target_pairs={{0,8},{8,0},{16,24},{24,16},{1,9},{9,1},{17,25},{25,17},{2,10},{10... | collective-permute-start | bytes 2359304 | tf_op jit(solution)/shard_map/ppermute | solution.py:20
  284.8 45.0 %collective-permute-start.40 = (bf16[1,6,4,64,256]{4,3,2,1,0:T(8,128)(2,1)}, bf16[1,6,4,64,256]{4,3,2,1,0:T(8,128)(2,1)S(1)}, u32[]{:S(2)}, u32[]{:S(2)}) collective-permute-start(bf16[1,6,4,64,256]{4,3,2,1,0:T(8,128)(2,1)} %get-tuple-element.126), channel_id=1, source_target_pairs={{0,16},{8,24},{16,0},{24,8},{1,17},{9,25},{17,1},{25,9},{2,18},{10... | collective-permute-start | bytes 2359304 | tf_op jit(solution)/shard_map/ppermute | solution.py:20
  301.4 38.9 %collective-permute-start.42 = (bf16[1,6,4,64,256]{4,3,2,1,0:T(8,128)(2,1)}, bf16[1,6,4,64,256]{4,3,2,1,0:T(8,128)(2,1)S(1)}, u32[]{:S(2)}, u32[]{:S(2)}) collective-permute-start(bf16[1,6,4,64,256]{4,3,2,1,0:T(8,128)(2,1)} %get-tuple-element.131), channel_id=1, source_target_pairs={{0,8},{8,0},{16,24},{24,16},{1,9},{9,1},{17,25},{25,17},{2,10},{10... | collective-permute-start | bytes 2359304 | tf_op jit(solution)/shard_map/ppermute | solution.py:20
  312.9 33.7 %collective-permute-start.36 = (bf16[1,6,4,64,256]{4,3,2,1,0:T(8,128)(2,1)S(1)}, bf16[1,6,4,64,256]{4,3,2,1,0:T(8,128)(2,1)S(1)}, u32[]{:S(2)}, u32[]{:S(2)}) collective-permute-start(bf16[1,6,4,64,256]{4,3,2,1,0:T(8,128)(2,1)S(1)} %copy-done.32), channel_id=1, source_target_pairs={{0,16},{8,24},{16,0},{24,8},{1,17},{9,25},{17,1},{25,9},{2,18},{10... | collective-permute-start | bytes 2359304 | tf_op jit(solution)/shard_map/ppermute | solution.py:20
  314.5 32.1 %collective-permute-start.38 = (bf16[1,6,4,64,256]{4,3,2,1,0:T(8,128)(2,1)}, bf16[1,6,4,64,256]{4,3,2,1,0:T(8,128)(2,1)S(1)}, u32[]{:S(2)}, u32[]{:S(2)}) collective-permute-start(bf16[1,6,4,64,256]{4,3,2,1,0:T(8,128)(2,1)} %get-tuple-element.121), channel_id=1, source_target_pairs={{0,8},{8,0},{16,24},{24,16},{1,9},{9,1},{17,25},{25,17},{2,10},{10... | collective-permute-start | bytes 2359304 | tf_op jit(solution)/shard_map/ppermute | solution.py:20
  320.6 40.6 %collective-permute-start.32 = (bf16[1,6,4,64,256]{4,3,2,1,0:T(8,128)(2,1)S(1)}, bf16[1,6,4,64,256]{4,3,2,1,0:T(8,128)(2,1)S(1)}, u32[]{:S(2)}, u32[]{:S(2)}) collective-permute-start(bf16[1,6,4,64,256]{4,3,2,1,0:T(8,128)(2,1)S(1)} %copy-done.31), channel_id=1, source_target_pairs={{0,16},{8,24},{16,0},{24,8},{1,17},{9,25},{17,1},{25,9},{2,18},{10... | collective-permute-start | bytes 2359304 | tf_op jit(solution)/shard_map/ppermute | solution.py:20
  329.7 31.5 %collective-permute-start.34 = (bf16[1,6,4,64,256]{4,3,2,1,0:T(8,128)(2,1)}, bf16[1,6,4,64,256]{4,3,2,1,0:T(8,128)(2,1)S(1)}, u32[]{:S(2)}, u32[]{:S(2)}) collective-permute-start(bf16[1,6,4,64,256]{4,3,2,1,0:T(8,128)(2,1)} %get-tuple-element.111), channel_id=1, source_target_pairs={{0,8},{8,0},{16,24},{24,16},{1,9},{9,1},{17,25},{25,17},{2,10},{10... | collective-permute-start | bytes 2359304 | tf_op jit(solution)/shard_map/ppermute | solution.py:20
  (44 other events, 575.2 us)

commit v2 on v1

v2 whole, which is shorter than its diff:
```python
import functools
import math

import jax
import jax.numpy as jnp
from jax import lax
from jax.experimental import pallas as pl
from jax.experimental.pallas import tpu as pltpu
from jax.sharding import PartitionSpec as P

coef = 0.7978845608028654
cubic = 0.044715
f32 = jnp.float32
bf16 = jnp.bfloat16
VMEM_LIMIT = 56 * 1024 * 1024
ANY = pl.BlockSpec(memory_space=pl.ANY)
LONG = 200_000_000_000


def swapped(array, axis, bit):
    return lax.ppermute(array, axis, [(i, i ^ 1 << bit) for i in range(lax.axis_size(axis))])


def after(value, *others):
    return lax.optimization_barrier((value,) + others)[0]


def cost(flops=1):
    return pl.CostEstimate(flops=flops, bytes_accessed=1, transcendentals=0)


def halo(array):
    peers = lax.axis_size("seq")
    up = [(i, i + 1) for i in range(peers - 1)]
    down = [(i + 1, i) for i in range(peers - 1)]
    rows = array.shape[0]
    before = lax.ppermute(lax.slice_in_dim(array, rows - 1, rows), "seq", up)
    behind = lax.ppermute(lax.slice_in_dim(array, 0, 1), "seq", down)
    return before, behind


def convolved_rows(x, before, behind, taps_ref, order):
    rows = x.shape[0]
    at = lax.broadcasted_iota(jnp.int32, x.shape, 0)
    earlier = jnp.where(at == 0, before.astype(f32), pltpu.roll(x, 1, 0))
    later = jnp.where(at == rows - 1, behind.astype(f32), pltpu.roll(x, rows - 1, 0))
    first, middle, last = order
    return (
        taps_ref[first : first + 1, :] * earlier
        + taps_ref[middle : middle + 1, :] * x
        + taps_ref[last : last + 1, :] * later
    ).astype(bf16)


def prepare_kernel(frames_ref, cot_ref, before_ref, behind_ref, taps_ref, grad_ref, *both_refs):
    grad = convolved_rows(cot_ref[...].astype(f32), before_ref[...], behind_ref[...], taps_ref, (2, 1, 0))
    grad_ref[...] = grad
    for j, both_ref in enumerate(both_refs):

        @pl.when(pl.program_id(0) == j + 1)
        def _():
            both_ref[0] = frames_ref[...]
            both_ref[1] = grad


def prepare(frames, cotangent, before, behind, taps, width):
    rows, local_width = frames.shape
    blocks = local_width // width
    column = lambda r: pl.BlockSpec((r, width), lambda i: (0, i))
    outs = pl.pallas_call(
        prepare_kernel,
        out_shape=[jax.ShapeDtypeStruct((rows, local_width), bf16)]
        + [jax.ShapeDtypeStruct((2, rows, width), bf16)] * (blocks - 1),
        grid=(blocks,),
        in_specs=[column(rows), column(rows), column(1), column(1), column(3)],
        out_specs=[column(rows)] + [pl.BlockSpec((2, rows, width), lambda i: (0, 0, 0))] * (blocks - 1),
        compiler_params=pltpu.CompilerParams(vmem_limit_bytes=VMEM_LIMIT),
        cost_estimate=cost(),
        name="prepare",
    )(frames, cotangent, before, behind, taps)
    return outs[0], outs[1:]


def convolution_kernel(x_ref, before_ref, behind_ref, taps_ref, out_ref, *, order):
    out_ref[...] = convolved_rows(x_ref[...].astype(f32), before_ref[...], behind_ref[...], taps_ref, order)


def convolution(x, before, behind, taps, order, width, blocks, flops=1):
    rows = x.shape[0]
    column = lambda r: pl.BlockSpec((r, width), lambda i: (0, i))
    return pl.pallas_call(
        functools.partial(convolution_kernel, order=order),
        out_shape=jax.ShapeDtypeStruct((rows, blocks * width), bf16),
        grid=(blocks,),
        in_specs=[column(rows), column(1), column(1), column(3)],
        out_specs=column(rows),
        compiler_params=pltpu.CompilerParams(vmem_limit_bytes=VMEM_LIMIT),
        cost_estimate=cost(flops),
        name="convolution",
    )(x, before, behind, taps)


def pair_parts(kept_ref, got_ref, bit):
    parts = [[], []]
    for r in range(kept_ref.shape[0]):
        total = (kept_ref[r].astype(f32) + got_ref[r].astype(f32)).astype(bf16)
        parts[r >> bit & 1].append(total)
    return parts


def level_index(level_bits, bit, levels):
    at = jnp.int32(0)
    for level in range(levels):
        at = at + jnp.where(level_bits[level] == bit, level + 1, 0)
    return at


def layer_kernel(level_bits, pattern, place, *refs, block, ratio, levels, peers, scale, older):
    terms = 1 + levels
    x_refs, refs = refs[:terms], refs[terms:]
    g_refs, refs = refs[:terms], refs[terms:]
    u_ref, d_ref = refs[:2]
    refs = refs[2:]
    if older:
        old_refs, refs = refs[:4], refs[4:]
    up_sent, up_kept, down_sent, down_kept, hidden_ref, grad_ref = refs[:6]
    refs = refs[6:]
    if older:
        (up_last, down_last), refs = refs[:2], refs[2:]
    x_all, x_turned, g_all, u_all, d_all, turned = refs
    h = pl.program_id(0)
    rows, width = x_refs[0].shape
    slab = width // peers
    k = block * ratio + h
    me = place[0]
    stages = peers.bit_length() - 1
    level_at = [level_index(level_bits, bit, levels) for bit in range(levels)]
    present = [pattern[k, at - 1] for at in level_at]

    @pl.when(h == 0)
    def _():
        for b in range(terms):
            value = x_refs[b][...]
            x_all[:, b * width : (b + 1) * width] = value
            g_all[:, b * width : (b + 1) * width] = g_refs[b][...]
            turned[...] = value.T
            for r in range(peers):
                start = pl.multiple_of((me ^ r) * slab, slab)
                x_turned[b * width + r * slab : b * width + (r + 1) * slab, :] = turned[pl.ds(start, slab), :]

    if older:
        up_parts = pair_parts(old_refs[0], old_refs[1], 0)
        down_parts = pair_parts(old_refs[2], old_refs[3], 0)
        up_last[0], down_sent[2] = up_parts[0][0], up_parts[1][0]
        down_last[0], up_sent[2] = down_parts[0][0], down_parts[1][0]

    for b in range(terms):
        if b == 0:
            u, d = u_ref[0, 0], d_ref[0, 0]
        else:
            mask = present[b - 1].astype(f32).astype(bf16)
            u, d = u_ref[level_at[b - 1], 0] * mask, d_ref[level_at[b - 1], 0] * mask
        u_all[b * width : (b + 1) * width, :] = u
        d_all[:, b * width : (b + 1) * width] = d

    pre = jnp.dot(x_all[...], u_all[...], preferred_element_type=f32)
    grad_hidden = lax.dot_general(
        g_all[...], d_all[...], (((1,), (1,)), ((), ())), preferred_element_type=f32
    )
    square = pre * pre
    inner = jnp.tanh(coef * (pre + cubic * (square * pre)))
    half = 0.5 * (1.0 + inner)
    slope = half + (0.5 * coef) * pre * (1.0 - inner * inner) * (1.0 + (3.0 * cubic) * square)
    hidden = (pre * half).astype(bf16)
    hidden_ref[...] = hidden
    turned[...] = hidden.T
    hidden_turned = jnp.concatenate(
        [
            turned[pl.ds(pl.multiple_of((me ^ r) * slab, slab), slab), :]
            for r in range(peers)
        ],
        axis=0,
    )
    grad_pre = (grad_hidden * slope).astype(bf16)
    grad_ref[...] = grad_pre

    for b in range(terms):
        span = slice(b * width, (b + 1) * width)
        up = jnp.dot(x_turned[span, :], grad_pre, preferred_element_type=f32)
        down = jnp.dot(hidden_turned, g_all[:, span], preferred_element_type=f32)
        if b == 0:
            factor, slot = scale, 0
        else:
            factor, slot = present[b - 1].astype(f32) * scale, level_at[b - 1]
        up, down = (up * factor).astype(bf16), (down * factor).astype(bf16)
        for value, sent, kept, bit in ((up, up_sent, up_kept, 0), (down, down_sent, down_kept, stages - 1)):
            counts = [0, 0]
            for r in range(peers):
                which = r >> bit & 1
                target = sent if which else kept
                target[counts[which], slot, 0] = value[r * slab : (r + 1) * slab, :]
                counts[which] += 1


def layer(level_bits, pattern, place, x, g, up_factors, down_factors, block, blocks_dev, peers, scale, older):
    terms, hidden_dev, width, _ = up_factors.shape
    levels = terms - 1
    rows = x[0][0].shape[0]
    ratio = hidden_dev // blocks_dev
    slab = width // peers
    inputs = [
        pl.BlockSpec((rows, width), lambda h, *s, at=at: at)
        if array.ndim == 2
        else pl.BlockSpec((None, rows, width), lambda h, *s, at=at: (at[0], 0, at[1]))
        for array, at in x + g
    ]
    weight = pl.BlockSpec((terms, 1, width, width), lambda h, *s: (0, block * ratio + h, 0, 0))
    piece = lambda n: pl.BlockSpec((n, terms, 1, slab, width), lambda h, *s: (0, 0, h, 0, 0))
    piece_shape = lambda n: jax.ShapeDtypeStruct((n, terms, ratio, slab, width), bf16)
    extra = [] if older is None else list(older)
    sums = [peers // 2 + (older is not None), peers // 2] * 2
    last = [] if older is None else [1, 1]
    outs = pl.pallas_call(
        functools.partial(
            layer_kernel,
            block=block,
            ratio=ratio,
            levels=levels,
            peers=peers,
            scale=scale,
            older=older is not None,
        ),
        out_shape=[piece_shape(n) for n in sums]
        + [jax.ShapeDtypeStruct((rows, ratio * width), bf16)] * 2
        + [piece_shape(n) for n in last],
        grid_spec=pltpu.PrefetchScalarGridSpec(
            num_scalar_prefetch=3,
            grid=(ratio,),
            in_specs=inputs + [weight] * 2 + [piece(2)] * len(extra),
            out_specs=[piece(n) for n in sums]
            + [pl.BlockSpec((rows, width), lambda h, *s: (0, h))] * 2
            + [piece(n) for n in last],
            scratch_shapes=[
                pltpu.VMEM((rows, terms * width), bf16),
                pltpu.VMEM((terms * width, rows), bf16),
                pltpu.VMEM((rows, terms * width), bf16),
                pltpu.VMEM((terms * width, width), bf16),
                pltpu.VMEM((width, terms * width), bf16),
                pltpu.VMEM((width, rows), bf16),
            ],
        ),
        compiler_params=pltpu.CompilerParams(vmem_limit_bytes=VMEM_LIMIT),
        cost_estimate=cost(LONG),
        name="layer",
    )(level_bits, pattern, place, *[array for array, _ in x + g], up_factors, down_factors, *extra)
    return outs[:4], outs[4], outs[5], outs[6:]


def terms_kernel(level_bits, pattern, hidden_ref, grad_ref, u_ref, d_ref, *refs, block, ratio, levels, local_bits, remote_bits):
    home_ref, *away_refs = refs[-1 - remote_bits :]
    b = pl.program_id(0)
    width = u_ref.shape[-1]
    at = level_index(level_bits, b - 1, levels)
    us, ds = [], []
    for h in range(ratio):
        present = jnp.where(b == 0, 1, pattern[block * ratio + h, jnp.maximum(at - 1, 0)])
        mask = present.astype(f32).astype(bf16)
        us.append(u_ref[0, h] * mask)
        ds.append(d_ref[0, h] * mask)
    mixed = jnp.dot(hidden_ref[...], jnp.concatenate(ds, axis=0), preferred_element_type=f32).astype(bf16)
    grad = lax.dot_general(
        grad_ref[...], jnp.concatenate(us, axis=1), (((1,), (1,)), ((), ())), preferred_element_type=f32
    ).astype(bf16)

    @pl.when(b <= local_bits)
    def _():
        home_ref[0, b], home_ref[1, b] = mixed, grad

    for bit, away_ref in enumerate(away_refs):

        @pl.when(b == 1 + local_bits + bit)
        def _():
            away_ref[0], away_ref[1] = mixed, grad


def term_sums(level_bits, pattern, hidden, grad, up_factors, down_factors, block, blocks_dev, together, away):
    terms, hidden_dev, width, _ = up_factors.shape
    levels = terms - 1
    rows = hidden.shape[0]
    ratio = hidden_dev // blocks_dev
    local_bits = blocks_dev.bit_length() - 1
    remote_bits = levels - local_bits
    whole = pl.BlockSpec((rows, ratio * width), lambda b, *s: (0, 0))
    weight = pl.BlockSpec(
        (1, ratio, width, width), lambda b, bits, *s: (level_index(bits, b - 1, levels), block, 0, 0)
    )
    extra = [] if away is None else list(away)
    outs = pl.pallas_call(
        functools.partial(
            terms_kernel, block=block, ratio=ratio, levels=levels, local_bits=local_bits, remote_bits=remote_bits
        ),
        out_shape=[jax.ShapeDtypeStruct((2, 1 + local_bits, rows, width), bf16)]
        + [jax.ShapeDtypeStruct((2 * together, rows, width), bf16)] * remote_bits,
        grid_spec=pltpu.PrefetchScalarGridSpec(
            num_scalar_prefetch=2,
            grid=(terms,),
            in_specs=[whole, whole, weight, weight] + [ANY] * len(extra),
            out_specs=[pl.BlockSpec((2, 1 + local_bits, rows, width), lambda b, *s: (0, 0, 0, 0))]
            + [pl.BlockSpec((2, rows, width), lambda b, *s: (block % together, 0, 0))] * remote_bits,
        ),
        input_output_aliases={6 + i: 1 + i for i in range(len(extra))},
        compiler_params=pltpu.CompilerParams(vmem_limit_bytes=VMEM_LIMIT),
        cost_estimate=cost(LONG if block == 0 else 1),
        name="term_sums",
    )(level_bits, pattern, hidden, grad, up_factors, down_factors, *extra)
    return outs[0], outs[1:]


def pair_kernel(*refs, bits):
    ins, outs = refs[: 2 * len(bits)], refs[2 * len(bits) :]
    for n, bit in enumerate(bits):
        kept, sent = pair_parts(ins[2 * n], ins[2 * n + 1], bit)
        for i, (a, b) in enumerate(zip(kept, sent)):
            outs[2 * n][i], outs[2 * n + 1][i] = a, b


def pair_sums(pairs, bits):
    parts, terms, blocks, slab, width = pairs[0][0].shape
    step = 2 if terms % 2 == 0 else 1
    spec = lambda n: pl.BlockSpec((n, terms // step, blocks, slab, width), lambda i: (0, i, 0, 0, 0))
    half = jax.ShapeDtypeStruct((parts // 2, terms, blocks, slab, width), bf16)
    outs = pl.pallas_call(
        functools.partial(pair_kernel, bits=bits),
        out_shape=[half] * 2 * len(pairs),
        grid=(step,),
        in_specs=[spec(parts)] * 2 * len(pairs),
        out_specs=[spec(parts // 2)] * 2 * len(pairs),
        compiler_params=pltpu.CompilerParams(vmem_limit_bytes=VMEM_LIMIT),
        cost_estimate=cost(LONG),
        name="pair_sums",
    )(*[array for pair in pairs for array in pair])
    return [outs[2 * i : 2 * i + 2] for i in range(len(pairs))]


def finish_kernel(a_kept, a_got, b_kept, b_got, *refs):
    a_out, b_out = refs[-2:]
    a_out[...] = a_kept[0].astype(f32) + a_got[0].astype(f32)
    b_out[...] = b_kept[0].astype(f32) + b_got[0].astype(f32)


def finish(a_kept, a_got, b_kept, b_got, outs, first, hidden_dev):
    _, terms, blocks, slab, width = a_kept.shape
    step = 2 if terms % 2 == 0 else 1
    spec = lambda array: pl.BlockSpec(
        (1, terms // step, blocks, slab, width), lambda i, row=array.shape[0] - 1: (row, i, 0, 0, 0)
    )
    out_spec = pl.BlockSpec((terms // step, blocks, slab, width), lambda i: (i, first // blocks, 0, 0))
    shape = jax.ShapeDtypeStruct((terms, hidden_dev, slab, width), f32)
    extra = [] if outs is None else list(outs)
    return pl.pallas_call(
        finish_kernel,
        out_shape=[shape, shape],
        grid=(step,),
        in_specs=[spec(array) for array in (a_kept, a_got, b_kept, b_got)] + [ANY] * len(extra),
        out_specs=[out_spec] * 2,
        input_output_aliases={4 + i: i for i in range(len(extra))},
        compiler_params=pltpu.CompilerParams(vmem_limit_bytes=VMEM_LIMIT),
        cost_estimate=cost(),
        name="finish",
    )(a_kept, a_got, b_kept, b_got, *extra)


def combine_kernel(*refs, blocks_dev, remote_bits, local_bits):
    homes, refs = refs[:blocks_dev], refs[blocks_dev:]
    aways, (mixed_ref, grad_ref) = refs[:-2], refs[-2:]
    width = homes[0].shape[-1]
    for j in range(blocks_dev):
        for side, target in ((0, mixed_ref), (1, grad_ref)):
            total = homes[j][side, 0].astype(f32)
            for bit in range(local_bits):
                total = total + homes[j ^ 1 << bit][side, 1 + bit].astype(f32)
            for bit in range(remote_bits):
                total = total + aways[j * remote_bits + bit][side].astype(f32)
            target[:, j * width : (j + 1) * width] = total.astype(bf16)


def combine(homes, aways, together):
    rows, width = homes[0].shape[-2:]
    blocks_dev = len(homes)
    local_bits, remote_bits = homes[0].shape[1] - 1, len(aways[0])
    chunk = min(rows, 128)
    home = pl.BlockSpec((2, 1 + local_bits, chunk, width), lambda i: (0, 0, i, 0))
    away = [
        pl.BlockSpec((2, chunk, width), lambda i, at=j % together: (at, i, 0))
        for j in range(blocks_dev)
        for _ in range(remote_bits)
    ]
    out = pl.BlockSpec((chunk, blocks_dev * width), lambda i: (i, 0))
    shape = jax.ShapeDtypeStruct((rows, blocks_dev * width), bf16)
    return pl.pallas_call(
        functools.partial(combine_kernel, remote_bits=remote_bits, local_bits=local_bits, blocks_dev=blocks_dev),
        out_shape=[shape, shape],
        grid=(rows // chunk,),
        in_specs=[home] * blocks_dev + away,
        out_specs=[out, out],
        compiler_params=pltpu.CompilerParams(vmem_limit_bytes=VMEM_LIMIT),
        cost_estimate=cost(),
        name="combine",
    )(*homes, *[part for j in range(blocks_dev) for part in aways[j // together]])


def local(frames, up_factors, down_factors, pattern, level_bits, taps, cotangent):
    rows, local_width = frames.shape
    terms, hidden_dev, width, _ = up_factors.shape
    blocks_dev = local_width // width
    ratio = hidden_dev // blocks_dev
    levels = terms - 1
    local_bits = blocks_dev.bit_length() - 1
    remote_bits = levels - local_bits
    far = list(range(1, remote_bits))
    together = min(2, blocks_dev)
    peers = lax.axis_size("seq")
    stages = peers.bit_length() - 1
    scale = 1.0 / math.sqrt(rows * peers)
    place = lax.axis_index("seq").astype(jnp.int32).reshape(1)

    def fetch(pieces, bits):
        got = {bit: swapped(pieces[bit], "tensor", bit) for bit in reversed(bits)}
        return [got[bit] for bit in bits]

    first = jnp.concatenate([frames[:, :width], frames[:16, :width]])
    x_first = fetch({bit: first for bit in far}, far)
    x_near = swapped(frames, "tensor", 0)
    before, behind = halo(cotangent)
    before = after(before, x_near)
    g_block = convolution(cotangent, before, behind, taps, (2, 1, 0), width, 1)
    g_first = fetch({bit: g_block for bit in far}, far)
    g_near_first = swapped(g_block, "tensor", 0)
    grad_mixed, both = prepare(frames, cotangent, after(before, g_block), behind, taps, width)
    g_near = swapped(grad_mixed, "tensor", 0)
    x_away = {0: [(value, (0, 0)) for value in x_first]}
    g_away = {0: [(value, (0, 0)) for value in g_first]}
    guards = [x_first, g_first]

    def fetch_far(pieces, *others):
        arrived = fetch({bit: after(pieces[bit], *[g[i] for g in guards], *others) for i, bit in enumerate(far)}, far)
        guards[:] = [arrived]
        return arrived

    def fetch_block(j, *others):
        arrived = fetch_far({bit: both[j - 1] for bit in far}, *others)
        x_away[j] = [(value, (0, 0)) for value in arrived]
        g_away[j] = [(value, (1, 0)) for value in arrived]

    if blocks_dev > 1:
        fetch_block(1)

    homes, aways, sums = [], [], {}
    merged = stages == 2
    x_got, y_got = {}, {}
    away = None
    made = []

    def give_terms(j, *others):
        nonlocal away
        hidden, grad_pre = made[j]
        home, away = term_sums(
            level_bits, pattern, after(hidden, *others) if others else hidden, grad_pre, up_factors, down_factors,
            j, blocks_dev, together, None if j % together == 0 else away,
        )
        homes.append(home)
        if (j + 1) % together == 0:
            aways.append((away[0], fetch_far(away)))

    for j in range(blocks_dev):
        older = None
        if merged and j >= 2:
            older = (sums[j - 2][0], x_got[j - 2], sums[j - 2][1], y_got[j - 2])
        flips = [0] + [1 << bit for bit in range(local_bits)]
        x = [(frames, (0, j ^ flip)) for flip in flips] + [(x_near, (0, j))] + x_away[j]
        g_near_block = (g_near_first, (0, 0)) if j == 0 else (g_near, (0, j))
        g = [(grad_mixed, (0, j ^ flip)) for flip in flips] + [g_near_block] + g_away[j]
        (up_sent, up_kept, down_sent, down_kept), hidden, grad_pre, last = layer(
            level_bits, pattern, place, x, g, up_factors, down_factors, j, blocks_dev, peers, scale, older
        )
        sums[j] = (up_kept, down_kept)
        if older is not None:
            sums[j - 2] = tuple(last)
        if j > 0:
            up_sent, down_sent = after(up_sent, x_got[j - 1]), after(down_sent, y_got[j - 1])
        x_got[j] = swapped(up_sent, "seq", 0)
        y_got[j] = swapped(down_sent, "seq", stages - 1)
        made.append((hidden, grad_pre))
        if j == 0:
            give_terms(0)
        if j + 2 < blocks_dev:
            fetch_block(j + 2, homes[0] if j == 0 else hidden)
        if j >= 2:
            give_terms(j - 1, hidden)
        if 0 < j == blocks_dev - 1:
            give_terms(j)

    def combined(*others):
        groups = []
        for near, rest in aways:
            groups.append([swapped(after(near, *others) if others else near, "tensor", 0)] + rest)
        mixed, grad_frames = combine(homes, groups, together)
        return mixed, grad_frames, *halo(mixed)

    outs = None
    if merged:

        def end(j):
            return (sums[j][0], y_got[j + 2], sums[j][1], x_got[j + 2])

        for j in range(max(blocks_dev - 2, 0), blocks_dev):
            got = [x_got[j], y_got[j]]
            if j == blocks_dev - 1:
                mixed, grad_frames, before, behind = combined(*([sums[j - 1][0]] if j else []))
                for done in range(blocks_dev - 3):
                    outs = finish(*end(done), outs, done * ratio, hidden_dev)
                got = [after(value, before, behind, *(outs or [])) for value in got]
            (up_last, up_next), (down_last, down_next) = pair_sums([(sums[j][0], got[0]), (sums[j][1], got[1])], (0, 0))
            if j + 1 < blocks_dev:
                down_next, up_next = after(down_next, x_got[j + 1]), after(up_next, y_got[j + 1])
            x_got[j + 2] = swapped(down_next, "seq", 0)
            y_got[j + 2] = swapped(up_next, "seq", 1)
            sums[j] = (up_last, down_last)
        convolved = convolution(mixed, before, behind, taps, (0, 1, 2), width, blocks_dev)
        for j in range(max(blocks_dev - 3, 0), blocks_dev):
            kept, got, down_kept, down_got = end(j)
            if j == blocks_dev - 2:
                got = after(got, convolved)
            outs = finish(kept, got, down_kept, down_got, outs, j * ratio, hidden_dev)
    else:
        for j in range(blocks_dev):
            got = [x_got[j], y_got[j]]
            kept = list(sums[j])
            orders = (list(range(stages)), list(range(stages))[::-1])
            for stage in range(1, stages):
                at = [sorted(order[stage:]).index(order[stage]) for order in orders]
                halves = pair_sums(list(zip(kept, got)), at)
                for side, order in enumerate(orders):
                    kept[side], sent = halves[side]
                    got[side] = swapped(sent, "seq", order[stage])
            outs = finish(kept[0], got[0], kept[1], got[1], outs, j * ratio, hidden_dev)
        mixed, grad_frames, before, behind = combined()
        convolved = convolution(mixed, before, behind, taps, (0, 1, 2), width, blocks_dev)
    return convolved, grad_frames, outs[0], outs[1]


def solution(mesh):
    in_specs = (
        P("seq", "tensor"),
        P(None, "tensor", None, None),
        P(None, "tensor", None, None),
        P("tensor", None),
        P(),
        P(None, "tensor"),
        P("seq", "tensor"),
    )
    out_specs = (
        P("seq", "tensor"),
        P("seq", "tensor"),
        P(None, "tensor", "seq", None),
        P(None, "tensor", "seq", None),
    )
    return jax.shard_map(local, mesh=mesh, in_specs=in_specs, out_specs=out_specs, check_vma=False)
```

time: 369 us -> 274 us (0.74)
  waiting for transfers between devices: 145 us -> 84.2 us
  starting transfers between devices: 55.7 us -> 41.1 us
  local copies, waits for them, and re-layouts: 19.6 us -> 7.01 us
  Pallas kernels: 145 us -> 139 us
    ppermute x43 -> x31, waiting for transfers between devices: 119 us -> 80 us  [swapped(): lax.ppermute(array, axis, [(i, i ^ 1 << bit) for i in range(lax.axis_size...]
    ppermute x2, waiting for transfers between devices: 26.6 us -> 4.16 us  [halo(): behind = lax.ppermute(lax.slice_in_dim(array, 0, 1), 'seq', down)]
    ppermute x43 -> x31, starting transfers between devices: 46.1 us -> 30.5 us  [swapped(): lax.ppermute(array, axis, [(i, i ^ 1 << bit) for i in range(lax.axis_size...]
    squeeze x9 -> x0, local copies, waits for them, and re-layouts: 7.54 us -> none  [local(): g_away.append([value[1] for value in arrived])]
    pallas_call x19 -> x18, Pallas kernels: 145 us -> 139 us  [the longest x4 60.5 us: layer(): pl.pallas_call(functools.partial(layer_kernel, block=block, ratio=ratio,...]
    unnamed x92 -> x35, local copies, waits for them, and re-layouts: 8.76 us -> 3.85 us
  transfers between devices with their start and end apart: 47 -> 35, of which waited for: 17 -> 13; matrix products, arithmetic and copies ran while one was open for 3% -> 1% of each run, Pallas kernels for 38% -> 50%
where the time goes in v2:
time: 274 us; the launch traced here: 272 us
  Pallas kernels  139 us (51%)
  waiting for transfers between devices  84.2 us (31%)
  starting transfers between devices  41.1 us (15%)
  local copies, waits for them, and re-layouts  7.01 us (3%)
    ppermute x31, waiting for transfers between devices, swapped(): lax.ppermute(array, axis, [(i, i ^ 1 << bit) for i in range(lax.axis_size...  80 us
    pallas_call x4, Pallas kernels, layer(): pl.pallas_call(functools.partial(layer_kernel, block=block, ratio=ratio,...  60.5 us
    pallas_call x4, Pallas kernels, term_sums(): pl.pallas_call(functools.partial(terms_kernel, block=block, ratio=ratio,...  40.8 us
    ppermute x31, starting transfers between devices, swapped(): lax.ppermute(array, axis, [(i, i ^ 1 << bit) for i in range(lax.axis_size...  30.5 us
    pallas_call x4, Pallas kernels, finish(): pl.pallas_call(finish_kernel, out_shape=[shape, shape], grid=(step,), in_...  12.7 us
    pallas_call x2, Pallas kernels, pair_sums(): pl.pallas_call(functools.partial(pair_kernel, bits=bits), out_shape=[half...  8.63 us
    ppermute x2, starting transfers between devices, halo(): before = lax.ppermute(lax.slice_in_dim(array, rows - 1, rows), 'seq', up)  7.94 us
    pallas_call x1, Pallas kernels, combine(): pl.pallas_call(functools.partial(combine_kernel, remote_bits=remote_bits,...  6.68 us
  transfers between devices with their start and end apart: 35, of which 13 were waited for; matrix products, arithmetic and copies ran while one was open for 1% of the time, Pallas kernels for 50%

profile of v2, /device:TPU:0, one launch (start us, length us, event | category | flops | bytes accessed | tf_op | source)
XLA Modules:
  0.0 272.5 jit_solution(3850716723892196872)
XLA Ops:
  1.9 1.0 slice.18
  2.9 3.7 %collective-permute-start.2 = (bf16[528,256]{1,0:T(8,128)(2,1)S(1)}, bf16[528,256]{1,0:T(8,128)(2,1)S(1)}, u32[]{:S(2)}, u32[]{:S(2)}) collective-permute-start(bf16[528,256]{1,0:T(8,128)(2,1)S(1)} %pad_maximum_fusion), channel_id=1, source_target_pairs={{0,4},{1,5},{2,6},{3,7},{4,0},{5,1},{6,2},{7,3},{8,12},{9,13},{10,... | collective-permute-start | bytes 811016 | tf_op jit(solution)/shard_map/ppermute | solution.py:21
  6.5 1.6 collective-permute-start.1
  8.8 3.4 %collective-permute-start.3 = (bf16[1,1024]{1,0:T(2,128)(2,1)S(1)}, bf16[1,1024]{1,0:T(2,128)(2,1)S(1)}, u32[]{:S(2)}, u32[]{:S(2)}) collective-permute-start(bf16[1,1024]{1,0:T(2,128)(2,1)S(1)} %get-tuple-element.193), channel_id=1, source_target_pairs={{0,8},{8,16},{16,24},{1,9},{9,17},{17,25},{2,10},{10,18},{18,26},{... | collective-permute-start | bytes 6152 | tf_op jit(solution)/shard_map/ppermute | solution.py:37
  12.2 1.3 collective-permute-start.4
  13.6 4.2 %collective-permute-done.4.behind_ref = bf16[1,1024]{1,0:T(2,128)(2,1)S(1)} collective-permute-done((bf16[1,1024]{1,0:T(2,128)(2,1)S(1)}, bf16[1,1024]{1,0:T(2,128)(2,1)S(1)}, u32[]{:S(2)}, u32[]{:S(2)}) %collective-permute-start.4) | collective-permute-done | bytes 2080 | tf_op jit(solution)/shard_map/ppermute | solution.py:38
  18.3 1.9 convolution.2
  21.7 4.5 %prepare.1 = (bf16[512,1024]{1,0:T(8,128)(2,1)}, bf16[2,512,256]{2,1,0:T(8,128)(2,1)}, bf16[2,512,256]{2,1,0:T(8,128)(2,1)}, bf16[2,512,256]{2,1,0:T(8,128)(2,1)}) custom-call(bf16[512,1024]{1,0:T(8,128)(2,1)} %refs_2_.7, bf16[512,1024]{1,0:T(8,128)(2,1)} %cot_ref.1, bf16[1,1024]{1,0:T(2,128)(2,1)} %copy-done.6, bf16[1,1024]{1,0:T(2,128)(2,1)} %copy-done.7, ...), custom_call_target="tpu_custom_call" | custom-call | flops 1 | bytes 1 | tf_op jit(solution)/shard_map/prepare/pallas_call | solution.py:70
  26.8 7.1 %collective-permute-done.7.refs_11_ = bf16[512,256]{1,0:T(8,128)(2,1)S(1)} collective-permute-done((bf16[512,256]{1,0:T(8,128)(2,1)}, bf16[512,256]{1,0:T(8,128)(2,1)S(1)}, u32[]{:S(2)}, u32[]{:S(2)}) %collective-permute-start.7) | collective-permute-done | bytes 262176 | tf_op jit(solution)/shard_map/ppermute | solution.py:21
  33.9 1.1 collective-permute-start.9
  35.8 14.1 %layer.4 = (bf16[2,6,4,64,256]{4,3,2,1,0:T(8,128)(2,1)}, bf16[2,6,4,64,256]{4,3,2,1,0:T(8,128)(2,1)}, bf16[2,6,4,64,256]{4,3,2,1,0:T(8,128)(2,1)}, bf16[2,6,4,64...) custom-call(s32[5]{0:T(128)} %level_bits.15, s32[16,5]{1,0:T(8,128)} %copy.24.pattern, ...), custom_call_target="tpu_custom_call" | custom-call | flops 199999995904 | bytes 1 | tf_op jit(solution)/shard_map/layer/pallas_call | solution.py:223
  49.9 2.4 collective-permute-start.13
  52.8 10.2 %term_sums.4 = (bf16[2,3,512,256]{3,2,1,0:T(8,128)(2,1)}, bf16[4,512,256]{2,1,0:T(8,128)(2,1)}, bf16[4,512,256]{2,1,0:T(8,128)(2,1)}, bf16[4,512,256]{2,1,0:T(8,128)(2,1)}) custom-call(s32[5]{0:T(128)} %level_bits.15, s32[16,5]{1,0:T(8,128)} %copy.24.pattern, bf16[512,1024]{1,0:T(8,128)(2,1)} %get-tuple-element.100.hidden_ref, ...), custom_call_target="tpu_custom_call" | custom-call | flops 199999995904 | bytes 1 | tf_op jit(solution)/shard_map/term_sums/pallas_call | solution.py:298
  63.7 2.4 collective-permute-start.12
  66.1 14.2 %layer.5 = (bf16[2,6,4,64,256]{4,3,2,1,0:T(8,128)(2,1)}, bf16[2,6,4,64,256]{4,3,2,1,0:T(8,128)(2,1)}, bf16[2,6,4,64,256]{4,3,2,1,0:T(8,128)(2,1)}, bf16[2,6,4,64...) custom-call(s32[5]{0:T(128)} %level_bits.15, s32[16,5]{1,0:T(8,128)} %copy.24.pattern, ...), custom_call_target="tpu_custom_call" | custom-call | flops 199999995904 | bytes 1 | tf_op jit(solution)/shard_map/layer/pallas_call | solution.py:223
  80.3 8.4 %collective-permute-done.12.refs_5_.refs_11_ = bf16[2,512,256]{2,1,0:T(8,128)(2,1)} collective-permute-done((bf16[2,512,256]{2,1,0:T(8,128)(2,1)}, bf16[2,512,256]{2,1,0:T(8,128)(2,1)}, u32[]{:S(2)}, u32[]{:S(2)}) %collective-permute-start.12) | collective-permute-done | bytes 524320 | tf_op jit(solution)/shard_map/ppermute | solution.py:21
  89.1 2.6 collective-permute-start.16
  91.8 1.7 collective-permute-start.18
  93.9 16.0 %layer.6 = (bf16[3,6,4,64,256]{4,3,2,1,0:T(8,128)(2,1)}, bf16[2,6,4,64,256]{4,3,2,1,0:T(8,128)(2,1)}, bf16[3,6,4,64,256]{4,3,2,1,0:T(8,128)(2,1)}, bf16[2,6,4,64...) custom-call(s32[5]{0:T(128)} %level_bits.15, ...), custom_call_target="tpu_custom_call" | custom-call | flops 199999995904 | bytes 1 | tf_op jit(solution)/shard_map/layer/pallas_call | solution.py:223
  109.8 10.2 %term_sums.5 = (bf16[2,3,512,256]{3,2,1,0:T(8,128)(2,1)}, bf16[4,512,256]{2,1,0:T(8,128)(2,1)}, bf16[4,512,256]{2,1,0:T(8,128)(2,1)}, bf16[4,512,256]{2,1,0:T(8,128)(2,1)}) custom-call(s32[5]{0:T(128)} %level_bits.15, s32[16,5]{1,0:T(8,128)} %copy.24.pattern, ...), custom_call_target="tpu_custom_call", output_to_operand_aliasing={{1}: (6, {}), {2}: (7, {}), {3}: (8, {})} | custom-call | flops 1 | bytes 1 | tf_op jit(solution)/shard_map/term_sums/pallas_call | solution.py:298
  120.4 1.7 collective-permute-start.22
  122.1 3.1 %collective-permute-done.18.refs_17_ = bf16[2,6,4,64,256]{4,3,2,1,0:T(8,128)(2,1)} collective-permute-done((bf16[2,6,4,64,256]{4,3,2,1,0:T(8,128)(2,1)}, bf16[2,6,4,64,256]{4,3,2,1,0:T(8,128)(2,1)}, u32[]{:S(2)}, u32[]{:S(2)}) %collective-permute-start.18) | collective-permute-done | bytes 1572896 | tf_op jit(solution)/shard_map/ppermute | solution.py:21
  125.1 2.9 %collective-permute-done.17.refs_15_ = bf16[2,6,4,64,256]{4,3,2,1,0:T(8,128)(2,1)} collective-permute-done((bf16[2,6,4,64,256]{4,3,2,1,0:T(8,128)(2,1)}, bf16[2,6,4,64,256]{4,3,2,1,0:T(8,128)(2,1)}, u32[]{:S(2)}, u32[]{:S(2)}) %collective-permute-start.17) | collective-permute-done | bytes 1572896 | tf_op jit(solution)/shard_map/ppermute | solution.py:21
  128.4 1.1 collective-permute-start.20
  129.5 16.2 %layer.7 = (bf16[3,6,4,64,256]{4,3,2,1,0:T(8,128)(2,1)}, bf16[2,6,4,64,256]{4,3,2,1,0:T(8,128)(2,1)}, bf16[3,6,4,64,256]{4,3,2,1,0:T(8,128)(2,1)}, bf16[2,6,4,64...) custom-call(s32[5]{0:T(128)} %level_bits.15, ...), custom_call_target="tpu_custom_call" | custom-call | flops 199999995904 | bytes 1 | tf_op jit(solution)/shard_map/layer/pallas_call | solution.py:223
  145.7 10.2 %term_sums.6 = (bf16[2,3,512,256]{3,2,1,0:T(8,128)(2,1)}, bf16[4,512,256]{2,1,0:T(8,128)(2,1)}, bf16[4,512,256]{2,1,0:T(8,128)(2,1)}, bf16[4,512,256]{2,1,0:T(8,128)(2,1)}) custom-call(s32[5]{0:T(128)} %level_bits.15, s32[16,5]{1,0:T(8,128)} %copy.24.pattern, bf16[512,1024]{1,0:T(8,128)(2,1)} %get-tuple-element.131.hidden_ref, ...), custom_call_target="tpu_custom_call" | custom-call | flops 1 | bytes 1 | tf_op jit(solution)/shard_map/term_sums/pallas_call | solution.py:298
  155.9 10.2 %term_sums.7 = (bf16[2,3,512,256]{3,2,1,0:T(8,128)(2,1)}, bf16[4,512,256]{2,1,0:T(8,128)(2,1)}, bf16[4,512,256]{2,1,0:T(8,128)(2,1)}, bf16[4,512,256]{2,1,0:T(8,128)(2,1)}) custom-call(s32[5]{0:T(128)} %level_bits.15, s32[16,5]{1,0:T(8,128)} %copy.24.pattern, ...), custom_call_target="tpu_custom_call", output_to_operand_aliasing={{1}: (6, {}), {2}: (7, {}), {3}: (8, {})} | custom-call | flops 1 | bytes 1 | tf_op jit(solution)/shard_map/term_sums/pallas_call | solution.py:298
  166.5 1.6 collective-permute-start.25
  168.1 11.1 %collective-permute-done.19.refs_1_.b_got = bf16[3,6,4,64,256]{4,3,2,1,0:T(8,128)(2,1)} collective-permute-done((bf16[3,6,4,64,256]{4,3,2,1,0:T(8,128)(2,1)}, bf16[3,6,4,64,256]{4,3,2,1,0:T(8,128)(2,1)}, u32[]{:S(2)}, u32[]{:S(2)}) %collective-permute-start.19) | collective-permute-done | bytes 2359328 | tf_op jit(solution)/shard_map/ppermute | solution.py:21
  180.3 4.4 %pair_sums.2 = (bf16[1,6,4,64,256]{4,3,2,1,0:T(8,128)(2,1)}, bf16[1,6,4,64,256]{4,3,2,1,0:T(8,128)(2,1)}, bf16[1,6,4,64,256]{4,3,2,1,0:T(8,128)(2,1)}, bf16[1,6,4,64,256]{4,3,2,1,0:T(8,128)(2,1)}) custom-call(bf16[2,6,4,64,256]{4,3,2,1,0:T(8,128)(2,1)} %get-tuple-element.140.refs_0_, bf16[3,6,4,64,256]{4,3,2,1,0:T(8,128)(2,1)} %collective-permute-done.19.refs_1_.b_got, ...), custom_call_target="tpu_custom_call" | custom-call | flops 199999995904 | bytes 1 | tf_op jit(solution)/shard_map/pair_sums/pallas_call | solution.py:332
  184.8 26.5 %collective-permute-done.26.refs_12_.refs_15_ = bf16[4,512,256]{2,1,0:T(8,128)(2,1)} collective-permute-done((bf16[4,512,256]{2,1,0:T(8,128)(2,1)}, bf16[4,512,256]{2,1,0:T(8,128)(2,1)}, u32[]{:S(2)}, u32[]{:S(2)}) %collective-permute-start.26) | collective-permute-done | bytes 1048608 | tf_op jit(solution)/shard_map/ppermute | solution.py:21
  211.3 1.0 collective-permute-done.25.refs_11_.refs_14_
  212.3 1.6 collective-permute-done.24.refs_10_.refs_13_
  214.0 1.0 copy-done.1
  214.9 6.7 %combine.1 = (bf16[512,1024]{1,0:T(8,128)(2,1)}, bf16[512,1024]{1,0:T(8,128)(2,1)}) custom-call(bf16[2,3,512,256]{3,2,1,0:T(8,128)(2,1)} %get-tuple-element.102.refs_0_, bf16[2,3,512,256]{3,2,1,0:T(8,128)(2,1)} %get-tuple-element.120.refs_1_, bf16[2,3,512,256]{3,2,1,0:T(8,128)(2,1)} %get-tuple-element.133.refs_2_, ...), custom_call_target="tpu_custom_call" | custom-call | flops 1 | bytes 1 | tf_op jit(solution)/shard_map/combine/pallas_call | solution.py:400
  222.4 1.3 collective-permute-start.28
  223.7 4.5 %collective-permute-start.27 = (bf16[1,1024]{1,0:T(2,128)(2,1)S(1)}, bf16[1,1024]{1,0:T(2,128)(2,1)S(1)}, u32[]{:S(2)}, u32[]{:S(2)}) collective-permute-start(bf16[1,1024]{1,0:T(2,128)(2,1)S(1)} %get-tuple-element.191), channel_id=1, source_target_pairs={{0,8},{8,16},{16,24},{1,9},{9,17},{17,25},{2,10},{10,18},{18,26},{... | collective-permute-start | bytes 6152 | tf_op jit(solution)/shard_map/ppermute | solution.py:37
  228.2 3.2 %finish.4 = (f32[6,16,64,256]{3,2,1,0:T(8,128)}, f32[6,16,64,256]{3,2,1,0:T(8,128)}) custom-call(bf16[1,6,4,64,256]{4,3,2,1,0:T(8,128)(2,1)} %get-tuple-element.163.a_kept, bf16[3,6,4,64,256]{4,3,2,1,0:T(8,128)(2,1)} %collective-permute-done.20.refs_3_.a_got, bf16[1,6,4,64,256]{4,3,2,1,0:T(8,128)(2,1)} %get-tuple-element.164.b_kept, ...), custom_call_target="tpu_custom_call" | custom-call | flops 1 | bytes 1 | tf_op jit(solution)/shard_map/finish/pallas_call | solution.py:360
  231.4 0.9 collective-permute-start.33
  232.3 1.5 collective-permute-start.34
  233.9 4.3 %pair_sums.3 = (bf16[1,6,4,64,256]{4,3,2,1,0:T(8,128)(2,1)}, bf16[1,6,4,64,256]{4,3,2,1,0:T(8,128)(2,1)}, bf16[1,6,4,64,256]{4,3,2,1,0:T(8,128)(2,1)}, bf16[1,6,4,64,256]{4,3,2,1,0:T(8,128)(2,1)}) custom-call(bf16[2,6,4,64,256]{4,3,2,1,0:T(8,128)(2,1)} %get-tuple-element.160.refs_0_, bf16[3,6,4,64,256]{4,3,2,1,0:T(8,128)(2,1)} %collective-permute-done.29.refs_1_.b_got, ...), custom_call_target="tpu_custom_call" | custom-call | flops 199999995904 | bytes 1 | tf_op jit(solution)/shard_map/pair_sums/pallas_call | solution.py:332
  238.1 2.0 collective-permute-start.31
  240.2 3.7 %convolution.3 = bf16[512,1024]{1,0:T(8,128)(2,1)} custom-call(bf16[512,1024]{1,0:T(8,128)(2,1)} %get-tuple-element.158.x_ref, bf16[1,1024]{1,0:T(2,128)(2,1)} %copy-done.9, bf16[1,1024]{1,0:T(2,128)(2,1)} %copy-done.8, f32[3,1024]{1,0:T(4,128)} %taps_ref.5), custom_call_target="tpu_custom_call" | custom-call | flops 1 | bytes 1 | tf_op jit(solution)/shard_map/convolution/pallas_call | solution.py:91
  243.9 3.2 %finish.5 = (f32[6,16,64,256]{3,2,1,0:T(8,128)}, f32[6,16,64,256]{3,2,1,0:T(8,128)}) custom-call(bf16[1,6,4,64,256]{4,3,2,1,0:T(8,128)(2,1)} %get-tuple-element.182.a_kept, bf16[3,6,4,64,256]{4,3,2,1,0:T(8,128)(2,1)} %collective-permute-done.30.refs_3_.a_got, ...), custom_call_target="tpu_custom_call", output_to_operand_aliasing={{0}: (4, {}), {1}: (5, {})} | custom-call | flops 1 | bytes 1 | tf_op jit(solution)/shard_map/finish/pallas_call | solution.py:360
  247.0 5.2 %collective-permute-done.33.a_got = bf16[1,6,4,64,256]{4,3,2,1,0:T(8,128)(2,1)} collective-permute-done((bf16[1,6,4,64,256]{4,3,2,1,0:T(8,128)(2,1)}, bf16[1,6,4,64,256]{4,3,2,1,0:T(8,128)(2,1)}, u32[]{:S(2)}, u32[]{:S(2)}) %collective-permute-start.33) | collective-permute-done | bytes 786464 | tf_op jit(solution)/shard_map/ppermute | solution.py:21
  253.1 3.2 %finish.6 = (f32[6,16,64,256]{3,2,1,0:T(8,128)}, f32[6,16,64,256]{3,2,1,0:T(8,128)}) custom-call(bf16[1,6,4,64,256]{4,3,2,1,0:T(8,128)(2,1)} %get-tuple-element.146.a_kept, bf16[1,6,4,64,256]{4,3,2,1,0:T(8,128)(2,1)} %collective-permute-done.33.a_got, ...), custom_call_target="tpu_custom_call", output_to_operand_aliasing={{0}: (4, {}), {1}: (5, {})} | custom-call | flops 1 | bytes 1 | tf_op jit(solution)/shard_map/finish/pallas_call | solution.py:360
  256.3 11.3 %collective-permute-done.31.a_got = bf16[1,6,4,64,256]{4,3,2,1,0:T(8,128)(2,1)S(1)} collective-permute-done((bf16[1,6,4,64,256]{4,3,2,1,0:T(8,128)(2,1)}, bf16[1,6,4,64,256]{4,3,2,1,0:T(8,128)(2,1)S(1)}, u32[]{:S(2)}, u32[]{:S(2)}) %collective-permute-start.31) | collective-permute-done | bytes 786464 | tf_op jit(solution)/shard_map/ppermute | solution.py:21
  269.3 3.2 %finish.7 = (f32[6,16,64,256]{3,2,1,0:T(8,128)}, f32[6,16,64,256]{3,2,1,0:T(8,128)}) custom-call(bf16[1,6,4,64,256]{4,3,2,1,0:T(8,128)(2,1)} %get-tuple-element.172.a_kept, bf16[1,6,4,64,256]{4,3,2,1,0:T(8,128)(2,1)} %copy-done.4, bf16[1,6,4,64,256]{4,3,2,1,0:T(8,128)(2,1)} %get-tuple-element.174.b_kept, ...), custom_call_target="tpu_custom_call", output_to_operand_aliasing={{0}: (4, {}), {1}: (5, {})} | custom-call | flops 1 | bytes 1 | tf_op jit(solution)/shard_map/finish/pallas_call | solution.py:360
  (80 shorter events, 13.0 us)
Async XLA Ops:
  0.6 20.4 %copy-start.10 = (s32[16,5]{0,1:T(8,128)S(1)}, s32[16,5]{0,1:T(8,128)}, u32[]{:S(2)}) copy-start(s32[16,5]{0,1:T(8,128)} %param.10) | copy-start | bytes 964
  0.6 12.9 %collective-permute-start = (bf16[512,1024]{1,0:T(8,128)(2,1)}, bf16[512,1024]{1,0:T(8,128)(2,1)S(1)}, u32[]{:S(2)}, u32[]{:S(2)}) collective-permute-start(bf16[512,1024]{1,0:T(8,128)(2,1)} %refs_2_.7), channel_id=1, source_target_pairs={{0,1},{1,0},{2,3},{3,2},{4,5},{5,4},{6,7},{7,6},{8,9},{9,8},{10,11... | collective-permute-start | bytes 3145736 | tf_op jit(solution)/shard_map/ppermute | solution.py:21
  2.9 23.3 %collective-permute-start.2 = (bf16[528,256]{1,0:T(8,128)(2,1)S(1)}, bf16[528,256]{1,0:T(8,128)(2,1)S(1)}, u32[]{:S(2)}, u32[]{:S(2)}) collective-permute-start(bf16[528,256]{1,0:T(8,128)(2,1)S(1)} %pad_maximum_fusion), channel_id=1, source_target_pairs={{0,4},{1,5},{2,6},{3,7},{4,0},{5,1},{6,2},{7,3},{8,12},{9,13},{10,... | collective-permute-start | bytes 811016 | tf_op jit(solution)/shard_map/ppermute | solution.py:21
  6.5 27.3 %collective-permute-start.1 = (bf16[528,256]{1,0:T(8,128)(2,1)S(1)}, bf16[528,256]{1,0:T(8,128)(2,1)S(1)}, u32[]{:S(2)}, u32[]{:S(2)}) collective-permute-start(bf16[528,256]{1,0:T(8,128)(2,1)S(1)} %pad_maximum_fusion), channel_id=1, source_target_pairs={{0,2},{1,3},{2,0},{3,1},{4,6},{5,7},{6,4},{7,5},{8,10},{9,11},{10,... | collective-permute-start | bytes 811016 | tf_op jit(solution)/shard_map/ppermute | solution.py:21
  8.8 4.7 %collective-permute-start.3 = (bf16[1,1024]{1,0:T(2,128)(2,1)S(1)}, bf16[1,1024]{1,0:T(2,128)(2,1)S(1)}, u32[]{:S(2)}, u32[]{:S(2)}) collective-permute-start(bf16[1,1024]{1,0:T(2,128)(2,1)S(1)} %get-tuple-element.193), channel_id=1, source_target_pairs={{0,8},{8,16},{16,24},{1,9},{9,17},{17,25},{2,10},{10,18},{18,26},{... | collective-permute-start | bytes 6152 | tf_op jit(solution)/shard_map/ppermute | solution.py:37
  12.2 5.5 %collective-permute-start.4 = (bf16[1,1024]{1,0:T(2,128)(2,1)S(1)}, bf16[1,1024]{1,0:T(2,128)(2,1)S(1)}, u32[]{:S(2)}, u32[]{:S(2)}) collective-permute-start(bf16[1,1024]{1,0:T(2,128)(2,1)S(1)} %get-tuple-element.192), channel_id=1, source_target_pairs={{8,0},{16,8},{24,16},{9,1},{17,9},{25,17},{10,2},{18,10},{26,18},{... | collective-permute-start | bytes 6152 | tf_op jit(solution)/shard_map/ppermute | solution.py:38
  13.6 4.2 %copy-start.6 = (bf16[1,1024]{1,0:T(2,128)(2,1)}, bf16[1,1024]{1,0:T(2,128)(2,1)S(1)}, u32[]{:S(2)}) copy-start(bf16[1,1024]{1,0:T(2,128)(2,1)S(1)} %collective-permute-done.3.before_ref) | copy-start | bytes 6148
  13.6 21.5 %copy-start.11 = (bf16[512,1024]{1,0:T(8,128)(2,1)}, bf16[512,1024]{1,0:T(8,128)(2,1)S(1)}, u32[]{:S(2)}) copy-start(bf16[512,1024]{1,0:T(8,128)(2,1)S(1)} %collective-permute-done.refs_3_) | copy-start | bytes 3145732
  20.2 13.6 %collective-permute-start.7 = (bf16[512,256]{1,0:T(8,128)(2,1)}, bf16[512,256]{1,0:T(8,128)(2,1)S(1)}, u32[]{:S(2)}, u32[]{:S(2)}) collective-permute-start(bf16[512,256]{1,0:T(8,128)(2,1)} %convolution.2), channel_id=1, source_target_pairs={{0,4},{1,5},{2,6},{3,7},{4,0},{5,1},{6,2},{7,3},{8,12},{9,13},{10,... | collective-permute-start | bytes 786440 | tf_op jit(solution)/shard_map/ppermute | solution.py:21
  20.5 13.3 %collective-permute-start.6 = (bf16[512,256]{1,0:T(8,128)(2,1)}, bf16[512,256]{1,0:T(8,128)(2,1)S(1)}, u32[]{:S(2)}, u32[]{:S(2)}) collective-permute-start(bf16[512,256]{1,0:T(8,128)(2,1)} %convolution.2), channel_id=1, source_target_pairs={{0,2},{1,3},{2,0},{3,1},{4,6},{5,7},{6,4},{7,5},{8,10},{9,11},{10,... | collective-permute-start | bytes 786440 | tf_op jit(solution)/shard_map/ppermute | solution.py:21
  21.0 14.1 %collective-permute-start.5 = (bf16[512,256]{1,0:T(8,128)(2,1)}, bf16[512,256]{1,0:T(8,128)(2,1)S(1)}, u32[]{:S(2)}, u32[]{:S(2)}) collective-permute-start(bf16[512,256]{1,0:T(8,128)(2,1)} %convolution.2), channel_id=1, source_target_pairs={{0,1},{1,0},{2,3},{3,2},{4,5},{5,4},{6,7},{7,6},{8,9},{9,8},{10,11... | collective-permute-start | bytes 786440 | tf_op jit(solution)/shard_map/ppermute | solution.py:21
  26.2 8.9 %copy-start.12 = (bf16[528,256]{1,0:T(8,128)(2,1)}, bf16[528,256]{1,0:T(8,128)(2,1)S(1)}, u32[]{:S(2)}) copy-start(bf16[528,256]{1,0:T(8,128)(2,1)S(1)} %collective-permute-done.2.refs_5_) | copy-start | bytes 811012
  26.2 40.0 %collective-permute-start.10 = (bf16[512,1024]{1,0:T(8,128)(2,1)}, bf16[512,1024]{1,0:T(8,128)(2,1)}, u32[]{:S(2)}, u32[]{:S(2)}) collective-permute-start(bf16[512,1024]{1,0:T(8,128)(2,1)} %get-tuple-element.99.refs_6_.refs_7_.refs_8_), channel_id=1, source_target_pairs={{0,1},{1,0},{2,3},{3,2},{4,5},{5,4},{6,7},{7,6},{8,9},{9,8},{10,11... | collective-permute-start | bytes 3145736 | tf_op jit(solution)/shard_map/ppermute | solution.py:21
  33.8 1.3 copy-start.14
  33.8 1.3 copy-start.13
  33.8 1.3 copy-start.15
  33.8 29.1 %collective-permute-start.8 = (bf16[2,512,256]{2,1,0:T(8,128)(2,1)}, bf16[2,512,256]{2,1,0:T(8,128)(2,1)}, u32[]{:S(2)}, u32[]{:S(2)}) collective-permute-start(bf16[2,512,256]{2,1,0:T(8,128)(2,1)} %get-tuple-element.105), channel_id=1, source_target_pairs={{0,2},{1,3},{2,0},{3,1},{4,6},{5,7},{6,4},{7,5},{8,10},{9,11},{10,... | collective-permute-start | bytes 1572872 | tf_op jit(solution)/shard_map/ppermute | solution.py:21
  33.9 29.1 %collective-permute-start.9 = (bf16[2,512,256]{2,1,0:T(8,128)(2,1)}, bf16[2,512,256]{2,1,0:T(8,128)(2,1)}, u32[]{:S(2)}, u32[]{:S(2)}) collective-permute-start(bf16[2,512,256]{2,1,0:T(8,128)(2,1)} %get-tuple-element.105), channel_id=1, source_target_pairs={{0,4},{1,5},{2,6},{3,7},{4,0},{5,1},{6,2},{7,3},{8,12},{9,13},{10,... | collective-permute-start | bytes 1572872 | tf_op jit(solution)/shard_map/ppermute | solution.py:21
  49.9 41.8 %collective-permute-start.13 = (bf16[2,6,4,64,256]{4,3,2,1,0:T(8,128)(2,1)}, bf16[2,6,4,64,256]{4,3,2,1,0:T(8,128)(2,1)}, u32[]{:S(2)}, u32[]{:S(2)}) collective-permute-start(bf16[2,6,4,64,256]{4,3,2,1,0:T(8,128)(2,1)} %get-tuple-element.111), channel_id=1, source_target_pairs={{0,8},{8,0},{16,24},{24,16},{1,9},{9,1},{17,25},{25,17},{2,10},{10... | collective-permute-start | bytes 4718600 | tf_op jit(solution)/shard_map/ppermute | solution.py:21
  52.3 39.5 %collective-permute-start.14 = (bf16[2,6,4,64,256]{4,3,2,1,0:T(8,128)(2,1)}, bf16[2,6,4,64,256]{4,3,2,1,0:T(8,128)(2,1)}, u32[]{:S(2)}, u32[]{:S(2)}) collective-permute-start(bf16[2,6,4,64,256]{4,3,2,1,0:T(8,128)(2,1)} %get-tuple-element.113), channel_id=1, source_target_pairs={{0,16},{8,24},{16,0},{24,8},{1,17},{9,25},{17,1},{25,9},{2,18},{10... | collective-permute-start | bytes 4718600 | tf_op jit(solution)/shard_map/ppermute | solution.py:21
  63.0 25.8 %collective-permute-start.11 = (bf16[2,512,256]{2,1,0:T(8,128)(2,1)}, bf16[2,512,256]{2,1,0:T(8,128)(2,1)}, u32[]{:S(2)}, u32[]{:S(2)}) collective-permute-start(bf16[2,512,256]{2,1,0:T(8,128)(2,1)} %get-tuple-element.109), channel_id=1, source_target_pairs={{0,2},{1,3},{2,0},{3,1},{4,6},{5,7},{6,4},{7,5},{8,10},{9,11},{10,... | collective-permute-start | bytes 1572872 | tf_op jit(solution)/shard_map/ppermute | solution.py:21
  63.7 25.0 %collective-permute-start.12 = (bf16[2,512,256]{2,1,0:T(8,128)(2,1)}, bf16[2,512,256]{2,1,0:T(8,128)(2,1)}, u32[]{:S(2)}, u32[]{:S(2)}) collective-permute-start(bf16[2,512,256]{2,1,0:T(8,128)(2,1)} %get-tuple-element.109), channel_id=1, source_target_pairs={{0,4},{1,5},{2,6},{3,7},{4,0},{5,1},{6,2},{7,3},{8,12},{9,13},{10,... | collective-permute-start | bytes 1572872 | tf_op jit(solution)/shard_map/ppermute | solution.py:21
  88.8 31.3 %collective-permute-start.15 = (bf16[2,512,256]{2,1,0:T(8,128)(2,1)}, bf16[2,512,256]{2,1,0:T(8,128)(2,1)}, u32[]{:S(2)}, u32[]{:S(2)}) collective-permute-start(bf16[2,512,256]{2,1,0:T(8,128)(2,1)} %get-tuple-element.123), channel_id=1, source_target_pairs={{0,2},{1,3},{2,0},{3,1},{4,6},{5,7},{6,4},{7,5},{8,10},{9,11},{10,... | collective-permute-start | bytes 1572872 | tf_op jit(solution)/shard_map/ppermute | solution.py:21
  89.1 30.9 %collective-permute-start.16 = (bf16[2,512,256]{2,1,0:T(8,128)(2,1)}, bf16[2,512,256]{2,1,0:T(8,128)(2,1)}, u32[]{:S(2)}, u32[]{:S(2)}) collective-permute-start(bf16[2,512,256]{2,1,0:T(8,128)(2,1)} %get-tuple-element.123), channel_id=1, source_target_pairs={{0,4},{1,5},{2,6},{3,7},{4,0},{5,1},{6,2},{7,3},{8,12},{9,13},{10,... | collective-permute-start | bytes 1572872 | tf_op jit(solution)/shard_map/ppermute | solution.py:21
  91.8 33.3 %collective-permute-start.18 = (bf16[2,6,4,64,256]{4,3,2,1,0:T(8,128)(2,1)}, bf16[2,6,4,64,256]{4,3,2,1,0:T(8,128)(2,1)}, u32[]{:S(2)}, u32[]{:S(2)}) collective-permute-start(bf16[2,6,4,64,256]{4,3,2,1,0:T(8,128)(2,1)} %get-tuple-element.129), channel_id=1, source_target_pairs={{0,16},{8,24},{16,0},{24,8},{1,17},{9,25},{17,1},{25,9},{2,18},{10... | collective-permute-start | bytes 4718600 | tf_op jit(solution)/shard_map/ppermute | solution.py:21
  93.5 34.6 %collective-permute-start.17 = (bf16[2,6,4,64,256]{4,3,2,1,0:T(8,128)(2,1)}, bf16[2,6,4,64,256]{4,3,2,1,0:T(8,128)(2,1)}, u32[]{:S(2)}, u32[]{:S(2)}) collective-permute-start(bf16[2,6,4,64,256]{4,3,2,1,0:T(8,128)(2,1)} %get-tuple-element.126), channel_id=1, source_target_pairs={{0,8},{8,0},{16,24},{24,16},{1,9},{9,1},{17,25},{25,17},{2,10},{10... | collective-permute-start | bytes 4718600 | tf_op jit(solution)/shard_map/ppermute | solution.py:21
  120.0 46.1 %collective-permute-start.23 = (bf16[4,512,256]{2,1,0:T(8,128)(2,1)}, bf16[4,512,256]{2,1,0:T(8,128)(2,1)}, u32[]{:S(2)}, u32[]{:S(2)}) collective-permute-start(bf16[4,512,256]{2,1,0:T(8,128)(2,1)} %get-tuple-element.151), channel_id=1, source_target_pairs={{0,4},{1,5},{2,6},{3,7},{4,0},{5,1},{6,2},{7,3},{8,12},{9,13},{10,... | collective-permute-start | bytes 3145736 | tf_op jit(solution)/shard_map/ppermute | solution.py:21
  120.4 45.7 %collective-permute-start.22 = (bf16[4,512,256]{2,1,0:T(8,128)(2,1)}, bf16[4,512,256]{2,1,0:T(8,128)(2,1)}, u32[]{:S(2)}, u32[]{:S(2)}) collective-permute-start(bf16[4,512,256]{2,1,0:T(8,128)(2,1)} %get-tuple-element.149), channel_id=1, source_target_pairs={{0,2},{1,3},{2,0},{3,1},{4,6},{5,7},{6,4},{7,5},{8,10},{9,11},{10,... | collective-permute-start | bytes 3145736 | tf_op jit(solution)/shard_map/ppermute | solution.py:21
  128.1 51.1 %collective-permute-start.19 = (bf16[3,6,4,64,256]{4,3,2,1,0:T(8,128)(2,1)}, bf16[3,6,4,64,256]{4,3,2,1,0:T(8,128)(2,1)}, u32[]{:S(2)}, u32[]{:S(2)}) collective-permute-start(bf16[3,6,4,64,256]{4,3,2,1,0:T(8,128)(2,1)} %get-tuple-element.142), channel_id=1, source_target_pairs={{0,8},{8,0},{16,24},{24,16},{1,9},{9,1},{17,25},{25,17},{2,10},{10... | collective-permute-start | bytes 7077896 | tf_op jit(solution)/shard_map/ppermute | solution.py:21
  128.4 50.8 %collective-permute-start.20 = (bf16[3,6,4,64,256]{4,3,2,1,0:T(8,128)(2,1)}, bf16[3,6,4,64,256]{4,3,2,1,0:T(8,128)(2,1)}, u32[]{:S(2)}, u32[]{:S(2)}) collective-permute-start(bf16[3,6,4,64,256]{4,3,2,1,0:T(8,128)(2,1)} %get-tuple-element.145), channel_id=1, source_target_pairs={{0,16},{8,24},{16,0},{24,8},{1,17},{9,25},{17,1},{25,9},{2,18},{10... | collective-permute-start | bytes 7077896 | tf_op jit(solution)/shard_map/ppermute | solution.py:21
  166.1 45.1 %collective-permute-start.26 = (bf16[4,512,256]{2,1,0:T(8,128)(2,1)}, bf16[4,512,256]{2,1,0:T(8,128)(2,1)}, u32[]{:S(2)}, u32[]{:S(2)}) collective-permute-start(bf16[4,512,256]{2,1,0:T(8,128)(2,1)} %get-tuple-element.157), channel_id=1, source_target_pairs={{0,4},{1,5},{2,6},{3,7},{4,0},{5,1},{6,2},{7,3},{8,12},{9,13},{10,... | collective-permute-start | bytes 3145736 | tf_op jit(solution)/shard_map/ppermute | solution.py:21
  166.5 45.8 %collective-permute-start.25 = (bf16[4,512,256]{2,1,0:T(8,128)(2,1)}, bf16[4,512,256]{2,1,0:T(8,128)(2,1)}, u32[]{:S(2)}, u32[]{:S(2)}) collective-permute-start(bf16[4,512,256]{2,1,0:T(8,128)(2,1)} %get-tuple-element.155), channel_id=1, source_target_pairs={{0,2},{1,3},{2,0},{3,1},{4,6},{5,7},{6,4},{7,5},{8,10},{9,11},{10,... | collective-permute-start | bytes 3145736 | tf_op jit(solution)/shard_map/ppermute | solution.py:21
  179.2 52.2 %collective-permute-start.30 = (bf16[3,6,4,64,256]{4,3,2,1,0:T(8,128)(2,1)}, bf16[3,6,4,64,256]{4,3,2,1,0:T(8,128)(2,1)}, u32[]{:S(2)}, u32[]{:S(2)}) collective-permute-start(bf16[3,6,4,64,256]{4,3,2,1,0:T(8,128)(2,1)} %get-tuple-element.170), channel_id=1, source_target_pairs={{0,16},{8,24},{16,0},{24,8},{1,17},{9,25},{17,1},{25,9},{2,18},{10... | collective-permute-start | bytes 7077896 | tf_op jit(solution)/shard_map/ppermute | solution.py:21
  179.5 52.8 %collective-permute-start.29 = (bf16[3,6,4,64,256]{4,3,2,1,0:T(8,128)(2,1)}, bf16[3,6,4,64,256]{4,3,2,1,0:T(8,128)(2,1)}, u32[]{:S(2)}, u32[]{:S(2)}) collective-permute-start(bf16[3,6,4,64,256]{4,3,2,1,0:T(8,128)(2,1)} %get-tuple-element.162), channel_id=1, source_target_pairs={{0,8},{8,0},{16,24},{24,16},{1,9},{9,1},{17,25},{25,17},{2,10},{10... | collective-permute-start | bytes 7077896 | tf_op jit(solution)/shard_map/ppermute | solution.py:21
  180.3 4.4 %copy-start.2 = (bf16[4,512,256]{2,1,0:T(8,128)(2,1)S(1)}, bf16[4,512,256]{2,1,0:T(8,128)(2,1)}, u32[]{:S(2)}) copy-start(bf16[4,512,256]{2,1,0:T(8,128)(2,1)} %get-tuple-element.147) | copy-start | bytes 3145732
  180.3 31.0 %copy-start.3 = (bf16[4,512,256]{2,1,0:T(8,128)(2,1)S(1)}, bf16[4,512,256]{2,1,0:T(8,128)(2,1)}, u32[]{:S(2)}) copy-start(bf16[4,512,256]{2,1,0:T(8,128)(2,1)} %get-tuple-element.153) | copy-start | bytes 3145732
  184.7 27.6 %collective-permute-start.21 = (bf16[4,512,256]{2,1,0:T(8,128)(2,1)S(1)}, bf16[4,512,256]{2,1,0:T(8,128)(2,1)S(1)}, u32[]{:S(2)}, u32[]{:S(2)}) collective-permute-start(bf16[4,512,256]{2,1,0:T(8,128)(2,1)S(1)} %copy-done.2), channel_id=1, source_target_pairs={{0,1},{1,0},{2,3},{3,2},{4,5},{5,4},{6,7},{7,6},{8,9},{9,8},{10,11... | collective-permute-start | bytes 3145736 | tf_op jit(solution)/shard_map/ppermute | solution.py:21
  211.3 2.7 collective-permute-start.24
  212.3 1.7 copy-start
  214.0 1.0 copy-start.1
  222.4 11.5 %collective-permute-start.28 = (bf16[1,1024]{1,0:T(2,128)(2,1)S(1)}, bf16[1,1024]{1,0:T(2,128)(2,1)S(1)}, u32[]{:S(2)}, u32[]{:S(2)}) collective-permute-start(bf16[1,1024]{1,0:T(2,128)(2,1)S(1)} %get-tuple-element.190), channel_id=1, source_target_pairs={{8,0},{16,8},{24,16},{9,1},{17,9},{25,17},{10,2},{18,10},{26,18},{... | collective-permute-start | bytes 6152 | tf_op jit(solution)/shard_map/ppermute | solution.py:38
  223.7 10.2 %collective-permute-start.27 = (bf16[1,1024]{1,0:T(2,128)(2,1)S(1)}, bf16[1,1024]{1,0:T(2,128)(2,1)S(1)}, u32[]{:S(2)}, u32[]{:S(2)}) collective-permute-start(bf16[1,1024]{1,0:T(2,128)(2,1)S(1)} %get-tuple-element.191), channel_id=1, source_target_pairs={{0,8},{8,16},{16,24},{1,9},{9,17},{17,25},{2,10},{10,18},{18,26},{... | collective-permute-start | bytes 6152 | tf_op jit(solution)/shard_map/ppermute | solution.py:37
  231.4 20.8 %collective-permute-start.33 = (bf16[1,6,4,64,256]{4,3,2,1,0:T(8,128)(2,1)}, bf16[1,6,4,64,256]{4,3,2,1,0:T(8,128)(2,1)}, u32[]{:S(2)}, u32[]{:S(2)}) collective-permute-start(bf16[1,6,4,64,256]{4,3,2,1,0:T(8,128)(2,1)} %get-tuple-element.177), channel_id=1, source_target_pairs={{0,16},{8,24},{16,0},{24,8},{1,17},{9,25},{17,1},{25,9},{2,18},{10... | collective-permute-start | bytes 2359304 | tf_op jit(solution)/shard_map/ppermute | solution.py:21
  232.3 20.8 %collective-permute-start.34 = (bf16[1,6,4,64,256]{4,3,2,1,0:T(8,128)(2,1)}, bf16[1,6,4,64,256]{4,3,2,1,0:T(8,128)(2,1)}, u32[]{:S(2)}, u32[]{:S(2)}) collective-permute-start(bf16[1,6,4,64,256]{4,3,2,1,0:T(8,128)(2,1)} %get-tuple-element.181), channel_id=1, source_target_pairs={{0,8},{8,0},{16,24},{24,16},{1,9},{9,1},{17,25},{25,17},{2,10},{10... | collective-permute-start | bytes 2359304 | tf_op jit(solution)/shard_map/ppermute | solution.py:21
  233.8 4.3 %copy-start.8 = (bf16[1,1024]{1,0:T(2,128)(2,1)}, bf16[1,1024]{1,0:T(2,128)(2,1)S(1)}, u32[]{:S(2)}) copy-start(bf16[1,1024]{1,0:T(2,128)(2,1)S(1)} %collective-permute-done.28.behind_ref) | copy-start | bytes 6148
  233.9 4.3 %copy-start.9 = (bf16[1,1024]{1,0:T(2,128)(2,1)}, bf16[1,1024]{1,0:T(2,128)(2,1)S(1)}, u32[]{:S(2)}) copy-start(bf16[1,1024]{1,0:T(2,128)(2,1)S(1)} %collective-permute-done.27.before_ref) | copy-start | bytes 6148
  238.1 29.4 %collective-permute-start.31 = (bf16[1,6,4,64,256]{4,3,2,1,0:T(8,128)(2,1)}, bf16[1,6,4,64,256]{4,3,2,1,0:T(8,128)(2,1)S(1)}, u32[]{:S(2)}, u32[]{:S(2)}) collective-permute-start(bf16[1,6,4,64,256]{4,3,2,1,0:T(8,128)(2,1)} %get-tuple-element.173), channel_id=1, source_target_pairs={{0,16},{8,24},{16,0},{24,8},{1,17},{9,25},{17,1},{25,9},{2,18},{10... | collective-permute-start | bytes 2359304 | tf_op jit(solution)/shard_map/ppermute | solution.py:21
  240.1 28.3 %collective-permute-start.32 = (bf16[1,6,4,64,256]{4,3,2,1,0:T(8,128)(2,1)}, bf16[1,6,4,64,256]{4,3,2,1,0:T(8,128)(2,1)S(1)}, u32[]{:S(2)}, u32[]{:S(2)}) collective-permute-start(bf16[1,6,4,64,256]{4,3,2,1,0:T(8,128)(2,1)} %get-tuple-element.175), channel_id=1, source_target_pairs={{0,8},{8,0},{16,24},{24,16},{1,9},{9,1},{17,25},{25,17},{2,10},{10... | collective-permute-start | bytes 2359304 | tf_op jit(solution)/shard_map/ppermute | solution.py:21
  (4 other events, 3.1 us)

commit v3 on v2

--- a/solution.py
+++ b/solution.py
@@ -310,7 +310,7 @@
         ),
         input_output_aliases={6 + i: 1 + i for i in range(len(extra))},
         compiler_params=pltpu.CompilerParams(vmem_limit_bytes=VMEM_LIMIT),
-        cost_estimate=cost(LONG if block == 0 else 1),
+        cost_estimate=cost(),
         name="term_sums",
     )(level_bits, pattern, hidden, grad, up_factors, down_factors, *extra)
     return outs[0], outs[1:]
@@ -368,6 +368,20 @@
         cost_estimate=cost(),
         name="finish",
     )(a_kept, a_got, b_kept, b_got, *extra)
+
+
+def pause_kernel(_, out_ref):
+    out_ref[...] = jnp.zeros(out_ref.shape, f32)
+
+
+def pause(behind):
+    return pl.pallas_call(
+        pause_kernel,
+        out_shape=jax.ShapeDtypeStruct((8, 128), f32),
+        in_specs=[ANY],
+        cost_estimate=cost(LONG),
+        name="pause",
+    )(behind)
 
 
 def combine_kernel(*refs, blocks_dev, remote_bits, local_bits):
@@ -428,7 +442,7 @@
         got = {bit: swapped(pieces[bit], "tensor", bit) for bit in reversed(bits)}
         return [got[bit] for bit in bits]
 
-    first = jnp.concatenate([frames[:, :width], frames[:16, :width]])
+    first = lax.pad(frames[:, :width], jnp.zeros((), frames.dtype), ((0, 16, 0), (0, 0, 0)))
     x_first = fetch({bit: first for bit in far}, far)
     x_near = swapped(frames, "tensor", 0)
     before, behind = halo(cotangent)
@@ -491,13 +505,11 @@
         x_got[j] = swapped(up_sent, "seq", 0)
         y_got[j] = swapped(down_sent, "seq", stages - 1)
         made.append((hidden, grad_pre))
-        if j == 0:
-            give_terms(0)
         if j + 2 < blocks_dev:
-            fetch_block(j + 2, homes[0] if j == 0 else hidden)
-        if j >= 2:
+            fetch_block(j + 2, pause(hidden) if j == 0 else hidden)
+        if j >= 1:
             give_terms(j - 1, hidden)
-        if 0 < j == blocks_dev - 1:
+        if j == blocks_dev - 1:
             give_terms(j)
 
     def combined(*others):
@@ -516,10 +528,11 @@
         for j in range(max(blocks_dev - 2, 0), blocks_dev):
             got = [x_got[j], y_got[j]]
             if j == blocks_dev - 1:
-                mixed, grad_frames, before, behind = combined(*([sums[j - 1][0]] if j else []))
                 for done in range(blocks_dev - 3):
                     outs = finish(*end(done), outs, done * ratio, hidden_dev)
-                got = [after(value, before, behind, *(outs or [])) for value in got]
+                homes[0] = after(homes[0], *(outs or []))
+                mixed, grad_frames, before, behind = combined(*([sums[j - 1][0]] if j else []))
+                got = [after(value, before, behind) for value in got]
             (up_last, up_next), (down_last, down_next) = pair_sums([(sums[j][0], got[0]), (sums[j][1], got[1])], (0, 0))
             if j + 1 < blocks_dev:
                 down_next, up_next = after(down_next, x_got[j + 1]), after(up_next, y_got[j + 1])

time: 274 us -> 271 us (0.989)
  transfers between devices with their start and end apart: 35 -> 35, of which waited for: 13 -> 12; matrix products, arithmetic and copies ran while one was open for 1% -> 1% of each run, Pallas kernels for 50% -> 50%
where the time goes in v3:
time: 271 us; the launch traced here: 270 us
  Pallas kernels  139 us (51%)
  waiting for transfers between devices  82.1 us (30%)
  starting transfers between devices  40.8 us (15%)
  local copies, waits for them, and re-layouts  6.89 us (3%)
    ppermute x31, waiting for transfers between devices, swapped(): lax.ppermute(array, axis, [(i, i ^ 1 << bit) for i in range(lax.axis_size...  77.9 us
    pallas_call x4, Pallas kernels, layer(): pl.pallas_call(functools.partial(layer_kernel, block=block, ratio=ratio,...  60.6 us
    pallas_call x4, Pallas kernels, term_sums(): pl.pallas_call(functools.partial(terms_kernel, block=block, ratio=ratio,...  40.8 us
    ppermute x31, starting transfers between devices, swapped(): lax.ppermute(array, axis, [(i, i ^ 1 << bit) for i in range(lax.axis_size...  29.7 us
    pallas_call x4, Pallas kernels, finish(): pl.pallas_call(finish_kernel, out_shape=[shape, shape], grid=(step,), in_...  12.7 us
    pallas_call x2, Pallas kernels, pair_sums(): pl.pallas_call(functools.partial(pair_kernel, bits=bits), out_shape=[half...  8.69 us
    ppermute x2, starting transfers between devices, halo(): before = lax.ppermute(lax.slice_in_dim(array, rows - 1, rows), 'seq', up)  8.54 us
    pallas_call x1, Pallas kernels, combine(): pl.pallas_call(functools.partial(combine_kernel, remote_bits=remote_bits,...  6.68 us
  transfers between devices with their start and end apart: 35, of which 12 were waited for; matrix products, arithmetic and copies ran while one was open for 1% of the time, Pallas kernels for 50%

profile of v3, /device:TPU:0, one launch (start us, length us, event | category | flops | bytes accessed | tf_op | source)
XLA Modules:
  0.0 270.2 jit_solution(7013869990793112165)
XLA Ops:
  1.2 1.0 slice.15
  2.2 3.7 %collective-permute-start.2 = (bf16[528,256]{1,0:T(8,128)(2,1)S(1)}, bf16[528,256]{1,0:T(8,128)(2,1)S(1)}, u32[]{:S(2)}, u32[]{:S(2)}) collective-permute-start(bf16[528,256]{1,0:T(8,128)(2,1)S(1)} %pad.3), channel_id=1, source_target_pairs={{0,4},{1,5},{2,6},{3,7},{4,0},{5,1},{6,2},{7,3},{8,12},{9,13},{10,... | collective-permute-start | bytes 811016 | tf_op jit(solution)/shard_map/ppermute | solution.py:21
  5.8 1.6 collective-permute-start.1
  7.4 0.7 fusion.1
  8.1 3.4 %collective-permute-start.3 = (bf16[1,1024]{1,0:T(2,128)(2,1)S(1)}, bf16[1,1024]{1,0:T(2,128)(2,1)S(1)}, u32[]{:S(2)}, u32[]{:S(2)}) collective-permute-start(bf16[1,1024]{1,0:T(2,128)(2,1)S(1)} %get-tuple-element.197), channel_id=1, source_target_pairs={{0,8},{8,16},{16,24},{1,9},{9,17},{17,25},{2,10},{10,18},{18,26},{... | collective-permute-start | bytes 6152 | tf_op jit(solution)/shard_map/ppermute | solution.py:37
  11.6 1.3 collective-permute-start.4
  12.9 4.2 %collective-permute-done.4.behind_ref = bf16[1,1024]{1,0:T(2,128)(2,1)S(1)} collective-permute-done((bf16[1,1024]{1,0:T(2,128)(2,1)S(1)}, bf16[1,1024]{1,0:T(2,128)(2,1)S(1)}, u32[]{:S(2)}, u32[]{:S(2)}) %collective-permute-start.4) | collective-permute-done | bytes 2080 | tf_op jit(solution)/shard_map/ppermute | solution.py:38
  17.6 1.9 convolution.2
  21.0 4.5 %prepare.1 = (bf16[512,1024]{1,0:T(8,128)(2,1)}, bf16[2,512,256]{2,1,0:T(8,128)(2,1)}, bf16[2,512,256]{2,1,0:T(8,128)(2,1)}, bf16[2,512,256]{2,1,0:T(8,128)(2,1)}) custom-call(bf16[512,1024]{1,0:T(8,128)(2,1)} %refs_2_.7, bf16[512,1024]{1,0:T(8,128)(2,1)} %cot_ref.1, bf16[1,1024]{1,0:T(2,128)(2,1)} %copy-done.6, bf16[1,1024]{1,0:T(2,128)(2,1)} %copy-done.7, ...), custom_call_target="tpu_custom_call" | custom-call | flops 1 | bytes 1 | tf_op jit(solution)/shard_map/prepare/pallas_call | solution.py:70
  26.0 7.1 %collective-permute-done.7.refs_11_ = bf16[512,256]{1,0:T(8,128)(2,1)S(1)} collective-permute-done((bf16[512,256]{1,0:T(8,128)(2,1)}, bf16[512,256]{1,0:T(8,128)(2,1)S(1)}, u32[]{:S(2)}, u32[]{:S(2)}) %collective-permute-start.7) | collective-permute-done | bytes 262176 | tf_op jit(solution)/shard_map/ppermute | solution.py:21
  33.2 1.1 collective-permute-start.9
  35.1 14.2 %layer.4 = (bf16[2,6,4,64,256]{4,3,2,1,0:T(8,128)(2,1)}, bf16[2,6,4,64,256]{4,3,2,1,0:T(8,128)(2,1)}, bf16[2,6,4,64,256]{4,3,2,1,0:T(8,128)(2,1)}, bf16[2,6,4,64...) custom-call(s32[5]{0:T(128)} %level_bits.15, s32[16,5]{1,0:T(8,128)} %copy.25.pattern, ...), custom_call_target="tpu_custom_call" | custom-call | flops 199999995904 | bytes 1 | tf_op jit(solution)/shard_map/layer/pallas_call | solution.py:223
  49.3 2.4 collective-permute-start.13
  52.1 7.5 %collective-permute-done.9.refs_5_.refs_11_ = bf16[2,512,256]{2,1,0:T(8,128)(2,1)} collective-permute-done((bf16[2,512,256]{2,1,0:T(8,128)(2,1)}, bf16[2,512,256]{2,1,0:T(8,128)(2,1)}, u32[]{:S(2)}, u32[]{:S(2)}) %collective-permute-start.9) | collective-permute-done | bytes 524320 | tf_op jit(solution)/shard_map/ppermute | solution.py:21
  59.6 2.0 collective-permute-start.12
  61.6 14.2 %layer.5 = (bf16[2,6,4,64,256]{4,3,2,1,0:T(8,128)(2,1)}, bf16[2,6,4,64,256]{4,3,2,1,0:T(8,128)(2,1)}, bf16[2,6,4,64,256]{4,3,2,1,0:T(8,128)(2,1)}, bf16[2,6,4,64...) custom-call(s32[5]{0:T(128)} %level_bits.15, s32[16,5]{1,0:T(8,128)} %copy.25.pattern, ...), custom_call_target="tpu_custom_call" | custom-call | flops 199999995904 | bytes 1 | tf_op jit(solution)/shard_map/layer/pallas_call | solution.py:223
  75.8 10.2 %term_sums.4 = (bf16[2,3,512,256]{3,2,1,0:T(8,128)(2,1)}, bf16[4,512,256]{2,1,0:T(8,128)(2,1)}, bf16[4,512,256]{2,1,0:T(8,128)(2,1)}, bf16[4,512,256]{2,1,0:T(8,128)(2,1)}) custom-call(s32[5]{0:T(128)} %level_bits.15, s32[16,5]{1,0:T(8,128)} %copy.25.pattern, bf16[512,1024]{1,0:T(8,128)(2,1)} %get-tuple-element.107.hidden_ref, ...), custom_call_target="tpu_custom_call" | custom-call | flops 1 | bytes 1 | tf_op jit(solution)/shard_map/term_sums/pallas_call | solution.py:298
  86.3 2.7 collective-permute-start.20
  89.0 2.1 collective-permute-start.17
  91.1 16.0 %layer.6 = (bf16[3,6,4,64,256]{4,3,2,1,0:T(8,128)(2,1)}, bf16[2,6,4,64,256]{4,3,2,1,0:T(8,128)(2,1)}, bf16[3,6,4,64,256]{4,3,2,1,0:T(8,128)(2,1)}, bf16[2,6,4,64...) custom-call(s32[5]{0:T(128)} %level_bits.15, ...), custom_call_target="tpu_custom_call" | custom-call | flops 199999995904 | bytes 1 | tf_op jit(solution)/shard_map/layer/pallas_call | solution.py:223
  107.1 10.2 %term_sums.5 = (bf16[2,3,512,256]{3,2,1,0:T(8,128)(2,1)}, bf16[4,512,256]{2,1,0:T(8,128)(2,1)}, bf16[4,512,256]{2,1,0:T(8,128)(2,1)}, bf16[4,512,256]{2,1,0:T(8,128)(2,1)}) custom-call(s32[5]{0:T(128)} %level_bits.15, s32[16,5]{1,0:T(8,128)} %copy.25.pattern, ...), custom_call_target="tpu_custom_call", output_to_operand_aliasing={{1}: (6, {}), {2}: (7, {}), {3}: (8, {})} | custom-call | flops 1 | bytes 1 | tf_op jit(solution)/shard_map/term_sums/pallas_call | solution.py:298
  117.6 1.7 collective-permute-start.22
  119.4 4.7 %collective-permute-done.17.refs_15_ = bf16[2,6,4,64,256]{4,3,2,1,0:T(8,128)(2,1)} collective-permute-done((bf16[2,6,4,64,256]{4,3,2,1,0:T(8,128)(2,1)}, bf16[2,6,4,64,256]{4,3,2,1,0:T(8,128)(2,1)}, u32[]{:S(2)}, u32[]{:S(2)}) %collective-permute-start.17) | collective-permute-done | bytes 1572896 | tf_op jit(solution)/shard_map/ppermute | solution.py:21
  124.0 1.6 collective-permute-done.15.refs_17_
  125.8 1.3 collective-permute-start.18
  127.1 16.2 %layer.7 = (bf16[3,6,4,64,256]{4,3,2,1,0:T(8,128)(2,1)}, bf16[2,6,4,64,256]{4,3,2,1,0:T(8,128)(2,1)}, bf16[3,6,4,64,256]{4,3,2,1,0:T(8,128)(2,1)}, bf16[2,6,4,64...) custom-call(s32[5]{0:T(128)} %level_bits.15, ...), custom_call_target="tpu_custom_call" | custom-call | flops 199999995904 | bytes 1 | tf_op jit(solution)/shard_map/layer/pallas_call | solution.py:223
  143.4 10.2 %term_sums.6 = (bf16[2,3,512,256]{3,2,1,0:T(8,128)(2,1)}, bf16[4,512,256]{2,1,0:T(8,128)(2,1)}, bf16[4,512,256]{2,1,0:T(8,128)(2,1)}, bf16[4,512,256]{2,1,0:T(8,128)(2,1)}) custom-call(s32[5]{0:T(128)} %level_bits.15, s32[16,5]{1,0:T(8,128)} %copy.25.pattern, bf16[512,1024]{1,0:T(8,128)(2,1)} %get-tuple-element.143.hidden_ref, ...), custom_call_target="tpu_custom_call" | custom-call | flops 1 | bytes 1 | tf_op jit(solution)/shard_map/term_sums/pallas_call | solution.py:298
  153.6 10.2 %term_sums.7 = (bf16[2,3,512,256]{3,2,1,0:T(8,128)(2,1)}, bf16[4,512,256]{2,1,0:T(8,128)(2,1)}, bf16[4,512,256]{2,1,0:T(8,128)(2,1)}, bf16[4,512,256]{2,1,0:T(8,128)(2,1)}) custom-call(s32[5]{0:T(128)} %level_bits.15, s32[16,5]{1,0:T(8,128)} %copy.25.pattern, ...), custom_call_target="tpu_custom_call", output_to_operand_aliasing={{1}: (6, {}), {2}: (7, {}), {3}: (8, {})} | custom-call | flops 1 | bytes 1 | tf_op jit(solution)/shard_map/term_sums/pallas_call | solution.py:298
  164.3 1.3 collective-permute-start.25
  165.6 10.8 %collective-permute-done.18.b_got.refs_1_ = bf16[3,6,4,64,256]{4,3,2,1,0:T(8,128)(2,1)} collective-permute-done((bf16[3,6,4,64,256]{4,3,2,1,0:T(8,128)(2,1)}, bf16[3,6,4,64,256]{4,3,2,1,0:T(8,128)(2,1)}, u32[]{:S(2)}, u32[]{:S(2)}) %collective-permute-start.18) | collective-permute-done | bytes 2359328 | tf_op jit(solution)/shard_map/ppermute | solution.py:21
  177.1 1.3 collective-permute-start.30
  179.0 4.4 %pair_sums.2 = (bf16[1,6,4,64,256]{4,3,2,1,0:T(8,128)(2,1)}, bf16[1,6,4,64,256]{4,3,2,1,0:T(8,128)(2,1)}, bf16[1,6,4,64,256]{4,3,2,1,0:T(8,128)(2,1)}, bf16[1,6,4,64,256]{4,3,2,1,0:T(8,128)(2,1)}) custom-call(bf16[2,6,4,64,256]{4,3,2,1,0:T(8,128)(2,1)} %get-tuple-element.152.refs_0_, bf16[3,6,4,64,256]{4,3,2,1,0:T(8,128)(2,1)} %collective-permute-done.18.b_got.refs_1_, ...), custom_call_target="tpu_custom_call" | custom-call | flops 199999995904 | bytes 1 | tf_op jit(solution)/shard_map/pair_sums/pallas_call | solution.py:332
  183.5 27.4 %collective-permute-done.26.refs_12_.refs_15_ = bf16[4,512,256]{2,1,0:T(8,128)(2,1)} collective-permute-done((bf16[4,512,256]{2,1,0:T(8,128)(2,1)}, bf16[4,512,256]{2,1,0:T(8,128)(2,1)}, u32[]{:S(2)}, u32[]{:S(2)}) %collective-permute-start.26) | collective-permute-done | bytes 1048608 | tf_op jit(solution)/shard_map/ppermute | solution.py:21
  210.9 3.2 %finish.4 = (f32[6,16,64,256]{3,2,1,0:T(8,128)}, f32[6,16,64,256]{3,2,1,0:T(8,128)}) custom-call(bf16[1,6,4,64,256]{4,3,2,1,0:T(8,128)(2,1)} %get-tuple-element.117.a_kept, bf16[3,6,4,64,256]{4,3,2,1,0:T(8,128)(2,1)} %collective-permute-done.16.a_got.refs_3_, bf16[1,6,4,64,256]{4,3,2,1,0:T(8,128)(2,1)} %get-tuple-element.122.b_kept, ...), custom_call_target="tpu_custom_call" | custom-call | flops 1 | bytes 1 | tf_op jit(solution)/shard_map/finish/pallas_call | solution.py:360
  214.1 0.9 copy-done
  215.5 6.7 %combine.1 = (bf16[512,1024]{1,0:T(8,128)(2,1)}, bf16[512,1024]{1,0:T(8,128)(2,1)}) custom-call(bf16[2,3,512,256]{3,2,1,0:T(8,128)(2,1)} %get-tuple-element.129.refs_0_, bf16[2,3,512,256]{3,2,1,0:T(8,128)(2,1)} %get-tuple-element.136.refs_1_, bf16[2,3,512,256]{3,2,1,0:T(8,128)(2,1)} %get-tuple-element.145.refs_2_, ...), custom_call_target="tpu_custom_call" | custom-call | flops 1 | bytes 1 | tf_op jit(solution)/shard_map/combine/pallas_call | solution.py:414
  222.2 0.7 fusion
  222.9 1.3 collective-permute-start.28
  224.2 5.1 %collective-permute-start.27 = (bf16[1,1024]{1,0:T(2,128)(2,1)S(1)}, bf16[1,1024]{1,0:T(2,128)(2,1)}, u32[]{:S(2)}, u32[]{:S(2)}) collective-permute-start(bf16[1,1024]{1,0:T(2,128)(2,1)S(1)} %get-tuple-element.195), channel_id=1, source_target_pairs={{0,8},{8,16},{16,24},{1,9},{9,17},{17,25},{2,10},{10,18},{18,26},{... | collective-permute-start | bytes 6152 | tf_op jit(solution)/shard_map/ppermute | solution.py:37
  230.1 4.3 %pair_sums.3 = (bf16[1,6,4,64,256]{4,3,2,1,0:T(8,128)(2,1)}, bf16[1,6,4,64,256]{4,3,2,1,0:T(8,128)(2,1)}, bf16[1,6,4,64,256]{4,3,2,1,0:T(8,128)(2,1)}, bf16[1,6,4,64,256]{4,3,2,1,0:T(8,128)(2,1)}) custom-call(bf16[2,6,4,64,256]{4,3,2,1,0:T(8,128)(2,1)} %get-tuple-element.168.refs_0_, bf16[3,6,4,64,256]{4,3,2,1,0:T(8,128)(2,1)} %collective-permute-done.29.refs_1_.b_got, ...), custom_call_target="tpu_custom_call" | custom-call | flops 199999995904 | bytes 1 | tf_op jit(solution)/shard_map/pair_sums/pallas_call | solution.py:332
  234.3 3.0 %collective-permute-start.31 = (bf16[1,6,4,64,256]{4,3,2,1,0:T(8,128)(2,1)}, bf16[1,6,4,64,256]{4,3,2,1,0:T(8,128)(2,1)S(1)}, u32[]{:S(2)}, u32[]{:S(2)}) collective-permute-start(bf16[1,6,4,64,256]{4,3,2,1,0:T(8,128)(2,1)} %get-tuple-element.177), channel_id=1, source_target_pairs={{0,16},{8,24},{16,0},{24,8},{1,17},{9,25},{17,1},{25,9},{2,18},{10... | collective-permute-start | bytes 2359304 | tf_op jit(solution)/shard_map/ppermute | solution.py:21
  237.7 3.7 %convolution.3 = bf16[512,1024]{1,0:T(8,128)(2,1)} custom-call(bf16[512,1024]{1,0:T(8,128)(2,1)} %get-tuple-element.166.x_ref, bf16[1,1024]{1,0:T(2,128)(2,1)} %collective-permute-done.27.before_ref, bf16[1,1024]{1,0:T(2,128)(2,1)} %collective-permute-done.28.behind_ref, f32[3,1024]{1,0:T(4,128)} %taps_ref.5), custom_call_target="tpu_custom_call" | custom-call | flops 1 | bytes 1 | tf_op jit(solution)/shard_map/convolution/pallas_call | solution.py:91
  241.4 3.2 %finish.5 = (f32[6,16,64,256]{3,2,1,0:T(8,128)}, f32[6,16,64,256]{3,2,1,0:T(8,128)}) custom-call(bf16[1,6,4,64,256]{4,3,2,1,0:T(8,128)(2,1)} %get-tuple-element.186.a_kept, bf16[3,6,4,64,256]{4,3,2,1,0:T(8,128)(2,1)} %collective-permute-done.30.refs_3_.a_got, ...), custom_call_target="tpu_custom_call", output_to_operand_aliasing={{0}: (4, {}), {1}: (5, {})} | custom-call | flops 1 | bytes 1 | tf_op jit(solution)/shard_map/finish/pallas_call | solution.py:360
  244.6 5.5 %collective-permute-done.33.a_got = bf16[1,6,4,64,256]{4,3,2,1,0:T(8,128)(2,1)} collective-permute-done((bf16[1,6,4,64,256]{4,3,2,1,0:T(8,128)(2,1)}, bf16[1,6,4,64,256]{4,3,2,1,0:T(8,128)(2,1)}, u32[]{:S(2)}, u32[]{:S(2)}) %collective-permute-start.33) | collective-permute-done | bytes 786464 | tf_op jit(solution)/shard_map/ppermute | solution.py:21
  250.3 3.2 %finish.6 = (f32[6,16,64,256]{3,2,1,0:T(8,128)}, f32[6,16,64,256]{3,2,1,0:T(8,128)}) custom-call(bf16[1,6,4,64,256]{4,3,2,1,0:T(8,128)(2,1)} %get-tuple-element.154.a_kept, bf16[1,6,4,64,256]{4,3,2,1,0:T(8,128)(2,1)} %collective-permute-done.33.a_got, ...), custom_call_target="tpu_custom_call", output_to_operand_aliasing={{0}: (4, {}), {1}: (5, {})} | custom-call | flops 1 | bytes 1 | tf_op jit(solution)/shard_map/finish/pallas_call | solution.py:360
  253.4 12.4 %collective-permute-done.31.a_got = bf16[1,6,4,64,256]{4,3,2,1,0:T(8,128)(2,1)S(1)} collective-permute-done((bf16[1,6,4,64,256]{4,3,2,1,0:T(8,128)(2,1)}, bf16[1,6,4,64,256]{4,3,2,1,0:T(8,128)(2,1)S(1)}, u32[]{:S(2)}, u32[]{:S(2)}) %collective-permute-start.31) | collective-permute-done | bytes 786464 | tf_op jit(solution)/shard_map/ppermute | solution.py:21
  265.9 0.8 copy-done.4
  267.0 3.2 %finish.7 = (f32[6,16,64,256]{3,2,1,0:T(8,128)}, f32[6,16,64,256]{3,2,1,0:T(8,128)}) custom-call(bf16[1,6,4,64,256]{4,3,2,1,0:T(8,128)(2,1)} %get-tuple-element.176.a_kept, bf16[1,6,4,64,256]{4,3,2,1,0:T(8,128)(2,1)} %copy-done.4, bf16[1,6,4,64,256]{4,3,2,1,0:T(8,128)(2,1)} %get-tuple-element.178.b_kept, ...), custom_call_target="tpu_custom_call", output_to_operand_aliasing={{0}: (4, {}), {1}: (5, {})} | custom-call | flops 1 | bytes 1 | tf_op jit(solution)/shard_map/finish/pallas_call | solution.py:360
  (75 shorter events, 9.2 us)
Async XLA Ops:
  0.6 19.7 %copy-start.8 = (s32[16,5]{0,1:T(8,128)S(1)}, s32[16,5]{0,1:T(8,128)}, u32[]{:S(2)}) copy-start(s32[16,5]{0,1:T(8,128)} %param.10) | copy-start | bytes 964
  0.6 12.2 %collective-permute-start = (bf16[512,1024]{1,0:T(8,128)(2,1)}, bf16[512,1024]{1,0:T(8,128)(2,1)S(1)}, u32[]{:S(2)}, u32[]{:S(2)}) collective-permute-start(bf16[512,1024]{1,0:T(8,128)(2,1)} %refs_2_.7), channel_id=1, source_target_pairs={{0,1},{1,0},{2,3},{3,2},{4,5},{5,4},{6,7},{7,6},{8,9},{9,8},{10,11... | collective-permute-start | bytes 3145736 | tf_op jit(solution)/shard_map/ppermute | solution.py:21
  2.2 23.3 %collective-permute-start.2 = (bf16[528,256]{1,0:T(8,128)(2,1)S(1)}, bf16[528,256]{1,0:T(8,128)(2,1)S(1)}, u32[]{:S(2)}, u32[]{:S(2)}) collective-permute-start(bf16[528,256]{1,0:T(8,128)(2,1)S(1)} %pad.3), channel_id=1, source_target_pairs={{0,4},{1,5},{2,6},{3,7},{4,0},{5,1},{6,2},{7,3},{8,12},{9,13},{10,... | collective-permute-start | bytes 811016 | tf_op jit(solution)/shard_map/ppermute | solution.py:21
  5.8 27.3 %collective-permute-start.1 = (bf16[528,256]{1,0:T(8,128)(2,1)S(1)}, bf16[528,256]{1,0:T(8,128)(2,1)S(1)}, u32[]{:S(2)}, u32[]{:S(2)}) collective-permute-start(bf16[528,256]{1,0:T(8,128)(2,1)S(1)} %pad.3), channel_id=1, source_target_pairs={{0,2},{1,3},{2,0},{3,1},{4,6},{5,7},{6,4},{7,5},{8,10},{9,11},{10,... | collective-permute-start | bytes 811016 | tf_op jit(solution)/shard_map/ppermute | solution.py:21
  8.1 4.7 %collective-permute-start.3 = (bf16[1,1024]{1,0:T(2,128)(2,1)S(1)}, bf16[1,1024]{1,0:T(2,128)(2,1)S(1)}, u32[]{:S(2)}, u32[]{:S(2)}) collective-permute-start(bf16[1,1024]{1,0:T(2,128)(2,1)S(1)} %get-tuple-element.197), channel_id=1, source_target_pairs={{0,8},{8,16},{16,24},{1,9},{9,17},{17,25},{2,10},{10,18},{18,26},{... | collective-permute-start | bytes 6152 | tf_op jit(solution)/shard_map/ppermute | solution.py:37
  11.6 5.5 %collective-permute-start.4 = (bf16[1,1024]{1,0:T(2,128)(2,1)S(1)}, bf16[1,1024]{1,0:T(2,128)(2,1)S(1)}, u32[]{:S(2)}, u32[]{:S(2)}) collective-permute-start(bf16[1,1024]{1,0:T(2,128)(2,1)S(1)} %get-tuple-element.196), channel_id=1, source_target_pairs={{8,0},{16,8},{24,16},{9,1},{17,9},{25,17},{10,2},{18,10},{26,18},{... | collective-permute-start | bytes 6152 | tf_op jit(solution)/shard_map/ppermute | solution.py:38
  12.9 4.2 %copy-start.6 = (bf16[1,1024]{1,0:T(2,128)(2,1)}, bf16[1,1024]{1,0:T(2,128)(2,1)S(1)}, u32[]{:S(2)}) copy-start(bf16[1,1024]{1,0:T(2,128)(2,1)S(1)} %collective-permute-done.3.before_ref) | copy-start | bytes 6148
  12.9 21.5 %copy-start.9 = (bf16[512,1024]{1,0:T(8,128)(2,1)}, bf16[512,1024]{1,0:T(8,128)(2,1)S(1)}, u32[]{:S(2)}) copy-start(bf16[512,1024]{1,0:T(8,128)(2,1)S(1)} %collective-permute-done.refs_3_) | copy-start | bytes 3145732
  19.5 13.6 %collective-permute-start.7 = (bf16[512,256]{1,0:T(8,128)(2,1)}, bf16[512,256]{1,0:T(8,128)(2,1)S(1)}, u32[]{:S(2)}, u32[]{:S(2)}) collective-permute-start(bf16[512,256]{1,0:T(8,128)(2,1)} %convolution.2), channel_id=1, source_target_pairs={{0,4},{1,5},{2,6},{3,7},{4,0},{5,1},{6,2},{7,3},{8,12},{9,13},{10,... | collective-permute-start | bytes 786440 | tf_op jit(solution)/shard_map/ppermute | solution.py:21
  19.8 13.3 %collective-permute-start.6 = (bf16[512,256]{1,0:T(8,128)(2,1)}, bf16[512,256]{1,0:T(8,128)(2,1)S(1)}, u32[]{:S(2)}, u32[]{:S(2)}) collective-permute-start(bf16[512,256]{1,0:T(8,128)(2,1)} %convolution.2), channel_id=1, source_target_pairs={{0,2},{1,3},{2,0},{3,1},{4,6},{5,7},{6,4},{7,5},{8,10},{9,11},{10,... | collective-permute-start | bytes 786440 | tf_op jit(solution)/shard_map/ppermute | solution.py:21
  20.3 14.1 %collective-permute-start.5 = (bf16[512,256]{1,0:T(8,128)(2,1)}, bf16[512,256]{1,0:T(8,128)(2,1)S(1)}, u32[]{:S(2)}, u32[]{:S(2)}) collective-permute-start(bf16[512,256]{1,0:T(8,128)(2,1)} %convolution.2), channel_id=1, source_target_pairs={{0,1},{1,0},{2,3},{3,2},{4,5},{5,4},{6,7},{7,6},{8,9},{9,8},{10,11... | collective-permute-start | bytes 786440 | tf_op jit(solution)/shard_map/ppermute | solution.py:21
  25.5 8.9 %copy-start.10 = (bf16[528,256]{1,0:T(8,128)(2,1)}, bf16[528,256]{1,0:T(8,128)(2,1)S(1)}, u32[]{:S(2)}) copy-start(bf16[528,256]{1,0:T(8,128)(2,1)S(1)} %collective-permute-done.2.refs_5_) | copy-start | bytes 811012
  25.5 36.1 %collective-permute-start.10 = (bf16[512,1024]{1,0:T(8,128)(2,1)}, bf16[512,1024]{1,0:T(8,128)(2,1)}, u32[]{:S(2)}, u32[]{:S(2)}) collective-permute-start(bf16[512,1024]{1,0:T(8,128)(2,1)} %get-tuple-element.101.refs_6_.refs_7_.refs_8_), channel_id=1, source_target_pairs={{0,1},{1,0},{2,3},{3,2},{4,5},{5,4},{6,7},{7,6},{8,9},{9,8},{10,11... | collective-permute-start | bytes 3145736 | tf_op jit(solution)/shard_map/ppermute | solution.py:21
  33.1 1.3 copy-start.12
  33.1 1.3 copy-start.11
  33.1 1.3 copy-start.13
  33.1 26.5 %collective-permute-start.8 = (bf16[2,512,256]{2,1,0:T(8,128)(2,1)}, bf16[2,512,256]{2,1,0:T(8,128)(2,1)}, u32[]{:S(2)}, u32[]{:S(2)}) collective-permute-start(bf16[2,512,256]{2,1,0:T(8,128)(2,1)} %get-tuple-element.105), channel_id=1, source_target_pairs={{0,2},{1,3},{2,0},{3,1},{4,6},{5,7},{6,4},{7,5},{8,10},{9,11},{10,... | collective-permute-start | bytes 1572872 | tf_op jit(solution)/shard_map/ppermute | solution.py:21
  33.2 26.4 %collective-permute-start.9 = (bf16[2,512,256]{2,1,0:T(8,128)(2,1)}, bf16[2,512,256]{2,1,0:T(8,128)(2,1)}, u32[]{:S(2)}, u32[]{:S(2)}) collective-permute-start(bf16[2,512,256]{2,1,0:T(8,128)(2,1)} %get-tuple-element.105), channel_id=1, source_target_pairs={{0,4},{1,5},{2,6},{3,7},{4,0},{5,1},{6,2},{7,3},{8,12},{9,13},{10,... | collective-permute-start | bytes 1572872 | tf_op jit(solution)/shard_map/ppermute | solution.py:21
  49.3 39.8 %collective-permute-start.13 = (bf16[2,6,4,64,256]{4,3,2,1,0:T(8,128)(2,1)}, bf16[2,6,4,64,256]{4,3,2,1,0:T(8,128)(2,1)}, u32[]{:S(2)}, u32[]{:S(2)}) collective-permute-start(bf16[2,6,4,64,256]{4,3,2,1,0:T(8,128)(2,1)} %get-tuple-element.114), channel_id=1, source_target_pairs={{0,8},{8,0},{16,24},{24,16},{1,9},{9,1},{17,25},{25,17},{2,10},{10... | collective-permute-start | bytes 4718600 | tf_op jit(solution)/shard_map/ppermute | solution.py:21
  51.6 37.4 %collective-permute-start.14 = (bf16[2,6,4,64,256]{4,3,2,1,0:T(8,128)(2,1)}, bf16[2,6,4,64,256]{4,3,2,1,0:T(8,128)(2,1)}, u32[]{:S(2)}, u32[]{:S(2)}) collective-permute-start(bf16[2,6,4,64,256]{4,3,2,1,0:T(8,128)(2,1)} %get-tuple-element.116), channel_id=1, source_target_pairs={{0,16},{8,24},{16,0},{24,8},{1,17},{9,25},{17,1},{25,9},{2,18},{10... | collective-permute-start | bytes 4718600 | tf_op jit(solution)/shard_map/ppermute | solution.py:21
  59.6 26.3 %collective-permute-start.11 = (bf16[2,512,256]{2,1,0:T(8,128)(2,1)}, bf16[2,512,256]{2,1,0:T(8,128)(2,1)}, u32[]{:S(2)}, u32[]{:S(2)}) collective-permute-start(bf16[2,512,256]{2,1,0:T(8,128)(2,1)} %get-tuple-element.112), channel_id=1, source_target_pairs={{0,2},{1,3},{2,0},{3,1},{4,6},{5,7},{6,4},{7,5},{8,10},{9,11},{10,... | collective-permute-start | bytes 1572872 | tf_op jit(solution)/shard_map/ppermute | solution.py:21
  59.6 26.3 %collective-permute-start.12 = (bf16[2,512,256]{2,1,0:T(8,128)(2,1)}, bf16[2,512,256]{2,1,0:T(8,128)(2,1)}, u32[]{:S(2)}, u32[]{:S(2)}) collective-permute-start(bf16[2,512,256]{2,1,0:T(8,128)(2,1)} %get-tuple-element.112), channel_id=1, source_target_pairs={{0,4},{1,5},{2,6},{3,7},{4,0},{5,1},{6,2},{7,3},{8,12},{9,13},{10,... | collective-permute-start | bytes 1572872 | tf_op jit(solution)/shard_map/ppermute | solution.py:21
  86.0 31.3 %collective-permute-start.19 = (bf16[2,512,256]{2,1,0:T(8,128)(2,1)}, bf16[2,512,256]{2,1,0:T(8,128)(2,1)}, u32[]{:S(2)}, u32[]{:S(2)}) collective-permute-start(bf16[2,512,256]{2,1,0:T(8,128)(2,1)} %get-tuple-element.139), channel_id=1, source_target_pairs={{0,2},{1,3},{2,0},{3,1},{4,6},{5,7},{6,4},{7,5},{8,10},{9,11},{10,... | collective-permute-start | bytes 1572872 | tf_op jit(solution)/shard_map/ppermute | solution.py:21
  86.3 31.0 %collective-permute-start.20 = (bf16[2,512,256]{2,1,0:T(8,128)(2,1)}, bf16[2,512,256]{2,1,0:T(8,128)(2,1)}, u32[]{:S(2)}, u32[]{:S(2)}) collective-permute-start(bf16[2,512,256]{2,1,0:T(8,128)(2,1)} %get-tuple-element.139), channel_id=1, source_target_pairs={{0,4},{1,5},{2,6},{3,7},{4,0},{5,1},{6,2},{7,3},{8,12},{9,13},{10,... | collective-permute-start | bytes 1572872 | tf_op jit(solution)/shard_map/ppermute | solution.py:21
  89.0 35.0 %collective-permute-start.17 = (bf16[2,6,4,64,256]{4,3,2,1,0:T(8,128)(2,1)}, bf16[2,6,4,64,256]{4,3,2,1,0:T(8,128)(2,1)}, u32[]{:S(2)}, u32[]{:S(2)}) collective-permute-start(bf16[2,6,4,64,256]{4,3,2,1,0:T(8,128)(2,1)} %get-tuple-element.125), channel_id=1, source_target_pairs={{0,8},{8,0},{16,24},{24,16},{1,9},{9,1},{17,25},{25,17},{2,10},{10... | collective-permute-start | bytes 4718600 | tf_op jit(solution)/shard_map/ppermute | solution.py:21
  91.1 34.6 %collective-permute-start.15 = (bf16[2,6,4,64,256]{4,3,2,1,0:T(8,128)(2,1)}, bf16[2,6,4,64,256]{4,3,2,1,0:T(8,128)(2,1)}, u32[]{:S(2)}, u32[]{:S(2)}) collective-permute-start(bf16[2,6,4,64,256]{4,3,2,1,0:T(8,128)(2,1)} %get-tuple-element.120), channel_id=1, source_target_pairs={{0,16},{8,24},{16,0},{24,8},{1,17},{9,25},{17,1},{25,9},{2,18},{10... | collective-permute-start | bytes 4718600 | tf_op jit(solution)/shard_map/ppermute | solution.py:21
  117.3 46.5 %collective-permute-start.23 = (bf16[4,512,256]{2,1,0:T(8,128)(2,1)}, bf16[4,512,256]{2,1,0:T(8,128)(2,1)}, u32[]{:S(2)}, u32[]{:S(2)}) collective-permute-start(bf16[4,512,256]{2,1,0:T(8,128)(2,1)} %get-tuple-element.159), channel_id=1, source_target_pairs={{0,4},{1,5},{2,6},{3,7},{4,0},{5,1},{6,2},{7,3},{8,12},{9,13},{10,... | collective-permute-start | bytes 3145736 | tf_op jit(solution)/shard_map/ppermute | solution.py:21
  117.6 46.1 %collective-permute-start.22 = (bf16[4,512,256]{2,1,0:T(8,128)(2,1)}, bf16[4,512,256]{2,1,0:T(8,128)(2,1)}, u32[]{:S(2)}, u32[]{:S(2)}) collective-permute-start(bf16[4,512,256]{2,1,0:T(8,128)(2,1)} %get-tuple-element.157), channel_id=1, source_target_pairs={{0,2},{1,3},{2,0},{3,1},{4,6},{5,7},{6,4},{7,5},{8,10},{9,11},{10,... | collective-permute-start | bytes 3145736 | tf_op jit(solution)/shard_map/ppermute | solution.py:21
  125.7 51.4 %collective-permute-start.16 = (bf16[3,6,4,64,256]{4,3,2,1,0:T(8,128)(2,1)}, bf16[3,6,4,64,256]{4,3,2,1,0:T(8,128)(2,1)}, u32[]{:S(2)}, u32[]{:S(2)}) collective-permute-start(bf16[3,6,4,64,256]{4,3,2,1,0:T(8,128)(2,1)} %get-tuple-element.121), channel_id=1, source_target_pairs={{0,16},{8,24},{16,0},{24,8},{1,17},{9,25},{17,1},{25,9},{2,18},{10... | collective-permute-start | bytes 7077896 | tf_op jit(solution)/shard_map/ppermute | solution.py:21
  125.8 50.7 %collective-permute-start.18 = (bf16[3,6,4,64,256]{4,3,2,1,0:T(8,128)(2,1)}, bf16[3,6,4,64,256]{4,3,2,1,0:T(8,128)(2,1)}, u32[]{:S(2)}, u32[]{:S(2)}) collective-permute-start(bf16[3,6,4,64,256]{4,3,2,1,0:T(8,128)(2,1)} %get-tuple-element.126), channel_id=1, source_target_pairs={{0,8},{8,0},{16,24},{24,16},{1,9},{9,1},{17,25},{25,17},{2,10},{10... | collective-permute-start | bytes 7077896 | tf_op jit(solution)/shard_map/ppermute | solution.py:21
  163.8 47.1 %collective-permute-start.26 = (bf16[4,512,256]{2,1,0:T(8,128)(2,1)}, bf16[4,512,256]{2,1,0:T(8,128)(2,1)}, u32[]{:S(2)}, u32[]{:S(2)}) collective-permute-start(bf16[4,512,256]{2,1,0:T(8,128)(2,1)} %get-tuple-element.165), channel_id=1, source_target_pairs={{0,4},{1,5},{2,6},{3,7},{4,0},{5,1},{6,2},{7,3},{8,12},{9,13},{10,... | collective-permute-start | bytes 3145736 | tf_op jit(solution)/shard_map/ppermute | solution.py:21
  164.3 49.8 %collective-permute-start.25 = (bf16[4,512,256]{2,1,0:T(8,128)(2,1)}, bf16[4,512,256]{2,1,0:T(8,128)(2,1)}, u32[]{:S(2)}, u32[]{:S(2)}) collective-permute-start(bf16[4,512,256]{2,1,0:T(8,128)(2,1)} %get-tuple-element.163), channel_id=1, source_target_pairs={{0,2},{1,3},{2,0},{3,1},{4,6},{5,7},{6,4},{7,5},{8,10},{9,11},{10,... | collective-permute-start | bytes 3145736 | tf_op jit(solution)/shard_map/ppermute | solution.py:21
  177.1 52.3 %collective-permute-start.30 = (bf16[3,6,4,64,256]{4,3,2,1,0:T(8,128)(2,1)}, bf16[3,6,4,64,256]{4,3,2,1,0:T(8,128)(2,1)}, u32[]{:S(2)}, u32[]{:S(2)}) collective-permute-start(bf16[3,6,4,64,256]{4,3,2,1,0:T(8,128)(2,1)} %get-tuple-element.174), channel_id=1, source_target_pairs={{0,16},{8,24},{16,0},{24,8},{1,17},{9,25},{17,1},{25,9},{2,18},{10... | collective-permute-start | bytes 7077896 | tf_op jit(solution)/shard_map/ppermute | solution.py:21
  178.4 51.1 %collective-permute-start.29 = (bf16[3,6,4,64,256]{4,3,2,1,0:T(8,128)(2,1)}, bf16[3,6,4,64,256]{4,3,2,1,0:T(8,128)(2,1)}, u32[]{:S(2)}, u32[]{:S(2)}) collective-permute-start(bf16[3,6,4,64,256]{4,3,2,1,0:T(8,128)(2,1)} %get-tuple-element.170), channel_id=1, source_target_pairs={{0,8},{8,0},{16,24},{24,16},{1,9},{9,1},{17,25},{25,17},{2,10},{10... | collective-permute-start | bytes 7077896 | tf_op jit(solution)/shard_map/ppermute | solution.py:21
  179.0 4.4 %copy-start.2 = (bf16[4,512,256]{2,1,0:T(8,128)(2,1)S(1)}, bf16[4,512,256]{2,1,0:T(8,128)(2,1)}, u32[]{:S(2)}) copy-start(bf16[4,512,256]{2,1,0:T(8,128)(2,1)} %get-tuple-element.155) | copy-start | bytes 3145732
  179.0 31.9 %copy-start.3 = (bf16[4,512,256]{2,1,0:T(8,128)(2,1)S(1)}, bf16[4,512,256]{2,1,0:T(8,128)(2,1)}, u32[]{:S(2)}) copy-start(bf16[4,512,256]{2,1,0:T(8,128)(2,1)} %get-tuple-element.161) | copy-start | bytes 3145732
  183.5 30.7 %collective-permute-start.21 = (bf16[4,512,256]{2,1,0:T(8,128)(2,1)S(1)}, bf16[4,512,256]{2,1,0:T(8,128)(2,1)S(1)}, u32[]{:S(2)}, u32[]{:S(2)}) collective-permute-start(bf16[4,512,256]{2,1,0:T(8,128)(2,1)S(1)} %copy-done.2), channel_id=1, source_target_pairs={{0,1},{1,0},{2,3},{3,2},{4,5},{5,4},{6,7},{7,6},{8,9},{9,8},{10,11... | collective-permute-start | bytes 3145736 | tf_op jit(solution)/shard_map/ppermute | solution.py:21
  210.9 3.2 %collective-permute-start.24 = (bf16[4,512,256]{2,1,0:T(8,128)(2,1)S(1)}, bf16[4,512,256]{2,1,0:T(8,128)(2,1)S(1)}, u32[]{:S(2)}, u32[]{:S(2)}) collective-permute-start(bf16[4,512,256]{2,1,0:T(8,128)(2,1)S(1)} %copy-done.3), channel_id=1, source_target_pairs={{0,1},{1,0},{2,3},{3,2},{4,5},{5,4},{6,7},{7,6},{8,9},{9,8},{10,11... | collective-permute-start | bytes 3145736 | tf_op jit(solution)/shard_map/ppermute | solution.py:21
  214.1 1.0 copy-start
  214.1 1.3 copy-start.1
  222.9 7.1 %collective-permute-start.28 = (bf16[1,1024]{1,0:T(2,128)(2,1)S(1)}, bf16[1,1024]{1,0:T(2,128)(2,1)}, u32[]{:S(2)}, u32[]{:S(2)}) collective-permute-start(bf16[1,1024]{1,0:T(2,128)(2,1)S(1)} %get-tuple-element.194), channel_id=1, source_target_pairs={{8,0},{16,8},{24,16},{9,1},{17,9},{25,17},{10,2},{18,10},{26,18},{... | collective-permute-start | bytes 6152 | tf_op jit(solution)/shard_map/ppermute | solution.py:38
  224.2 5.9 %collective-permute-start.27 = (bf16[1,1024]{1,0:T(2,128)(2,1)S(1)}, bf16[1,1024]{1,0:T(2,128)(2,1)}, u32[]{:S(2)}, u32[]{:S(2)}) collective-permute-start(bf16[1,1024]{1,0:T(2,128)(2,1)S(1)} %get-tuple-element.195), channel_id=1, source_target_pairs={{0,8},{8,16},{16,24},{1,9},{9,17},{17,25},{2,10},{10,18},{18,26},{... | collective-permute-start | bytes 6152 | tf_op jit(solution)/shard_map/ppermute | solution.py:37
  229.4 20.7 %collective-permute-start.33 = (bf16[1,6,4,64,256]{4,3,2,1,0:T(8,128)(2,1)}, bf16[1,6,4,64,256]{4,3,2,1,0:T(8,128)(2,1)}, u32[]{:S(2)}, u32[]{:S(2)}) collective-permute-start(bf16[1,6,4,64,256]{4,3,2,1,0:T(8,128)(2,1)} %get-tuple-element.181), channel_id=1, source_target_pairs={{0,16},{8,24},{16,0},{24,8},{1,17},{9,25},{17,1},{25,9},{2,18},{10... | collective-permute-start | bytes 2359304 | tf_op jit(solution)/shard_map/ppermute | solution.py:21
  229.5 20.7 %collective-permute-start.34 = (bf16[1,6,4,64,256]{4,3,2,1,0:T(8,128)(2,1)}, bf16[1,6,4,64,256]{4,3,2,1,0:T(8,128)(2,1)}, u32[]{:S(2)}, u32[]{:S(2)}) collective-permute-start(bf16[1,6,4,64,256]{4,3,2,1,0:T(8,128)(2,1)} %get-tuple-element.185), channel_id=1, source_target_pairs={{0,8},{8,0},{16,24},{24,16},{1,9},{9,1},{17,25},{25,17},{2,10},{10... | collective-permute-start | bytes 2359304 | tf_op jit(solution)/shard_map/ppermute | solution.py:21
  234.3 31.4 %collective-permute-start.31 = (bf16[1,6,4,64,256]{4,3,2,1,0:T(8,128)(2,1)}, bf16[1,6,4,64,256]{4,3,2,1,0:T(8,128)(2,1)S(1)}, u32[]{:S(2)}, u32[]{:S(2)}) collective-permute-start(bf16[1,6,4,64,256]{4,3,2,1,0:T(8,128)(2,1)} %get-tuple-element.177), channel_id=1, source_target_pairs={{0,16},{8,24},{16,0},{24,8},{1,17},{9,25},{17,1},{25,9},{2,18},{10... | collective-permute-start | bytes 2359304 | tf_op jit(solution)/shard_map/ppermute | solution.py:21
  237.4 28.5 %collective-permute-start.32 = (bf16[1,6,4,64,256]{4,3,2,1,0:T(8,128)(2,1)}, bf16[1,6,4,64,256]{4,3,2,1,0:T(8,128)(2,1)S(1)}, u32[]{:S(2)}, u32[]{:S(2)}) collective-permute-start(bf16[1,6,4,64,256]{4,3,2,1,0:T(8,128)(2,1)} %get-tuple-element.179), channel_id=1, source_target_pairs={{0,8},{8,0},{16,24},{24,16},{1,9},{9,1},{17,25},{25,17},{2,10},{10... | collective-permute-start | bytes 2359304 | tf_op jit(solution)/shard_map/ppermute | solution.py:21
  265.8 0.9 copy-start.4
  265.9 1.1 copy-start.5
  (2 other events, 1.3 us)

commit v4 on v3

--- a/solution.py
+++ b/solution.py
@@ -348,7 +348,15 @@
     b_out[...] = b_kept[0].astype(f32) + b_got[0].astype(f32)
 
 
-def finish(a_kept, a_got, b_kept, b_got, outs, first, hidden_dev):
+def finish_resident_kernel(a_kept, a_got, b_kept, b_got, *refs):
+    a_out, b_out = refs[-2:]
+    size = a_out.shape[0]
+    at = pl.ds(pl.program_id(0) * size, size)
+    a_out[...] = a_kept[0, at].astype(f32) + a_got[a_got.shape[0] - 1, at].astype(f32)
+    b_out[...] = b_kept[0, at].astype(f32) + b_got[b_got.shape[0] - 1, at].astype(f32)
+
+
+def finish(a_kept, a_got, b_kept, b_got, outs, first, hidden_dev, resident=False):
     _, terms, blocks, slab, width = a_kept.shape
     step = 2 if terms % 2 == 0 else 1
     spec = lambda array: pl.BlockSpec(
@@ -358,13 +366,16 @@
     shape = jax.ShapeDtypeStruct((terms, hidden_dev, slab, width), f32)
     extra = [] if outs is None else list(outs)
     return pl.pallas_call(
-        finish_kernel,
+        finish_resident_kernel if resident else finish_kernel,
         out_shape=[shape, shape],
         grid=(step,),
-        in_specs=[spec(array) for array in (a_kept, a_got, b_kept, b_got)] + [ANY] * len(extra),
+        in_specs=[
+            pl.BlockSpec(memory_space=pltpu.VMEM) if resident else spec(array) for array in (a_kept, a_got, b_kept, b_got)
+        ]
+        + [ANY] * len(extra),
         out_specs=[out_spec] * 2,
         input_output_aliases={4 + i: i for i in range(len(extra))},
-        compiler_params=pltpu.CompilerParams(vmem_limit_bytes=VMEM_LIMIT),
+        compiler_params=pltpu.CompilerParams(vmem_limit_bytes=VMEM_LIMIT // 2 if resident else VMEM_LIMIT),
         cost_estimate=cost(),
         name="finish",
     )(a_kept, a_got, b_kept, b_got, *extra)
@@ -544,7 +555,7 @@
             kept, got, down_kept, down_got = end(j)
             if j == blocks_dev - 2:
                 got = after(got, convolved)
-            outs = finish(kept, got, down_kept, down_got, outs, j * ratio, hidden_dev)
+            outs = finish(kept, got, down_kept, down_got, outs, j * ratio, hidden_dev, j == blocks_dev - 1)
     else:
         for j in range(blocks_dev):
             got = [x_got[j], y_got[j]]

time: 271 us -> 269 us (level)
  transfers between devices with their start and end apart: 35 -> 35, of which waited for: 12 -> 12; matrix products, arithmetic and copies ran while one was open for 1% -> 1% of each run, Pallas kernels for 50% -> 51%
where the time goes in v4:
time: 269 us; the launch traced here: 268 us
  Pallas kernels  138 us (51%)
  waiting for transfers between devices  82 us (30%)
  starting transfers between devices  40.8 us (15%)
  local copies, waits for them, and re-layouts  5.78 us (2%)
    ppermute x31, waiting for transfers between devices, swapped(): lax.ppermute(array, axis, [(i, i ^ 1 << bit) for i in range(lax.axis_size...  77.8 us
    pallas_call x4, Pallas kernels, layer(): pl.pallas_call(functools.partial(layer_kernel, block=block, ratio=ratio,...  60.6 us
    pallas_call x4, Pallas kernels, term_sums(): pl.pallas_call(functools.partial(terms_kernel, block=block, ratio=ratio,...  40.8 us
    ppermute x31, starting transfers between devices, swapped(): lax.ppermute(array, axis, [(i, i ^ 1 << bit) for i in range(lax.axis_size...  29.7 us
    pallas_call x4, Pallas kernels, finish(): pl.pallas_call(finish_resident_kernel if resident else finish_kernel, out...  11.5 us
    pallas_call x2, Pallas kernels, pair_sums(): pl.pallas_call(functools.partial(pair_kernel, bits=bits), out_shape=[half...  8.68 us
    ppermute x2, starting transfers between devices, halo(): before = lax.ppermute(lax.slice_in_dim(array, rows - 1, rows), 'seq', up)  8.54 us
    pallas_call x1, Pallas kernels, combine(): pl.pallas_call(functools.partial(combine_kernel, remote_bits=remote_bits,...  6.68 us
  transfers between devices with their start and end apart: 35, of which 12 were waited for; matrix products, arithmetic and copies ran while one was open for 1% of the time, Pallas kernels for 51%

profile of v4, /device:TPU:0, one launch (start us, length us, event | category | flops | bytes accessed | tf_op | source)
XLA Modules:
  0.0 267.7 jit_solution(11726802871690128340)
XLA Ops:
  1.2 1.0 slice.15
  2.2 3.7 %collective-permute-start.2 = (bf16[528,256]{1,0:T(8,128)(2,1)S(1)}, bf16[528,256]{1,0:T(8,128)(2,1)S(1)}, u32[]{:S(2)}, u32[]{:S(2)}) collective-permute-start(bf16[528,256]{1,0:T(8,128)(2,1)S(1)} %pad.3), channel_id=1, source_target_pairs={{0,4},{1,5},{2,6},{3,7},{4,0},{5,1},{6,2},{7,3},{8,12},{9,13},{10,... | collective-permute-start | bytes 811016 | tf_op jit(solution)/shard_map/ppermute | solution.py:21
  5.8 1.6 collective-permute-start.1
  7.4 0.7 fusion.1
  8.1 3.4 %collective-permute-start.3 = (bf16[1,1024]{1,0:T(2,128)(2,1)S(1)}, bf16[1,1024]{1,0:T(2,128)(2,1)S(1)}, u32[]{:S(2)}, u32[]{:S(2)}) collective-permute-start(bf16[1,1024]{1,0:T(2,128)(2,1)S(1)} %get-tuple-element.197), channel_id=1, source_target_pairs={{0,8},{8,16},{16,24},{1,9},{9,17},{17,25},{2,10},{10,18},{18,26},{... | collective-permute-start | bytes 6152 | tf_op jit(solution)/shard_map/ppermute | solution.py:37
  11.6 1.3 collective-permute-start.4
  12.9 4.2 %collective-permute-done.4.behind_ref = bf16[1,1024]{1,0:T(2,128)(2,1)S(1)} collective-permute-done((bf16[1,1024]{1,0:T(2,128)(2,1)S(1)}, bf16[1,1024]{1,0:T(2,128)(2,1)S(1)}, u32[]{:S(2)}, u32[]{:S(2)}) %collective-permute-start.4) | collective-permute-done | bytes 2080 | tf_op jit(solution)/shard_map/ppermute | solution.py:38
  17.6 1.9 convolution.2
  20.3 0.7 copy.25.pattern
  21.0 4.5 %prepare.1 = (bf16[512,1024]{1,0:T(8,128)(2,1)}, bf16[2,512,256]{2,1,0:T(8,128)(2,1)}, bf16[2,512,256]{2,1,0:T(8,128)(2,1)}, bf16[2,512,256]{2,1,0:T(8,128)(2,1)}) custom-call(bf16[512,1024]{1,0:T(8,128)(2,1)} %refs_2_.7, bf16[512,1024]{1,0:T(8,128)(2,1)} %cot_ref.1, bf16[1,1024]{1,0:T(2,128)(2,1)} %copy-done.6, bf16[1,1024]{1,0:T(2,128)(2,1)} %copy-done.7, ...), custom_call_target="tpu_custom_call" | custom-call | flops 1 | bytes 1 | tf_op jit(solution)/shard_map/prepare/pallas_call | solution.py:70
  26.0 7.1 %collective-permute-done.7.refs_11_ = bf16[512,256]{1,0:T(8,128)(2,1)S(1)} collective-permute-done((bf16[512,256]{1,0:T(8,128)(2,1)}, bf16[512,256]{1,0:T(8,128)(2,1)S(1)}, u32[]{:S(2)}, u32[]{:S(2)}) %collective-permute-start.7) | collective-permute-done | bytes 262176 | tf_op jit(solution)/shard_map/ppermute | solution.py:21
  33.2 1.1 collective-permute-start.9
  35.1 14.2 %layer.4 = (bf16[2,6,4,64,256]{4,3,2,1,0:T(8,128)(2,1)}, bf16[2,6,4,64,256]{4,3,2,1,0:T(8,128)(2,1)}, bf16[2,6,4,64,256]{4,3,2,1,0:T(8,128)(2,1)}, bf16[2,6,4,64...) custom-call(s32[5]{0:T(128)} %level_bits.15, s32[16,5]{1,0:T(8,128)} %copy.25.pattern, ...), custom_call_target="tpu_custom_call" | custom-call | flops 199999995904 | bytes 1 | tf_op jit(solution)/shard_map/layer/pallas_call | solution.py:223
  49.3 2.4 collective-permute-start.13
  52.1 7.5 %collective-permute-done.9.refs_5_.refs_11_ = bf16[2,512,256]{2,1,0:T(8,128)(2,1)} collective-permute-done((bf16[2,512,256]{2,1,0:T(8,128)(2,1)}, bf16[2,512,256]{2,1,0:T(8,128)(2,1)}, u32[]{:S(2)}, u32[]{:S(2)}) %collective-permute-start.9) | collective-permute-done | bytes 524320 | tf_op jit(solution)/shard_map/ppermute | solution.py:21
  59.6 2.0 collective-permute-start.12
  61.6 14.2 %layer.5 = (bf16[2,6,4,64,256]{4,3,2,1,0:T(8,128)(2,1)}, bf16[2,6,4,64,256]{4,3,2,1,0:T(8,128)(2,1)}, bf16[2,6,4,64,256]{4,3,2,1,0:T(8,128)(2,1)}, bf16[2,6,4,64...) custom-call(s32[5]{0:T(128)} %level_bits.15, s32[16,5]{1,0:T(8,128)} %copy.25.pattern, ...), custom_call_target="tpu_custom_call" | custom-call | flops 199999995904 | bytes 1 | tf_op jit(solution)/shard_map/layer/pallas_call | solution.py:223
  75.8 10.2 %term_sums.4 = (bf16[2,3,512,256]{3,2,1,0:T(8,128)(2,1)}, bf16[4,512,256]{2,1,0:T(8,128)(2,1)}, bf16[4,512,256]{2,1,0:T(8,128)(2,1)}, bf16[4,512,256]{2,1,0:T(8,128)(2,1)}) custom-call(s32[5]{0:T(128)} %level_bits.15, s32[16,5]{1,0:T(8,128)} %copy.25.pattern, bf16[512,1024]{1,0:T(8,128)(2,1)} %get-tuple-element.107.hidden_ref, ...), custom_call_target="tpu_custom_call" | custom-call | flops 1 | bytes 1 | tf_op jit(solution)/shard_map/term_sums/pallas_call | solution.py:298
  86.3 2.7 collective-permute-start.20
  89.0 2.1 collective-permute-start.17
  91.1 16.0 %layer.6 = (bf16[3,6,4,64,256]{4,3,2,1,0:T(8,128)(2,1)}, bf16[2,6,4,64,256]{4,3,2,1,0:T(8,128)(2,1)}, bf16[3,6,4,64,256]{4,3,2,1,0:T(8,128)(2,1)}, bf16[2,6,4,64...) custom-call(s32[5]{0:T(128)} %level_bits.15, ...), custom_call_target="tpu_custom_call" | custom-call | flops 199999995904 | bytes 1 | tf_op jit(solution)/shard_map/layer/pallas_call | solution.py:223
  107.1 10.2 %term_sums.5 = (bf16[2,3,512,256]{3,2,1,0:T(8,128)(2,1)}, bf16[4,512,256]{2,1,0:T(8,128)(2,1)}, bf16[4,512,256]{2,1,0:T(8,128)(2,1)}, bf16[4,512,256]{2,1,0:T(8,128)(2,1)}) custom-call(s32[5]{0:T(128)} %level_bits.15, s32[16,5]{1,0:T(8,128)} %copy.25.pattern, ...), custom_call_target="tpu_custom_call", output_to_operand_aliasing={{1}: (6, {}), {2}: (7, {}), {3}: (8, {})} | custom-call | flops 1 | bytes 1 | tf_op jit(solution)/shard_map/term_sums/pallas_call | solution.py:298
  117.6 1.7 collective-permute-start.22
  119.4 4.7 %collective-permute-done.17.refs_15_ = bf16[2,6,4,64,256]{4,3,2,1,0:T(8,128)(2,1)} collective-permute-done((bf16[2,6,4,64,256]{4,3,2,1,0:T(8,128)(2,1)}, bf16[2,6,4,64,256]{4,3,2,1,0:T(8,128)(2,1)}, u32[]{:S(2)}, u32[]{:S(2)}) %collective-permute-start.17) | collective-permute-done | bytes 1572896 | tf_op jit(solution)/shard_map/ppermute | solution.py:21
  124.0 1.6 collective-permute-done.15.refs_17_
  125.8 1.3 collective-permute-start.18
  127.1 16.2 %layer.7 = (bf16[3,6,4,64,256]{4,3,2,1,0:T(8,128)(2,1)}, bf16[2,6,4,64,256]{4,3,2,1,0:T(8,128)(2,1)}, bf16[3,6,4,64,256]{4,3,2,1,0:T(8,128)(2,1)}, bf16[2,6,4,64...) custom-call(s32[5]{0:T(128)} %level_bits.15, ...), custom_call_target="tpu_custom_call" | custom-call | flops 199999995904 | bytes 1 | tf_op jit(solution)/shard_map/layer/pallas_call | solution.py:223
  143.4 10.2 %term_sums.6 = (bf16[2,3,512,256]{3,2,1,0:T(8,128)(2,1)}, bf16[4,512,256]{2,1,0:T(8,128)(2,1)}, bf16[4,512,256]{2,1,0:T(8,128)(2,1)}, bf16[4,512,256]{2,1,0:T(8,128)(2,1)}) custom-call(s32[5]{0:T(128)} %level_bits.15, s32[16,5]{1,0:T(8,128)} %copy.25.pattern, bf16[512,1024]{1,0:T(8,128)(2,1)} %get-tuple-element.143.hidden_ref, ...), custom_call_target="tpu_custom_call" | custom-call | flops 1 | bytes 1 | tf_op jit(solution)/shard_map/term_sums/pallas_call | solution.py:298
  153.6 10.2 %term_sums.7 = (bf16[2,3,512,256]{3,2,1,0:T(8,128)(2,1)}, bf16[4,512,256]{2,1,0:T(8,128)(2,1)}, bf16[4,512,256]{2,1,0:T(8,128)(2,1)}, bf16[4,512,256]{2,1,0:T(8,128)(2,1)}) custom-call(s32[5]{0:T(128)} %level_bits.15, s32[16,5]{1,0:T(8,128)} %copy.25.pattern, ...), custom_call_target="tpu_custom_call", output_to_operand_aliasing={{1}: (6, {}), {2}: (7, {}), {3}: (8, {})} | custom-call | flops 1 | bytes 1 | tf_op jit(solution)/shard_map/term_sums/pallas_call | solution.py:298
  164.3 1.3 collective-permute-start.25
  165.6 10.8 %collective-permute-done.18.b_got.refs_1_ = bf16[3,6,4,64,256]{4,3,2,1,0:T(8,128)(2,1)} collective-permute-done((bf16[3,6,4,64,256]{4,3,2,1,0:T(8,128)(2,1)}, bf16[3,6,4,64,256]{4,3,2,1,0:T(8,128)(2,1)}, u32[]{:S(2)}, u32[]{:S(2)}) %collective-permute-start.18) | collective-permute-done | bytes 2359328 | tf_op jit(solution)/shard_map/ppermute | solution.py:21
  177.1 1.3 collective-permute-start.30
  179.0 4.4 %pair_sums.2 = (bf16[1,6,4,64,256]{4,3,2,1,0:T(8,128)(2,1)}, bf16[1,6,4,64,256]{4,3,2,1,0:T(8,128)(2,1)}, bf16[1,6,4,64,256]{4,3,2,1,0:T(8,128)(2,1)}, bf16[1,6,4,64,256]{4,3,2,1,0:T(8,128)(2,1)}) custom-call(bf16[2,6,4,64,256]{4,3,2,1,0:T(8,128)(2,1)} %get-tuple-element.152.refs_0_, bf16[3,6,4,64,256]{4,3,2,1,0:T(8,128)(2,1)} %collective-permute-done.18.b_got.refs_1_, ...), custom_call_target="tpu_custom_call" | custom-call | flops 199999995904 | bytes 1 | tf_op jit(solution)/shard_map/pair_sums/pallas_call | solution.py:332
  183.5 27.4 %collective-permute-done.26.refs_12_.refs_15_ = bf16[4,512,256]{2,1,0:T(8,128)(2,1)} collective-permute-done((bf16[4,512,256]{2,1,0:T(8,128)(2,1)}, bf16[4,512,256]{2,1,0:T(8,128)(2,1)}, u32[]{:S(2)}, u32[]{:S(2)}) %collective-permute-start.26) | collective-permute-done | bytes 1048608 | tf_op jit(solution)/shard_map/ppermute | solution.py:21
  210.9 3.2 %finish.4 = (f32[6,16,64,256]{3,2,1,0:T(8,128)}, f32[6,16,64,256]{3,2,1,0:T(8,128)}) custom-call(bf16[1,6,4,64,256]{4,3,2,1,0:T(8,128)(2,1)} %get-tuple-element.117.a_kept, bf16[3,6,4,64,256]{4,3,2,1,0:T(8,128)(2,1)} %collective-permute-done.16.a_got.refs_3_, bf16[1,6,4,64,256]{4,3,2,1,0:T(8,128)(2,1)} %get-tuple-element.122.b_kept, ...), custom_call_target="tpu_custom_call" | custom-call | flops 1 | bytes 1 | tf_op jit(solution)/shard_map/finish/pallas_call | solution.py:368
  214.1 0.9 copy-done.2
  215.5 6.7 %combine.1 = (bf16[512,1024]{1,0:T(8,128)(2,1)}, bf16[512,1024]{1,0:T(8,128)(2,1)}) custom-call(bf16[2,3,512,256]{3,2,1,0:T(8,128)(2,1)} %get-tuple-element.129.refs_0_, bf16[2,3,512,256]{3,2,1,0:T(8,128)(2,1)} %get-tuple-element.136.refs_1_, bf16[2,3,512,256]{3,2,1,0:T(8,128)(2,1)} %get-tuple-element.145.refs_2_, ...), custom_call_target="tpu_custom_call" | custom-call | flops 1 | bytes 1 | tf_op jit(solution)/shard_map/combine/pallas_call | solution.py:425
  222.2 0.7 fusion
  222.9 1.3 collective-permute-start.28
  224.2 5.1 %collective-permute-start.27 = (bf16[1,1024]{1,0:T(2,128)(2,1)S(1)}, bf16[1,1024]{1,0:T(2,128)(2,1)}, u32[]{:S(2)}, u32[]{:S(2)}) collective-permute-start(bf16[1,1024]{1,0:T(2,128)(2,1)S(1)} %get-tuple-element.195), channel_id=1, source_target_pairs={{0,8},{8,16},{16,24},{1,9},{9,17},{17,25},{2,10},{10,18},{18,26},{... | collective-permute-start | bytes 6152 | tf_op jit(solution)/shard_map/ppermute | solution.py:37
  230.1 4.3 %pair_sums.3 = (bf16[1,6,4,64,256]{4,3,2,1,0:T(8,128)(2,1)}, bf16[1,6,4,64,256]{4,3,2,1,0:T(8,128)(2,1)}, bf16[1,6,4,64,256]{4,3,2,1,0:T(8,128)(2,1)}, bf16[1,6,4,64,256]{4,3,2,1,0:T(8,128)(2,1)}) custom-call(bf16[2,6,4,64,256]{4,3,2,1,0:T(8,128)(2,1)} %get-tuple-element.168.refs_0_, bf16[3,6,4,64,256]{4,3,2,1,0:T(8,128)(2,1)} %collective-permute-done.29.refs_1_.b_got, ...), custom_call_target="tpu_custom_call" | custom-call | flops 199999995904 | bytes 1 | tf_op jit(solution)/shard_map/pair_sums/pallas_call | solution.py:332
  234.3 3.0 %collective-permute-start.31 = (bf16[1,6,4,64,256]{4,3,2,1,0:T(8,128)(2,1)}, bf16[1,6,4,64,256]{4,3,2,1,0:T(8,128)(2,1)S(1)}, u32[]{:S(2)}, u32[]{:S(2)}) collective-permute-start(bf16[1,6,4,64,256]{4,3,2,1,0:T(8,128)(2,1)} %get-tuple-element.177), channel_id=1, source_target_pairs={{0,16},{8,24},{16,0},{24,8},{1,17},{9,25},{17,1},{25,9},{2,18},{10... | collective-permute-start | bytes 2359304 | tf_op jit(solution)/shard_map/ppermute | solution.py:21
  237.7 3.7 %convolution.3 = bf16[512,1024]{1,0:T(8,128)(2,1)} custom-call(bf16[512,1024]{1,0:T(8,128)(2,1)} %get-tuple-element.166.x_ref, bf16[1,1024]{1,0:T(2,128)(2,1)} %collective-permute-done.27.before_ref, bf16[1,1024]{1,0:T(2,128)(2,1)} %collective-permute-done.28.behind_ref, f32[3,1024]{1,0:T(4,128)} %taps_ref.5), custom_call_target="tpu_custom_call" | custom-call | flops 1 | bytes 1 | tf_op jit(solution)/shard_map/convolution/pallas_call | solution.py:91
  241.4 3.2 %finish.5 = (f32[6,16,64,256]{3,2,1,0:T(8,128)}, f32[6,16,64,256]{3,2,1,0:T(8,128)}) custom-call(bf16[1,6,4,64,256]{4,3,2,1,0:T(8,128)(2,1)} %get-tuple-element.186.a_kept, bf16[3,6,4,64,256]{4,3,2,1,0:T(8,128)(2,1)} %collective-permute-done.30.refs_3_.a_got, ...), custom_call_target="tpu_custom_call", output_to_operand_aliasing={{0}: (4, {}), {1}: (5, {})} | custom-call | flops 1 | bytes 1 | tf_op jit(solution)/shard_map/finish/pallas_call | solution.py:368
  244.6 5.5 %collective-permute-done.33.a_got = bf16[1,6,4,64,256]{4,3,2,1,0:T(8,128)(2,1)} collective-permute-done((bf16[1,6,4,64,256]{4,3,2,1,0:T(8,128)(2,1)}, bf16[1,6,4,64,256]{4,3,2,1,0:T(8,128)(2,1)}, u32[]{:S(2)}, u32[]{:S(2)}) %collective-permute-start.33) | collective-permute-done | bytes 786464 | tf_op jit(solution)/shard_map/ppermute | solution.py:21
  250.3 3.3 %finish.6 = (f32[6,16,64,256]{3,2,1,0:T(8,128)}, f32[6,16,64,256]{3,2,1,0:T(8,128)}) custom-call(bf16[1,6,4,64,256]{4,3,2,1,0:T(8,128)(2,1)} %get-tuple-element.154.a_kept, bf16[1,6,4,64,256]{4,3,2,1,0:T(8,128)(2,1)} %collective-permute-done.33.a_got, ...), custom_call_target="tpu_custom_call", output_to_operand_aliasing={{0}: (4, {}), {1}: (5, {})} | custom-call | flops 1 | bytes 1 | tf_op jit(solution)/shard_map/finish/pallas_call | solution.py:368
  253.6 12.2 %collective-permute-done.31.a_got = bf16[1,6,4,64,256]{4,3,2,1,0:T(8,128)(2,1)S(1)} collective-permute-done((bf16[1,6,4,64,256]{4,3,2,1,0:T(8,128)(2,1)}, bf16[1,6,4,64,256]{4,3,2,1,0:T(8,128)(2,1)S(1)}, u32[]{:S(2)}, u32[]{:S(2)}) %collective-permute-start.31) | collective-permute-done | bytes 786464 | tf_op jit(solution)/shard_map/ppermute | solution.py:21
  265.9 1.8 finish.7
  (75 shorter events, 8.2 us)
Async XLA Ops:
  0.6 19.7 %copy-start.8 = (s32[16,5]{0,1:T(8,128)S(1)}, s32[16,5]{0,1:T(8,128)}, u32[]{:S(2)}) copy-start(s32[16,5]{0,1:T(8,128)} %param.10) | copy-start | bytes 964
  0.6 12.2 %collective-permute-start = (bf16[512,1024]{1,0:T(8,128)(2,1)}, bf16[512,1024]{1,0:T(8,128)(2,1)S(1)}, u32[]{:S(2)}, u32[]{:S(2)}) collective-permute-start(bf16[512,1024]{1,0:T(8,128)(2,1)} %refs_2_.7), channel_id=1, source_target_pairs={{0,1},{1,0},{2,3},{3,2},{4,5},{5,4},{6,7},{7,6},{8,9},{9,8},{10,11... | collective-permute-start | bytes 3145736 | tf_op jit(solution)/shard_map/ppermute | solution.py:21
  2.2 23.3 %collective-permute-start.2 = (bf16[528,256]{1,0:T(8,128)(2,1)S(1)}, bf16[528,256]{1,0:T(8,128)(2,1)S(1)}, u32[]{:S(2)}, u32[]{:S(2)}) collective-permute-start(bf16[528,256]{1,0:T(8,128)(2,1)S(1)} %pad.3), channel_id=1, source_target_pairs={{0,4},{1,5},{2,6},{3,7},{4,0},{5,1},{6,2},{7,3},{8,12},{9,13},{10,... | collective-permute-start | bytes 811016 | tf_op jit(solution)/shard_map/ppermute | solution.py:21
  5.8 27.3 %collective-permute-start.1 = (bf16[528,256]{1,0:T(8,128)(2,1)S(1)}, bf16[528,256]{1,0:T(8,128)(2,1)S(1)}, u32[]{:S(2)}, u32[]{:S(2)}) collective-permute-start(bf16[528,256]{1,0:T(8,128)(2,1)S(1)} %pad.3), channel_id=1, source_target_pairs={{0,2},{1,3},{2,0},{3,1},{4,6},{5,7},{6,4},{7,5},{8,10},{9,11},{10,... | collective-permute-start | bytes 811016 | tf_op jit(solution)/shard_map/ppermute | solution.py:21
  8.1 4.7 %collective-permute-start.3 = (bf16[1,1024]{1,0:T(2,128)(2,1)S(1)}, bf16[1,1024]{1,0:T(2,128)(2,1)S(1)}, u32[]{:S(2)}, u32[]{:S(2)}) collective-permute-start(bf16[1,1024]{1,0:T(2,128)(2,1)S(1)} %get-tuple-element.197), channel_id=1, source_target_pairs={{0,8},{8,16},{16,24},{1,9},{9,17},{17,25},{2,10},{10,18},{18,26},{... | collective-permute-start | bytes 6152 | tf_op jit(solution)/shard_map/ppermute | solution.py:37
  11.6 5.5 %collective-permute-start.4 = (bf16[1,1024]{1,0:T(2,128)(2,1)S(1)}, bf16[1,1024]{1,0:T(2,128)(2,1)S(1)}, u32[]{:S(2)}, u32[]{:S(2)}) collective-permute-start(bf16[1,1024]{1,0:T(2,128)(2,1)S(1)} %get-tuple-element.196), channel_id=1, source_target_pairs={{8,0},{16,8},{24,16},{9,1},{17,9},{25,17},{10,2},{18,10},{26,18},{... | collective-permute-start | bytes 6152 | tf_op jit(solution)/shard_map/ppermute | solution.py:38
  12.9 4.2 %copy-start.6 = (bf16[1,1024]{1,0:T(2,128)(2,1)}, bf16[1,1024]{1,0:T(2,128)(2,1)S(1)}, u32[]{:S(2)}) copy-start(bf16[1,1024]{1,0:T(2,128)(2,1)S(1)} %collective-permute-done.3.before_ref) | copy-start | bytes 6148
  12.9 21.5 %copy-start.9 = (bf16[512,1024]{1,0:T(8,128)(2,1)}, bf16[512,1024]{1,0:T(8,128)(2,1)S(1)}, u32[]{:S(2)}) copy-start(bf16[512,1024]{1,0:T(8,128)(2,1)S(1)} %collective-permute-done.refs_3_) | copy-start | bytes 3145732
  19.5 13.6 %collective-permute-start.7 = (bf16[512,256]{1,0:T(8,128)(2,1)}, bf16[512,256]{1,0:T(8,128)(2,1)S(1)}, u32[]{:S(2)}, u32[]{:S(2)}) collective-permute-start(bf16[512,256]{1,0:T(8,128)(2,1)} %convolution.2), channel_id=1, source_target_pairs={{0,4},{1,5},{2,6},{3,7},{4,0},{5,1},{6,2},{7,3},{8,12},{9,13},{10,... | collective-permute-start | bytes 786440 | tf_op jit(solution)/shard_map/ppermute | solution.py:21
  19.8 13.3 %collective-permute-start.6 = (bf16[512,256]{1,0:T(8,128)(2,1)}, bf16[512,256]{1,0:T(8,128)(2,1)S(1)}, u32[]{:S(2)}, u32[]{:S(2)}) collective-permute-start(bf16[512,256]{1,0:T(8,128)(2,1)} %convolution.2), channel_id=1, source_target_pairs={{0,2},{1,3},{2,0},{3,1},{4,6},{5,7},{6,4},{7,5},{8,10},{9,11},{10,... | collective-permute-start | bytes 786440 | tf_op jit(solution)/shard_map/ppermute | solution.py:21
  20.3 14.1 %collective-permute-start.5 = (bf16[512,256]{1,0:T(8,128)(2,1)}, bf16[512,256]{1,0:T(8,128)(2,1)S(1)}, u32[]{:S(2)}, u32[]{:S(2)}) collective-permute-start(bf16[512,256]{1,0:T(8,128)(2,1)} %convolution.2), channel_id=1, source_target_pairs={{0,1},{1,0},{2,3},{3,2},{4,5},{5,4},{6,7},{7,6},{8,9},{9,8},{10,11... | collective-permute-start | bytes 786440 | tf_op jit(solution)/shard_map/ppermute | solution.py:21
  25.5 8.9 %copy-start.10 = (bf16[528,256]{1,0:T(8,128)(2,1)}, bf16[528,256]{1,0:T(8,128)(2,1)S(1)}, u32[]{:S(2)}) copy-start(bf16[528,256]{1,0:T(8,128)(2,1)S(1)} %collective-permute-done.2.refs_5_) | copy-start | bytes 811012
  25.5 36.1 %collective-permute-start.10 = (bf16[512,1024]{1,0:T(8,128)(2,1)}, bf16[512,1024]{1,0:T(8,128)(2,1)}, u32[]{:S(2)}, u32[]{:S(2)}) collective-permute-start(bf16[512,1024]{1,0:T(8,128)(2,1)} %get-tuple-element.101.refs_6_.refs_7_.refs_8_), channel_id=1, source_target_pairs={{0,1},{1,0},{2,3},{3,2},{4,5},{5,4},{6,7},{7,6},{8,9},{9,8},{10,11... | collective-permute-start | bytes 3145736 | tf_op jit(solution)/shard_map/ppermute | solution.py:21
  33.1 1.3 copy-start.12
  33.1 1.3 copy-start.11
  33.1 1.3 copy-start.13
  33.1 26.5 %collective-permute-start.8 = (bf16[2,512,256]{2,1,0:T(8,128)(2,1)}, bf16[2,512,256]{2,1,0:T(8,128)(2,1)}, u32[]{:S(2)}, u32[]{:S(2)}) collective-permute-start(bf16[2,512,256]{2,1,0:T(8,128)(2,1)} %get-tuple-element.105), channel_id=1, source_target_pairs={{0,2},{1,3},{2,0},{3,1},{4,6},{5,7},{6,4},{7,5},{8,10},{9,11},{10,... | collective-permute-start | bytes 1572872 | tf_op jit(solution)/shard_map/ppermute | solution.py:21
  33.2 26.4 %collective-permute-start.9 = (bf16[2,512,256]{2,1,0:T(8,128)(2,1)}, bf16[2,512,256]{2,1,0:T(8,128)(2,1)}, u32[]{:S(2)}, u32[]{:S(2)}) collective-permute-start(bf16[2,512,256]{2,1,0:T(8,128)(2,1)} %get-tuple-element.105), channel_id=1, source_target_pairs={{0,4},{1,5},{2,6},{3,7},{4,0},{5,1},{6,2},{7,3},{8,12},{9,13},{10,... | collective-permute-start | bytes 1572872 | tf_op jit(solution)/shard_map/ppermute | solution.py:21
  49.3 39.8 %collective-permute-start.13 = (bf16[2,6,4,64,256]{4,3,2,1,0:T(8,128)(2,1)}, bf16[2,6,4,64,256]{4,3,2,1,0:T(8,128)(2,1)}, u32[]{:S(2)}, u32[]{:S(2)}) collective-permute-start(bf16[2,6,4,64,256]{4,3,2,1,0:T(8,128)(2,1)} %get-tuple-element.114), channel_id=1, source_target_pairs={{0,8},{8,0},{16,24},{24,16},{1,9},{9,1},{17,25},{25,17},{2,10},{10... | collective-permute-start | bytes 4718600 | tf_op jit(solution)/shard_map/ppermute | solution.py:21
  51.6 37.4 %collective-permute-start.14 = (bf16[2,6,4,64,256]{4,3,2,1,0:T(8,128)(2,1)}, bf16[2,6,4,64,256]{4,3,2,1,0:T(8,128)(2,1)}, u32[]{:S(2)}, u32[]{:S(2)}) collective-permute-start(bf16[2,6,4,64,256]{4,3,2,1,0:T(8,128)(2,1)} %get-tuple-element.116), channel_id=1, source_target_pairs={{0,16},{8,24},{16,0},{24,8},{1,17},{9,25},{17,1},{25,9},{2,18},{10... | collective-permute-start | bytes 4718600 | tf_op jit(solution)/shard_map/ppermute | solution.py:21
  59.6 26.3 %collective-permute-start.11 = (bf16[2,512,256]{2,1,0:T(8,128)(2,1)}, bf16[2,512,256]{2,1,0:T(8,128)(2,1)}, u32[]{:S(2)}, u32[]{:S(2)}) collective-permute-start(bf16[2,512,256]{2,1,0:T(8,128)(2,1)} %get-tuple-element.112), channel_id=1, source_target_pairs={{0,2},{1,3},{2,0},{3,1},{4,6},{5,7},{6,4},{7,5},{8,10},{9,11},{10,... | collective-permute-start | bytes 1572872 | tf_op jit(solution)/shard_map/ppermute | solution.py:21
  59.6 26.3 %collective-permute-start.12 = (bf16[2,512,256]{2,1,0:T(8,128)(2,1)}, bf16[2,512,256]{2,1,0:T(8,128)(2,1)}, u32[]{:S(2)}, u32[]{:S(2)}) collective-permute-start(bf16[2,512,256]{2,1,0:T(8,128)(2,1)} %get-tuple-element.112), channel_id=1, source_target_pairs={{0,4},{1,5},{2,6},{3,7},{4,0},{5,1},{6,2},{7,3},{8,12},{9,13},{10,... | collective-permute-start | bytes 1572872 | tf_op jit(solution)/shard_map/ppermute | solution.py:21
  86.0 31.3 %collective-permute-start.19 = (bf16[2,512,256]{2,1,0:T(8,128)(2,1)}, bf16[2,512,256]{2,1,0:T(8,128)(2,1)}, u32[]{:S(2)}, u32[]{:S(2)}) collective-permute-start(bf16[2,512,256]{2,1,0:T(8,128)(2,1)} %get-tuple-element.139), channel_id=1, source_target_pairs={{0,2},{1,3},{2,0},{3,1},{4,6},{5,7},{6,4},{7,5},{8,10},{9,11},{10,... | collective-permute-start | bytes 1572872 | tf_op jit(solution)/shard_map/ppermute | solution.py:21
  86.3 31.0 %collective-permute-start.20 = (bf16[2,512,256]{2,1,0:T(8,128)(2,1)}, bf16[2,512,256]{2,1,0:T(8,128)(2,1)}, u32[]{:S(2)}, u32[]{:S(2)}) collective-permute-start(bf16[2,512,256]{2,1,0:T(8,128)(2,1)} %get-tuple-element.139), channel_id=1, source_target_pairs={{0,4},{1,5},{2,6},{3,7},{4,0},{5,1},{6,2},{7,3},{8,12},{9,13},{10,... | collective-permute-start | bytes 1572872 | tf_op jit(solution)/shard_map/ppermute | solution.py:21
  89.0 35.0 %collective-permute-start.17 = (bf16[2,6,4,64,256]{4,3,2,1,0:T(8,128)(2,1)}, bf16[2,6,4,64,256]{4,3,2,1,0:T(8,128)(2,1)}, u32[]{:S(2)}, u32[]{:S(2)}) collective-permute-start(bf16[2,6,4,64,256]{4,3,2,1,0:T(8,128)(2,1)} %get-tuple-element.125), channel_id=1, source_target_pairs={{0,8},{8,0},{16,24},{24,16},{1,9},{9,1},{17,25},{25,17},{2,10},{10... | collective-permute-start | bytes 4718600 | tf_op jit(solution)/shard_map/ppermute | solution.py:21
  91.1 34.6 %collective-permute-start.15 = (bf16[2,6,4,64,256]{4,3,2,1,0:T(8,128)(2,1)}, bf16[2,6,4,64,256]{4,3,2,1,0:T(8,128)(2,1)}, u32[]{:S(2)}, u32[]{:S(2)}) collective-permute-start(bf16[2,6,4,64,256]{4,3,2,1,0:T(8,128)(2,1)} %get-tuple-element.120), channel_id=1, source_target_pairs={{0,16},{8,24},{16,0},{24,8},{1,17},{9,25},{17,1},{25,9},{2,18},{10... | collective-permute-start | bytes 4718600 | tf_op jit(solution)/shard_map/ppermute | solution.py:21
  117.3 46.5 %collective-permute-start.23 = (bf16[4,512,256]{2,1,0:T(8,128)(2,1)}, bf16[4,512,256]{2,1,0:T(8,128)(2,1)}, u32[]{:S(2)}, u32[]{:S(2)}) collective-permute-start(bf16[4,512,256]{2,1,0:T(8,128)(2,1)} %get-tuple-element.159), channel_id=1, source_target_pairs={{0,4},{1,5},{2,6},{3,7},{4,0},{5,1},{6,2},{7,3},{8,12},{9,13},{10,... | collective-permute-start | bytes 3145736 | tf_op jit(solution)/shard_map/ppermute | solution.py:21
  117.6 46.1 %collective-permute-start.22 = (bf16[4,512,256]{2,1,0:T(8,128)(2,1)}, bf16[4,512,256]{2,1,0:T(8,128)(2,1)}, u32[]{:S(2)}, u32[]{:S(2)}) collective-permute-start(bf16[4,512,256]{2,1,0:T(8,128)(2,1)} %get-tuple-element.157), channel_id=1, source_target_pairs={{0,2},{1,3},{2,0},{3,1},{4,6},{5,7},{6,4},{7,5},{8,10},{9,11},{10,... | collective-permute-start | bytes 3145736 | tf_op jit(solution)/shard_map/ppermute | solution.py:21
  125.7 51.4 %collective-permute-start.16 = (bf16[3,6,4,64,256]{4,3,2,1,0:T(8,128)(2,1)}, bf16[3,6,4,64,256]{4,3,2,1,0:T(8,128)(2,1)}, u32[]{:S(2)}, u32[]{:S(2)}) collective-permute-start(bf16[3,6,4,64,256]{4,3,2,1,0:T(8,128)(2,1)} %get-tuple-element.121), channel_id=1, source_target_pairs={{0,16},{8,24},{16,0},{24,8},{1,17},{9,25},{17,1},{25,9},{2,18},{10... | collective-permute-start | bytes 7077896 | tf_op jit(solution)/shard_map/ppermute | solution.py:21
  125.8 50.7 %collective-permute-start.18 = (bf16[3,6,4,64,256]{4,3,2,1,0:T(8,128)(2,1)}, bf16[3,6,4,64,256]{4,3,2,1,0:T(8,128)(2,1)}, u32[]{:S(2)}, u32[]{:S(2)}) collective-permute-start(bf16[3,6,4,64,256]{4,3,2,1,0:T(8,128)(2,1)} %get-tuple-element.126), channel_id=1, source_target_pairs={{0,8},{8,0},{16,24},{24,16},{1,9},{9,1},{17,25},{25,17},{2,10},{10... | collective-permute-start | bytes 7077896 | tf_op jit(solution)/shard_map/ppermute | solution.py:21
  163.8 47.1 %collective-permute-start.26 = (bf16[4,512,256]{2,1,0:T(8,128)(2,1)}, bf16[4,512,256]{2,1,0:T(8,128)(2,1)}, u32[]{:S(2)}, u32[]{:S(2)}) collective-permute-start(bf16[4,512,256]{2,1,0:T(8,128)(2,1)} %get-tuple-element.165), channel_id=1, source_target_pairs={{0,4},{1,5},{2,6},{3,7},{4,0},{5,1},{6,2},{7,3},{8,12},{9,13},{10,... | collective-permute-start | bytes 3145736 | tf_op jit(solution)/shard_map/ppermute | solution.py:21
  164.3 49.8 %collective-permute-start.25 = (bf16[4,512,256]{2,1,0:T(8,128)(2,1)}, bf16[4,512,256]{2,1,0:T(8,128)(2,1)}, u32[]{:S(2)}, u32[]{:S(2)}) collective-permute-start(bf16[4,512,256]{2,1,0:T(8,128)(2,1)} %get-tuple-element.163), channel_id=1, source_target_pairs={{0,2},{1,3},{2,0},{3,1},{4,6},{5,7},{6,4},{7,5},{8,10},{9,11},{10,... | collective-permute-start | bytes 3145736 | tf_op jit(solution)/shard_map/ppermute | solution.py:21
  177.1 52.3 %collective-permute-start.30 = (bf16[3,6,4,64,256]{4,3,2,1,0:T(8,128)(2,1)}, bf16[3,6,4,64,256]{4,3,2,1,0:T(8,128)(2,1)}, u32[]{:S(2)}, u32[]{:S(2)}) collective-permute-start(bf16[3,6,4,64,256]{4,3,2,1,0:T(8,128)(2,1)} %get-tuple-element.174), channel_id=1, source_target_pairs={{0,16},{8,24},{16,0},{24,8},{1,17},{9,25},{17,1},{25,9},{2,18},{10... | collective-permute-start | bytes 7077896 | tf_op jit(solution)/shard_map/ppermute | solution.py:21
  178.4 51.1 %collective-permute-start.29 = (bf16[3,6,4,64,256]{4,3,2,1,0:T(8,128)(2,1)}, bf16[3,6,4,64,256]{4,3,2,1,0:T(8,128)(2,1)}, u32[]{:S(2)}, u32[]{:S(2)}) collective-permute-start(bf16[3,6,4,64,256]{4,3,2,1,0:T(8,128)(2,1)} %get-tuple-element.170), channel_id=1, source_target_pairs={{0,8},{8,0},{16,24},{24,16},{1,9},{9,1},{17,25},{25,17},{2,10},{10... | collective-permute-start | bytes 7077896 | tf_op jit(solution)/shard_map/ppermute | solution.py:21
  179.0 4.4 %copy-start.4 = (bf16[4,512,256]{2,1,0:T(8,128)(2,1)S(1)}, bf16[4,512,256]{2,1,0:T(8,128)(2,1)}, u32[]{:S(2)}) copy-start(bf16[4,512,256]{2,1,0:T(8,128)(2,1)} %get-tuple-element.155) | copy-start | bytes 3145732
  179.0 31.9 %copy-start.5 = (bf16[4,512,256]{2,1,0:T(8,128)(2,1)S(1)}, bf16[4,512,256]{2,1,0:T(8,128)(2,1)}, u32[]{:S(2)}) copy-start(bf16[4,512,256]{2,1,0:T(8,128)(2,1)} %get-tuple-element.161) | copy-start | bytes 3145732
  183.5 30.7 %collective-permute-start.21 = (bf16[4,512,256]{2,1,0:T(8,128)(2,1)S(1)}, bf16[4,512,256]{2,1,0:T(8,128)(2,1)S(1)}, u32[]{:S(2)}, u32[]{:S(2)}) collective-permute-start(bf16[4,512,256]{2,1,0:T(8,128)(2,1)S(1)} %copy-done.4), channel_id=1, source_target_pairs={{0,1},{1,0},{2,3},{3,2},{4,5},{5,4},{6,7},{7,6},{8,9},{9,8},{10,11... | collective-permute-start | bytes 3145736 | tf_op jit(solution)/shard_map/ppermute | solution.py:21
  210.9 3.2 %collective-permute-start.24 = (bf16[4,512,256]{2,1,0:T(8,128)(2,1)S(1)}, bf16[4,512,256]{2,1,0:T(8,128)(2,1)S(1)}, u32[]{:S(2)}, u32[]{:S(2)}) collective-permute-start(bf16[4,512,256]{2,1,0:T(8,128)(2,1)S(1)} %copy-done.5), channel_id=1, source_target_pairs={{0,1},{1,0},{2,3},{3,2},{4,5},{5,4},{6,7},{7,6},{8,9},{9,8},{10,11... | collective-permute-start | bytes 3145736 | tf_op jit(solution)/shard_map/ppermute | solution.py:21
  214.1 1.0 copy-start.2
  214.1 1.3 copy-start.3
  222.9 7.1 %collective-permute-start.28 = (bf16[1,1024]{1,0:T(2,128)(2,1)S(1)}, bf16[1,1024]{1,0:T(2,128)(2,1)}, u32[]{:S(2)}, u32[]{:S(2)}) collective-permute-start(bf16[1,1024]{1,0:T(2,128)(2,1)S(1)} %get-tuple-element.194), channel_id=1, source_target_pairs={{8,0},{16,8},{24,16},{9,1},{17,9},{25,17},{10,2},{18,10},{26,18},{... | collective-permute-start | bytes 6152 | tf_op jit(solution)/shard_map/ppermute | solution.py:38
  224.2 5.9 %collective-permute-start.27 = (bf16[1,1024]{1,0:T(2,128)(2,1)S(1)}, bf16[1,1024]{1,0:T(2,128)(2,1)}, u32[]{:S(2)}, u32[]{:S(2)}) collective-permute-start(bf16[1,1024]{1,0:T(2,128)(2,1)S(1)} %get-tuple-element.195), channel_id=1, source_target_pairs={{0,8},{8,16},{16,24},{1,9},{9,17},{17,25},{2,10},{10,18},{18,26},{... | collective-permute-start | bytes 6152 | tf_op jit(solution)/shard_map/ppermute | solution.py:37
  229.4 20.7 %collective-permute-start.33 = (bf16[1,6,4,64,256]{4,3,2,1,0:T(8,128)(2,1)}, bf16[1,6,4,64,256]{4,3,2,1,0:T(8,128)(2,1)}, u32[]{:S(2)}, u32[]{:S(2)}) collective-permute-start(bf16[1,6,4,64,256]{4,3,2,1,0:T(8,128)(2,1)} %get-tuple-element.181), channel_id=1, source_target_pairs={{0,16},{8,24},{16,0},{24,8},{1,17},{9,25},{17,1},{25,9},{2,18},{10... | collective-permute-start | bytes 2359304 | tf_op jit(solution)/shard_map/ppermute | solution.py:21
  229.5 20.7 %collective-permute-start.34 = (bf16[1,6,4,64,256]{4,3,2,1,0:T(8,128)(2,1)}, bf16[1,6,4,64,256]{4,3,2,1,0:T(8,128)(2,1)}, u32[]{:S(2)}, u32[]{:S(2)}) collective-permute-start(bf16[1,6,4,64,256]{4,3,2,1,0:T(8,128)(2,1)} %get-tuple-element.185), channel_id=1, source_target_pairs={{0,8},{8,0},{16,24},{24,16},{1,9},{9,1},{17,25},{25,17},{2,10},{10... | collective-permute-start | bytes 2359304 | tf_op jit(solution)/shard_map/ppermute | solution.py:21
  234.3 31.5 %collective-permute-start.31 = (bf16[1,6,4,64,256]{4,3,2,1,0:T(8,128)(2,1)}, bf16[1,6,4,64,256]{4,3,2,1,0:T(8,128)(2,1)S(1)}, u32[]{:S(2)}, u32[]{:S(2)}) collective-permute-start(bf16[1,6,4,64,256]{4,3,2,1,0:T(8,128)(2,1)} %get-tuple-element.177), channel_id=1, source_target_pairs={{0,16},{8,24},{16,0},{24,8},{1,17},{9,25},{17,1},{25,9},{2,18},{10... | collective-permute-start | bytes 2359304 | tf_op jit(solution)/shard_map/ppermute | solution.py:21
  237.4 28.5 %collective-permute-start.32 = (bf16[1,6,4,64,256]{4,3,2,1,0:T(8,128)(2,1)}, bf16[1,6,4,64,256]{4,3,2,1,0:T(8,128)(2,1)S(1)}, u32[]{:S(2)}, u32[]{:S(2)}) collective-permute-start(bf16[1,6,4,64,256]{4,3,2,1,0:T(8,128)(2,1)} %get-tuple-element.179), channel_id=1, source_target_pairs={{0,8},{8,0},{16,24},{24,16},{1,9},{9,1},{17,25},{25,17},{2,10},{10... | collective-permute-start | bytes 2359304 | tf_op jit(solution)/shard_map/ppermute | solution.py:21
  250.3 15.6 %copy-start = (bf16[1,6,4,64,256]{4,3,2,1,0:T(8,128)(2,1)S(1)}, bf16[1,6,4,64,256]{4,3,2,1,0:T(8,128)(2,1)}, u32[]{:S(2)}) copy-start(bf16[1,6,4,64,256]{4,3,2,1,0:T(8,128)(2,1)} %get-tuple-element.176.a_kept) | copy-start | bytes 2359300
  250.3 15.6 %copy-start.1 = (bf16[1,6,4,64,256]{4,3,2,1,0:T(8,128)(2,1)S(1)}, bf16[1,6,4,64,256]{4,3,2,1,0:T(8,128)(2,1)}, u32[]{:S(2)}) copy-start(bf16[1,6,4,64,256]{4,3,2,1,0:T(8,128)(2,1)} %get-tuple-element.178.b_kept) | copy-start | bytes 2359300
  (2 other events, 1.3 us)
